TPU v7x, 32 devices: a whole 2x2x4 slice. The times are simulated.
32 devices in a mesh: dp: 8 (over z, y), mp: 4 (over x, core).
Axes of the slice: x: 2, y: 2, z: 4, core: 2. Of those that a mesh axis runs over, the one named last changes fastest.
Arguments:
- patches: bfloat16 [32, 256, 768], P('dp'), may hold values from -20 to 20
- segment_ids: int32 [32, 256], P('dp'), may hold values from 0 to 1, never falling along the last dimension, each value on 1 to 196 neighbouring positions
- mask_slots: int32 [32, 64], P('dp'), may hold values from 0 to 255
- gain_attn: bfloat16 [768], replicated, may hold values from 0.099609375 to 1.8984375
- qkv_weight: bfloat16 [3, 768, 768], P(None, None, 'mp'), may hold values from -0.21875 to 0.21875
- out_weight: bfloat16 [768, 768], P('mp'), may hold values from -2 to 2
- gain_mlp: bfloat16 [768], replicated, may hold values from 0.099609375 to 1.8984375
- up_weight: bfloat16 [768, 3072], P(None, 'mp'), may hold values from -0.21875 to 0.21875
- down_weight: bfloat16 [3072, 768], P('mp'), may hold values from -0.109375 to 0.109375
- embed_weight: bfloat16 [768, 384], P(None, 'mp'), may hold values from -0.21875 to 0.21875
- mask_token: bfloat16 [384], replicated, may hold values from -4 to 4
- pred_gain_attn: bfloat16 [384], replicated, may hold values from 0.099609375 to 1.8984375
- pred_qkv: bfloat16 [3, 384, 384], P(None, None, 'mp'), may hold values from -0.3125 to 0.3125
- pred_out: bfloat16 [384, 384], P('mp'), may hold values from -3 to 3
- pred_gain_mlp: bfloat16 [384], replicated, may hold values from 0.099609375 to 1.8984375
- pred_up: bfloat16 [384, 1536], P(None, 'mp'), may hold values from -0.3125 to 0.3125
- pred_down: bfloat16 [1536, 384], P('mp'), may hold values from -0.15625 to 0.15625
- cotangent: bfloat16 [32, 256, 384], P('dp'), may hold values from -6 to 6
Outputs:
- predictions: bfloat16 [32, 256, 384], P('dp')
- patches_grad: bfloat16 [32, 256, 768], P('dp')
- variance: float32 [384], P('mp')
- grad_gain_attn: float32 [768], P('dp')
- grad_qkv: float32 [3, 768, 768], P(None, 'dp', 'mp')
- grad_out: float32 [768, 768], P('mp', 'dp')
- grad_gain_mlp: float32 [768], P('dp')
- grad_up: float32 [768, 3072], P('dp', 'mp')
- grad_down: float32 [3072, 768], P('mp', 'dp')
- grad_embed: float32 [768, 384], P('dp', 'mp')
- grad_mask_token: float32 [384], P('dp')
- grad_pred_gain_attn: float32 [384], P('dp')
- grad_pred_qkv: float32 [3, 384, 384], P(None, 'dp', 'mp')
- grad_pred_out: float32 [384, 384], P('mp', 'dp')
- grad_pred_gain_mlp: float32 [384], P('dp')
- grad_pred_up: float32 [384, 1536], P('dp', 'mp')
- grad_pred_down: float32 [1536, 384], P('mp', 'dp')
Inputs may be any that keep to these rules, and one draw needn't show every extreme that they name: `segment_ids`: each row holds image 0 then image 1, each of 60 to 196 tokens. `mask_slots`: positions within the row that take the mask token; a position may repeat.
All inputs are finite; a program needn't handle non-finite values.
Results may differ from a plain program's by a relative error of at most 0.03.
Values may be sent and summed in bfloat16 or wider, within the bound.
No kernel may reach another device: no remote copies, remote signals or barrier semaphores. Data moves between devices by JAX's collectives and lax.ppermute only.
A program may use at most 128 MiB of HBM per device.

v0:
```python
import math

import jax
import jax.numpy as jnp
from jax import lax
from jax.experimental import pallas as pl
from jax.experimental.pallas import tpu as pltpu
from jax.sharding import PartitionSpec as P

HEAD_DIM = 64
P_HEAD_DIM = 32
SHARDS = 4
EPS = 1e-06
BF = jnp.bfloat16
F32 = jnp.float32
VMEM_BYTES = 48 * 1024 * 1024


def contract(left, right, at_left, at_right):
    return lax.dot_general(left, right, (((at_left,), (at_right,)), ((), ())), preferred_element_type=F32)


def nn(left, right):
    return contract(left, right, 1, 0)


def nt(left, right):
    return contract(left, right, 1, 1)


def tn(left, right):
    return contract(left, right, 0, 0)


def norm(value):
    centred = value - jnp.mean(value, -1, keepdims=True)
    inverse = lax.rsqrt(jnp.mean(centred * centred, -1, keepdims=True) + EPS)
    return centred * inverse, inverse


def norm_back(normed, inverse, gain, grad):
    scaled = grad * gain
    along = jnp.mean(scaled * normed, -1, keepdims=True)
    d_value = (scaled - jnp.mean(scaled, -1, keepdims=True) - normed * along) * inverse
    return d_value, jnp.sum(grad * normed, 0, keepdims=True)


def gelu_parts(pre):
    cdf = 0.5 * (1.0 + lax.erf(pre * 0.7071067811865476))
    density = 0.3989422804014327 * jnp.exp(-0.5 * pre * pre)
    return pre * cdf, cdf + pre * density


def turned(source_rows, value):
    width = value.shape[1]
    one_hot = (lax.broadcasted_iota(jnp.int32, (width, width), 1) == source_rows).astype(BF)
    return nt(one_hot, value).astype(BF)


def head_rows(head, per, head_dim):
    shard = head // per
    first = shard * (3 * per * head_dim) + (head - shard * per) * head_dim
    return [pl.ds(pl.multiple_of(first + part * per * head_dim, head_dim), head_dim) for part in range(3)]


def attend(qkv_ref, probs_ref, mixed_ref, same, per, head_dim):
    factor = head_dim ** (-0.5) * math.log2(math.e)

    def one_head(head, carry):
        q_at, k_at, u_at = head_rows(head, per, head_dim)
        scores = jnp.where(same, tn(qkv_ref[k_at, :], qkv_ref[q_at, :]), -1e9)
        top = jnp.max(scores, 0, keepdims=True)
        expd = jnp.exp2((scores - top) * factor)
        probs = (expd * (1.0 / jnp.sum(expd, 0, keepdims=True))).astype(BF)
        probs_ref[head] = probs
        at = pl.ds(pl.multiple_of(head * head_dim, head_dim), head_dim)
        mixed_ref[at, :] = nn(qkv_ref[u_at, :], probs).astype(BF)
        return carry

    lax.fori_loop(0, SHARDS * per, one_head, 0, unroll=2)


def attend_back(qkv_ref, probs_ref, d_mixed_ref, d_qkv_ref, per, head_dim):
    scale = head_dim ** (-0.5)

    def one_head(head, carry):
        q_at, k_at, u_at = head_rows(head, per, head_dim)
        at = pl.ds(pl.multiple_of(head * head_dim, head_dim), head_dim)
        d_mixed = d_mixed_ref[at, :]
        low = probs_ref[head]
        probs = low.astype(F32)
        d_probs = tn(qkv_ref[u_at, :], d_mixed)
        along = jnp.sum(d_probs * probs, 0, keepdims=True)
        d_scores = (probs * (d_probs - along)).astype(BF)
        d_qkv_ref[q_at, :] = (nn(qkv_ref[k_at, :], d_scores) * scale).astype(BF)
        d_qkv_ref[k_at, :] = (nt(qkv_ref[q_at, :], d_scores) * scale).astype(BF)
        d_qkv_ref[u_at, :] = nt(d_mixed, low).astype(BF)
        return carry

    lax.fori_loop(0, SHARDS * per, one_head, 0, unroll=2)


ANYWHERE = pl.BlockSpec(memory_space=pl.ANY)


ANYWHERE = pl.BlockSpec(memory_space=pl.ANY)


def call(kernel, outs, args, micros, scratch=(), tokens=()):
    shapes = [jax.ShapeDtypeStruct(shape, kind) for shape, kind in outs]
    moved = sum(math.prod(a.shape) * a.dtype.itemsize for a in list(args) + shapes)
    n_args, n_all = len(args), len(args) + len(tokens)
    return pl.pallas_call(
        lambda *refs: kernel(*refs[:n_args], *refs[n_all:]),
        out_shape=shapes,
        in_specs=[pl.BlockSpec(memory_space=pltpu.SMEM)]
        + [pl.BlockSpec(memory_space=pltpu.VMEM)] * (n_args - 1)
        + [ANYWHERE] * len(tokens),
        out_specs=[pl.BlockSpec(memory_space=pltpu.VMEM)] * len(shapes),
        scratch_shapes=[pltpu.VMEM(shape, kind) for shape, kind in scratch],
        compiler_params=pltpu.CompilerParams(vmem_limit_bytes=VMEM_BYTES),
        cost_estimate=pl.CostEstimate(flops=int(micros * 1e10), bytes_accessed=moved, transcendentals=0),
    )(*args, *tokens)


def gate(values, tokens):
    return pl.pallas_call(
        lambda *refs: None,
        out_shape=[jax.ShapeDtypeStruct(v.shape, v.dtype) for v in values],
        in_specs=[ANYWHERE] * (len(values) + len(tokens)),
        out_specs=[ANYWHERE] * len(values),
        input_output_aliases={at: at for at in range(len(values))},
    )(*values, *tokens)


def units(value):
    return [value[:, at * 128 : (at + 1) * 128] for at in range(value.shape[1] // 128)]


class Segments:
    def __init__(self, rows, cols):
        self.half, blocks = rows // 2, cols // 128
        self.left, self.right = blocks // 2, blocks - blocks // 2
        a, b = self.half * self.left, self.half * self.right
        self.over_x, self.over_y = (0, 2 * a), (2 * a, 2 * b)
        self.then_y, self.then_x = (2 * a + 2 * b, a), (3 * a + 2 * b, b)
        self.keep_left, self.keep_right = (3 * a + 3 * b, a), (4 * a + 3 * b, b)
        self.shape = (4 * (a + b), 128)
        self.a, self.b = a, b

    def put(self, ref, shard, block, value):
        half, a, b = self.half, self.a, self.b
        if shard:
            starts_left = (self.over_x[0], self.over_x[0] + a)
            starts_right = (self.then_x[0], self.over_y[0] + b)
        else:
            starts_left = (self.keep_left[0], self.then_y[0])
            starts_right = (self.keep_right[0], self.over_y[0])
        for side in range(2):
            if isinstance(block, int):
                at = starts_left[side] + block * half if block < self.left else starts_right[side] + (block - self.left) * half
            else:
                at = jnp.where(block < self.left, starts_left[side], starts_right[side] - self.left * half) + block * half
                at = pl.multiple_of(at, half)
            ref[pl.ds(at, half), :] = value[side * half : (side + 1) * half].astype(BF)


def combine(outs, tokens):
    arrays, terms = [], []
    for segments in outs:
        for parts in segments:
            for array, first, size in parts:
                if not any(array is known for known in arrays):
                    arrays.append(array)
                terms.append((next(i for i, known in enumerate(arrays) if known is array), first, size))
    n_in, n_out, n_terms = len(arrays) + len(tokens), len(outs), len(terms)
    sizes = [sum(parts[0][2] for parts in segments) for segments in outs]

    def kernel(*refs):
        held, sem = refs[n_in + n_out : -1], refs[-1]
        copies = [
            pltpu.make_async_copy(refs[which].at[pl.ds(first, size), :], held[at], sem.at[at])
            for at, (which, first, size) in enumerate(terms)
        ]
        for copy in copies:
            copy.start()
        at = 0
        for out, segments in zip(refs[n_in:], outs):
            row = 0
            for parts in segments:
                size = parts[0][2]
                mine = list(range(at, at + len(parts)))
                for term in mine:
                    copies[term].wait()

                def add(step, carry, row=row, mine=mine, out=out):
                    here = pl.ds(pl.multiple_of(step * 64, 64), 64)
                    total = held[mine[0]][here, :].astype(F32)
                    for term in mine[1:]:
                        total = total + held[term][here, :].astype(F32)
                    out[pl.ds(pl.multiple_of(row + step * 64, 64), 64), :] = total.astype(BF)
                    return carry

                lax.fori_loop(0, size // 64, add, 0, unroll=2)
                at += len(parts)
                row += size

    moved = 256 * (sum(t[2] for t in terms) + sum(sizes))
    return pl.pallas_call(
        kernel,
        out_shape=[jax.ShapeDtypeStruct((size, 128), BF) for size in sizes],
        in_specs=[ANYWHERE] * n_in,
        out_specs=[pl.BlockSpec(memory_space=pltpu.VMEM)] * n_out,
        scratch_shapes=[pltpu.VMEM((size, 128), BF) for _, _, size in terms] + [pltpu.SemaphoreType.DMA((n_terms,))],
        compiler_params=pltpu.CompilerParams(vmem_limit_bytes=VMEM_BYTES),
        cost_estimate=pl.CostEstimate(flops=int(3e10), bytes_accessed=moved, transcendentals=0),
    )(*arrays, *tokens)


def pack_attn_kernel(pos, qkv, out, own, direct):
    cols = qkv.shape[2]
    for part in range(3):
        own[part * cols : (part + 1) * cols, :] = qkv[part].T
    own[3 * cols :, :] = out[...]
    half = direct.shape[0]
    direct[...] = own[pl.ds(pl.multiple_of(pos[1] * half, half), half), :]


def pack_mlp_kernel(pos, up, down, up_direct, down_direct):
    half = up_direct.shape[1]
    at = pl.ds(pl.multiple_of(pos[1] * half, half), half)
    up_direct[...] = up[:, at]
    down_direct[...] = down[at, :]


def pack_pred_kernel(pos, qkv, out, embed, up, down, attn, mlp):
    cols, half_width = qkv.shape[2], attn.shape[2]
    attn[0, :cols, :] = qkv[0].T
    attn[0, cols : 2 * cols, :] = qkv[1].T
    attn[0, 2 * cols :, :] = embed[:half_width, :].T
    attn[1, :cols, :] = qkv[2].T
    attn[1, cols : 2 * cols, :] = out[...]
    attn[1, 2 * cols :, :] = embed[half_width:, :].T
    half = mlp.shape[2]
    turned_up = up[...].T
    for side in range(2):
        mlp[side, 0] = turned_up[side * half : (side + 1) * half, :]
        mlp[side, 1] = down[side * half : (side + 1) * half, :]


def enc_attn_kernel(pos, x, seg_row, seg_col, gain, own, core, d_x, e_x, d_c, e_c, middle, qkv, probs, mixed, far):
    side = pos[1]
    half = d_x.shape[0]
    per = own.shape[0] // 4 // HEAD_DIM
    rows = 3 * per * HEAD_DIM
    for at, (first, second) in enumerate(((d_x, e_x), (d_c, e_c))):
        far[at, pl.ds(pl.multiple_of(side * half, half), half), :] = first[...]
        far[at, pl.ds(pl.multiple_of((1 - side) * half, half), half), :] = second[...]
    value = x[...].astype(F32)
    normed, _ = norm(value)
    low = (normed * gain[...]).astype(BF)
    packs = (own, core, far.at[0], far.at[1])
    for shard, pack in enumerate(packs):
        qkv[shard * rows : (shard + 1) * rows, :] = nt(pack[:rows, :], low).astype(BF)
    attend(qkv, probs, mixed, seg_col[...] == seg_row[...], per, HEAD_DIM)
    total = value
    for shard, pack in enumerate(packs):
        total = total + tn(mixed[shard * rows // 3 : (shard + 1) * rows // 3, :], pack[rows:, :])
    middle[...] = total


def hidden_pieces(side, mats, width):
    half = width // 2
    own, core, d_x, e_x, d_c, e_c = mats
    first, second = side * half, (1 - side) * half
    return (
        (own, 0, width), (core, width, width),
        (d_x, 2 * width + first, half), (e_x, 2 * width + second, half),
        (d_c, 3 * width + first, half), (e_c, 3 * width + second, half),
    )


def columns(first, size):
    return pl.ds(first if isinstance(first, int) else pl.multiple_of(first, 128), size)


def enc_up_forward_kernel(pos, middle, gain, *refs):
    ups, (hidden, slope) = refs[:6], refs[6:]
    width = ups[0].shape[1]
    normed, _ = norm(middle[...])
    low = (normed * gain[...]).astype(BF)
    for up, first, size in hidden_pieces(pos[1], ups, width):
        act, back = gelu_parts(nn(low, up[...]))
        hidden[:, columns(first, size)] = act.astype(BF)
        slope[:, columns(first, size)] = back.astype(BF)


def enc_down_forward_kernel(pos, middle, hidden, *refs):
    downs, out = refs[:6], refs[6]
    total = middle[...]
    for down, first, size in hidden_pieces(pos[1], downs, downs[0].shape[0]):
        total = total + nn(hidden[:, columns(first, size)], down[...])
    out[...] = total.astype(BF)


def pred_kernel(
    pos, enc, seg_row, seg_col, masked, token, gain_one, gain_two, cot, rows_at,
    a_own, a_core, a_x, a_xc, m_own, m_core, m_x, m_xc,
    pred_out, stats, g_mine, g_theirs, d_embedded, d_enc, d_gains,
    w_qkv, w_out, w_embed, w_up, w_down, qkv, probs, mixed, d_mixed, d_qkv,
):
    me = pos[0]
    length = cot.shape[0]
    cols = w_out.shape[0] // SHARDS
    segments = Segments(w_out.shape[0], 4 * cols + 4 * m_x.shape[2])
    per = cols // P_HEAD_DIM
    half = m_x.shape[2]
    hid = 2 * half
    width = w_out.shape[1]
    for shard, pack in enumerate((a_own, a_core, a_x, a_xc)):
        w_qkv[shard * 3 * cols : shard * 3 * cols + 2 * cols, :] = pack[0, : 2 * cols]
        w_qkv[shard * 3 * cols + 2 * cols : (shard + 1) * 3 * cols, :] = pack[1, :cols]
        w_out[shard * cols : (shard + 1) * cols, :] = pack[1, cols : 2 * cols]
        at = pl.ds(pl.multiple_of((me ^ shard) * cols, 16), cols)
        w_embed[at, :width] = pack[0, 2 * cols :]
        w_embed[at, width:] = pack[1, 2 * cols :]
    for shard, pack in enumerate((m_own, m_core, m_x, m_xc)):
        for which in range(2):
            at = slice(shard * hid + which * half, shard * hid + (which + 1) * half)
            w_up[at, :] = pack[which, 0]
            w_down[at, :] = pack[which, 1]

    hidden_mask = masked[...] > 0.0
    start = jnp.where(hidden_mask, token[...], nt(enc[...], w_embed[...]))
    n_one, r_one = norm(start)
    a = (n_one * gain_one[...]).astype(BF)
    qkv[...] = nt(w_qkv[...], a).astype(BF)
    attend(qkv, probs, mixed, seg_col[...] == seg_row[...], per, P_HEAD_DIM)
    middle = start + tn(mixed[...], w_out[...])
    n_two, r_two = norm(middle)
    b = (n_two * gain_two[...]).astype(BF)
    act, slope = gelu_parts(nt(b, w_up[...]))
    act = act.astype(BF)
    predicted = middle + nn(act, w_down[...])
    for at, block in enumerate(units(predicted)):
        pred_out[at * length : (at + 1) * length, :] = block.astype(BF)
    stats[0:1, :] = jnp.sum(predicted, 0, keepdims=True)
    stats[1:2, :] = jnp.sum(predicted * predicted, 0, keepdims=True)

    homes = ((g_mine, 0), (g_theirs, 0), (g_mine, 1), (g_theirs, 1))
    grad_low = cot[...]
    d_pre = (nt(grad_low, w_down[...]) * slope).astype(BF)
    source = rows_at[...]
    grad_turned, b_turned = turned(source, grad_low), turned(source, b)
    for shard, (home, at) in enumerate(homes):
        cut = slice(shard * hid, (shard + 1) * hid)
        blocks = units(nn(b_turned, d_pre[:, cut])) + units(nn(grad_turned, act[:, cut]))
        for block, value in enumerate(blocks):
            segments.put(home, at, 4 * cols // 128 + block, value)
    d_middle, d_gain_two = norm_back(n_two, r_two, gain_two[...], nn(d_pre, w_up[...]))
    grad_mid = grad_low.astype(F32) + d_middle
    mid_low = grad_mid.astype(BF)
    d_mixed[...] = nt(w_out[...], mid_low).astype(BF)
    attend_back(qkv, probs, d_mixed, d_qkv, per, P_HEAD_DIM)
    a_turned, mid_turned = turned(source, a), turned(source, mid_low)
    for shard, (home, at) in enumerate(homes):
        g_qkv = nt(a_turned, d_qkv[shard * 3 * cols : (shard + 1) * 3 * cols, :])
        g_out = nt(mid_turned, mixed[shard * cols : (shard + 1) * cols, :])
        for block, value in enumerate(units(jnp.concatenate([g_qkv, g_out], 1))):
            segments.put(home, at, block, value)
    d_value, d_gain_one = norm_back(n_one, r_one, gain_one[...], tn(d_qkv[...], w_qkv[...]))
    d_start = grad_mid + d_value
    d_gains[0:1, :] = d_gain_one
    d_gains[1:2, :] = d_gain_two
    d_gains[2:3, :] = jnp.sum(jnp.where(hidden_mask, d_start, 0.0), 0, keepdims=True)
    d_low = jnp.where(hidden_mask, 0.0, d_start).astype(BF)
    d_embedded[...] = d_low
    d_enc[...] = nn(d_low, w_embed[...])


def enc_down_kernel(pos, rows_at, grad, hidden, mine, theirs):
    width = hidden.shape[1] // SHARDS
    segments = Segments(grad.shape[1], width)
    grad_turned = turned(rows_at[...], grad[...].astype(BF))
    for shard, (home, at) in ((1, (theirs, 0)), (3, (theirs, 1)), (0, (mine, 0)), (2, (mine, 1))):
        for block, value in enumerate(units(nn(grad_turned, hidden[:, shard * width : (shard + 1) * width]))):
            segments.put(home, at, block, value)


def enc_up_kernel(pos, rows_at, grad, middle, gain, slope, *refs):
    ups, downs, (mine, theirs, grad_mid, d_gain) = refs[:6], refs[6:12], refs[12:]
    width = ups[0].shape[1]
    value = middle[...]
    segments = Segments(value.shape[1], width)
    n_two, r_two = norm(value)
    b_turned = turned(rows_at[...], (n_two * gain[...]).astype(BF))
    homes = ((mine, 0), (theirs, 0), (mine, 1), (theirs, 1))
    low = grad[...].astype(BF)
    d_b = jnp.zeros_like(value)
    pieces = hidden_pieces(pos[1], ups, width)
    for piece in (1, 4, 5, 0, 2, 3):
        up, first, size = pieces[piece]
        shard = (0, 1, 2, 2, 3, 3)[piece]
        d_pre = (nt(low, downs[piece][...]) * slope[:, columns(first, size)].astype(F32)).astype(BF)
        d_b = d_b + nt(d_pre, up[...])
        home, at = homes[shard]
        first_block = (first - shard * width) // 128
        for block, part in enumerate(units(nn(b_turned, d_pre))):
            segments.put(home, at, first_block + block, part)
    d_middle, d_gain_two = norm_back(n_two, r_two, gain[...], d_b)
    grad_mid[...] = grad[...] + d_middle
    d_gain[...] = d_gain_two


def enc_attn_back_kernel(
    pos, rows_at, x, gain, grad, qkv, probs, mixed, d_embedded, enc, smalls, own, core, d_x, e_x, d_c, e_c,
    mine, theirs, d_input, far, d_mixed, d_qkv,
):
    me, side = pos[0], pos[1]
    half = d_x.shape[0]
    per = own.shape[0] // 4 // HEAD_DIM
    cols = per * HEAD_DIM
    for at, (first, second) in enumerate(((d_x, e_x), (d_c, e_c))):
        far[at, pl.ds(pl.multiple_of(side * half, half), half), :] = first[...]
        far[at, pl.ds(pl.multiple_of((1 - side) * half, half), half), :] = second[...]
    packs = (own, core, far.at[0], far.at[1])
    low = grad[...].astype(BF)
    for shard, pack in enumerate(packs):
        d_mixed[shard * cols : (shard + 1) * cols, :] = nt(pack[3 * cols :, :], low).astype(BF)
    attend_back(qkv, probs, d_mixed, d_qkv, per, HEAD_DIM)
    value = x[...].astype(F32)
    length, width = value.shape
    normed, inverse = norm(value)
    d_a = jnp.zeros_like(value)
    for shard in range(SHARDS):
        d_a = d_a + tn(d_qkv[shard * 3 * cols : (shard + 1) * 3 * cols, :], packs[shard][: 3 * cols, :])
    d_value, d_gain_one = norm_back(normed, inverse, gain[...], d_a)
    for at, block in enumerate(units(grad[...] + d_value)):
        d_input[at * length : (at + 1) * length, :] = block.astype(BF)

    source = rows_at[...]
    a_turned = turned(source, (normed * gain[...]).astype(BF))
    mid_turned = turned(source, low)
    channels = d_embedded.shape[1]
    e_cols = channels // SHARDS
    row = lax.broadcasted_iota(jnp.int32, (channels, SHARDS * 128), 0)
    column = lax.broadcasted_iota(jnp.int32, (channels, SHARDS * 128), 1)
    within = column & 127
    one_hot = ((((column >> 7) ^ me) * e_cols + within == row) & (within < e_cols)).astype(BF)
    g_embed = nn(turned(source, enc[...]), nn(d_embedded[...], one_hot).astype(BF))
    which = lax.broadcasted_iota(jnp.int32, smalls.shape, 0)
    lines = jnp.where(which == 0, d_gain_one, smalls[...]).astype(BF)
    lane = lax.broadcasted_iota(jnp.int32, (smalls.shape[0], 128), 1)
    line = lax.broadcasted_iota(jnp.int32, (smalls.shape[0], 128), 0)
    g_small = nn(turned(source, lines), (lane == line + e_cols).astype(BF))

    segments = Segments(width, 4 * cols + 128)
    homes = ((mine, 0), (theirs, 0), (mine, 1), (theirs, 1))
    for shard in (1, 3, 0, 2):
        home, at = homes[shard]
        g_qkv = nt(a_turned, d_qkv[shard * 3 * cols : (shard + 1) * 3 * cols, :])
        g_out = nt(mid_turned, mixed[shard * cols : (shard + 1) * cols, :])
        blocks = units(jnp.concatenate([g_qkv, g_out], 1)) + [g_embed[:, shard * 128 : (shard + 1) * 128] + g_small]
        for block, part in enumerate(blocks):
            segments.put(home, at, block, part)


def in_order_kernel(pos, own, core, x, xc, out):
    length = out.shape[1]
    for shard, ref in enumerate((own, core, x, xc)):
        for at in range(out.shape[2] // 128):
            out[pos[0] ^ shard, :, at * 128 : (at + 1) * 128] = ref[at * length : (at + 1) * length, :]


def swap(value, axis, bit):
    size = lax.axis_size(axis)
    return lax.ppermute(value, axis, [(i, i ^ bit) for i in range(size)])


def pick(value, index, axis=0):
    return lax.dynamic_index_in_dim(value, index, axis, keepdims=False)


def send_last(kept, segments):
    size = lax.axis_size("dp")
    groups = [[i for i in range(size) if i % 2 == side] for side in range(2)]
    kept = kept.reshape(segments.left + segments.right, size // 2, -1, 128)
    return lax.all_to_all(jnp.swapaxes(kept, 0, 1), "dp", 0, 0, axis_index_groups=groups, tiled=True)


def summed(parts):
    total = jnp.sum(parts.astype(F32), 0)
    return jnp.swapaxes(total, 0, 1).reshape(total.shape[1], -1)


def source_rows(width, side):
    size = lax.axis_size("dp")
    blocks = jnp.arange(width, dtype=jnp.int32).reshape(size // 2, 2, width // size)
    order = jnp.where(side == 0, blocks, blocks[:, ::-1])
    return jnp.swapaxes(order, 0, 1).reshape(width, 1)


def body(
    patches, segment_ids, mask_slots, gain_attn, qkv_weight, out_weight, gain_mlp, up_weight, down_weight,
    embed_weight, mask_token, pred_gain_attn, pred_qkv, pred_out, pred_gain_mlp, pred_up, pred_down, cotangent,
):
    me = lax.axis_index("mp")
    side = lax.axis_index("dp") % 2
    dp_size = lax.axis_size("dp")
    length, width = patches.shape[1:]
    channels = cotangent.shape[2]
    cols, hid = qkv_weight.shape[2], up_weight.shape[1]
    p_cols, p_hid = pred_qkv.shape[2], pred_up.shape[1]
    heads = SHARDS * cols // HEAD_DIM
    p_heads = SHARDS * p_cols // P_HEAD_DIM
    pos = jnp.stack([me, side]).astype(jnp.int32)

    attn_own, attn_direct = call(
        pack_attn_kernel, [((4 * cols, width), BF), ((2 * cols, width), BF)], (pos, qkv_weight, out_weight), 1
    )
    up_direct, down_direct = call(
        pack_mlp_kernel, [((width, hid // 2), BF), ((hid // 2, width), BF)],
        (pos, up_weight, down_weight), 1, tokens=(attn_direct,),
    )
    p_attn_own, p_mlp_own = call(
        pack_pred_kernel,
        [((2, 3 * p_cols, channels), BF), ((2, 2, p_hid // 2, channels), BF)],
        (pos, pred_qkv, pred_out, embed_weight, pred_up, pred_down), 2, tokens=(up_direct,),
    )

    attn_core, up_core, down_core = swap(attn_own, "mp", 1), swap(up_weight, "mp", 1), swap(down_weight, "mp", 1)
    p_attn_core, p_mlp_core = swap(p_attn_own, "mp", 1), swap(p_mlp_own, "mp", 1)
    attn_x = swap(attn_direct, "mp", 2)
    up_x = swap(up_direct, "mp", 2)
    attn_y = swap(attn_x, "dp", 1)
    (down_direct,) = gate([down_direct], [attn_x])
    down_x = swap(down_direct, "mp", 2)
    up_y = swap(up_x, "dp", 1)
    (p_attn_own,) = gate([p_attn_own], [up_x])
    p_attn_x = swap(p_attn_own, "mp", 2)
    attn = (attn_own, attn_core, attn_x, attn_y, swap(attn_x, "mp", 1), swap(attn_y, "mp", 1))

    x = pick(patches, me)
    segments = pick(segment_ids, me)
    seg_row, seg_col = segments[None, :], segments[:, None]
    slots = pick(mask_slots, me)
    masked = jnp.any(jnp.arange(length, dtype=jnp.int32)[:, None] == slots[None, :], -1, keepdims=True).astype(F32)
    cot = pick(cotangent, me)
    row = lambda gain: gain.astype(F32)[None, :]
    rows_at, p_rows_at = source_rows(width, side), source_rows(channels, side)

    middle, qkv, probs, mixed = call(
        enc_attn_kernel,
        [((length, width), F32), ((3 * width, length), BF), ((heads, length, length), BF), ((width, length), BF)],
        (pos, x, seg_row, seg_col, row(gain_attn)) + attn, 9,
        [((2, 4 * cols, width), BF)], tokens=(up_x,),
    )
    up_y, down_x, p_mlp_own = gate([up_y, down_x, p_mlp_own], [middle])
    up = (up_weight, up_core, up_x, up_y, swap(up_x, "mp", 1), swap(up_y, "mp", 1))
    down_y = swap(down_x, "dp", 1)
    p_mlp_x = swap(p_mlp_own, "mp", 2)
    hidden, slope = call(
        enc_up_forward_kernel, [((length, SHARDS * hid), BF), ((length, SHARDS * hid), BF)],
        (pos, middle, row(gain_mlp)) + up, 6, tokens=(down_x,),
    )
    down_y, p_attn_x = gate([down_y, p_attn_x], [hidden])
    down = (down_weight, down_core, down_x, down_y, swap(down_x, "mp", 1), swap(down_y, "mp", 1))
    p_attn = (p_attn_own, p_attn_core, p_attn_x, swap(p_attn_x, "mp", 1))
    (enc,) = call(enc_down_forward_kernel, [((length, width), BF)], (pos, middle, hidden) + down, 4)
    (p_mlp_x,) = gate([p_mlp_x], [enc])
    p_mlp = (p_mlp_own, p_mlp_core, p_mlp_x, swap(p_mlp_x, "mp", 1))
    p_seg, d_seg = Segments(channels, 4 * p_cols + 2 * p_hid), Segments(width, hid)
    u_seg, a_seg = Segments(width, hid), Segments(width, 4 * cols + 128)
    p_blocks, x_blocks = channels // 128, width // 128
    predicted, stats, p_mine, p_theirs, d_embedded, d_enc, p_d_gains = call(
        pred_kernel,
        [((p_blocks * length, 128), BF), ((2, channels), F32), (p_seg.shape, BF), (p_seg.shape, BF), ((length, channels), BF),
         ((length, width), F32), ((3, channels), F32)],
        (pos, enc, seg_row, seg_col, masked, row(mask_token), row(pred_gain_attn), row(pred_gain_mlp), cot, p_rows_at)
        + p_attn + p_mlp, 30,
        [((3 * channels, channels), BF), ((channels, channels), BF), ((channels, width), BF),
         ((SHARDS * p_hid, channels), BF), ((SHARDS * p_hid, channels), BF), ((3 * channels, length), BF),
         ((p_heads, length, length), BF), ((channels, length), BF), ((channels, length), BF),
         ((3 * channels, length), BF)],
    )

    def hop(value, axis, bit):
        return value + swap(value, axis, bit)

    p_away, stats = swap(p_theirs, "mp", 1), hop(stats, "mp", 1)
    d_mine, d_theirs = call(enc_down_kernel, [(d_seg.shape, BF)] * 2, (pos, rows_at, d_enc, hidden), 4)

    p_own = (p_mine, p_away)
    send_x, send_y = combine(
        [[[(g, *p_seg.over_x) for g in p_own], [(predicted, 0, predicted.shape[0])]], [[(g, *p_seg.over_y) for g in p_own]]],
        [d_theirs],
    )
    (stats,) = gate([stats], [send_x])
    d_away, got_x, got_y, stats = swap(d_theirs, "mp", 1), swap(send_x, "mp", 2), swap(send_y, "dp", 1), hop(stats, "mp", 2)
    p_x, p_y = (got_x, 0, 2 * p_seg.a), (got_y, 0, 2 * p_seg.b)
    u_mine, u_theirs, grad_mid, d_gain_two = call(
        enc_up_kernel,
        [(u_seg.shape, BF), (u_seg.shape, BF), ((length, width), F32), ((1, width), F32)],
        (pos, rows_at, d_enc, middle, row(gain_mlp), slope) + up + down, 14, tokens=(send_x, send_y),
    )

    def first(terms, part):
        return (terms[0], terms[1], part)

    def second(terms, part):
        return (terms[0], terms[1] + part, part)

    d_own = (d_mine, d_away)
    predicted_x = lax.slice_in_dim(got_x, 2 * p_seg.a, got_x.shape[0])
    send_x, send_y = combine(
        [[[(g, *d_seg.over_x) for g in d_own], [(g, *p_seg.then_x) for g in p_own] + [second(p_y, p_seg.b)]],
         [[(g, *d_seg.over_y) for g in d_own], [(g, *p_seg.then_y) for g in p_own] + [second(p_x, p_seg.a)]]],
        [u_theirs],
    )
    predicted, predicted_x, stats = gate([predicted, predicted_x, stats], [send_x])
    u_away, got_x, got_y, stats = swap(u_theirs, "mp", 1), swap(send_x, "mp", 2), swap(send_y, "dp", 1), hop(stats, "dp", 1)
    predicted_c, predicted_xc = swap(predicted, "mp", 1), swap(predicted_x, "mp", 1)
    d_x, p_then_x = (got_x, 0, 2 * d_seg.a), (got_x, 2 * d_seg.a, p_seg.b)
    d_y, p_then_y = (got_y, 0, 2 * d_seg.b), (got_y, 2 * d_seg.b, p_seg.a)
    by_block = lambda left, right: jnp.concatenate([left.reshape(dp_size, -1), right.reshape(dp_size, -1)], 1).reshape(1, width)
    zeros = jnp.zeros((channels,), F32)
    smalls = jnp.concatenate(
        [jnp.zeros((1, width), F32), d_gain_two, by_block(p_d_gains[0], p_d_gains[1]), by_block(p_d_gains[2], zeros),
         jnp.zeros((4, width), F32)]
    )
    a_mine, a_theirs, d_input = call(
        enc_attn_back_kernel,
        [(a_seg.shape, BF), (a_seg.shape, BF), ((x_blocks * length, 128), BF)],
        (pos, rows_at, x, row(gain_attn), grad_mid, qkv, probs, mixed, d_embedded, enc, smalls) + attn, 14,
        [((2, 4 * cols, width), BF), ((width, length), BF), ((3 * width, length), BF)], tokens=(send_x, send_y),
    )

    def kept(own, seg, over_x, over_y, then_x, then_y):
        return [[(g, *seg.keep_left) for g in own] + [first(over_x, seg.a), then_y],
                [(g, *seg.keep_right) for g in own] + [first(over_y, seg.b), then_x]]

    u_own = (u_mine, u_away)
    send_x, send_y, p_kept = combine(
        [[[(g, *u_seg.over_x) for g in u_own], [(g, *d_seg.then_x) for g in d_own] + [second(d_y, d_seg.b)],
          [(d_input, 0, d_input.shape[0])]],
         [[(g, *u_seg.over_y) for g in u_own], [(g, *d_seg.then_y) for g in d_own] + [second(d_x, d_seg.a)]],
         kept(p_own, p_seg, p_x, p_y, p_then_x, p_then_y)],
        [a_theirs, predicted_c, predicted_xc],
    )
    stats, d_input = gate([stats, d_input], [send_x])
    a_away, got_x, got_y = swap(a_theirs, "mp", 1), swap(send_x, "mp", 2), swap(send_y, "dp", 1)
    p_parts, input_c = send_last(p_kept, p_seg), swap(d_input, "mp", 1)
    u_x, d_then_x = (got_x, 0, 2 * u_seg.a), (got_x, 2 * u_seg.a, d_seg.b)
    u_y, d_then_y = (got_y, 0, 2 * u_seg.b), (got_y, 2 * u_seg.b, d_seg.a)
    (predictions,) = call(
        in_order_kernel, [((SHARDS, length, channels), BF)], (pos, predicted, predicted_c, predicted_x, predicted_xc), 2,
        tokens=(send_x, send_y),
    )

    a_own = (a_mine, a_away)
    input_x = lax.slice_in_dim(got_x, 2 * u_seg.a + d_seg.b, got_x.shape[0])
    send_x, send_y, d_kept = combine(
        [[[(g, *a_seg.over_x) for g in a_own], [(g, *u_seg.then_x) for g in u_own] + [second(u_y, u_seg.b)]],
         [[(g, *a_seg.over_y) for g in a_own], [(g, *u_seg.then_y) for g in u_own] + [second(u_x, u_seg.a)]],
         kept(d_own, d_seg, d_x, d_y, d_then_x, d_then_y)],
        [predictions, p_parts, input_c],
    )
    input_x, p_parts = gate([input_x, p_parts], [send_x])
    got_x, got_y, d_parts, input_xc = swap(send_x, "mp", 2), swap(send_y, "dp", 1), send_last(d_kept, d_seg), swap(input_x, "mp", 1)
    a_x, u_then_x = (got_x, 0, 2 * a_seg.a), (got_x, 2 * a_seg.a, u_seg.b)
    a_y, u_then_y = (got_y, 0, 2 * a_seg.b), (got_y, 2 * a_seg.b, u_seg.a)
    r_pred = summed(p_parts)

    send_x, send_y, u_kept = combine(
        [[[(g, *a_seg.then_x) for g in a_own] + [second(a_y, a_seg.b)]], [[(g, *a_seg.then_y) for g in a_own] + [second(a_x, a_seg.a)]],
         kept(u_own, u_seg, u_x, u_y, u_then_x, u_then_y)],
        [r_pred, d_parts, input_xc],
    )
    (d_parts,) = gate([d_parts], [send_x])
    got_x, got_y, u_parts = swap(send_x, "mp", 2), swap(send_y, "dp", 1), send_last(u_kept, u_seg)
    r_down = summed(d_parts)
    (patches_grad,) = call(
        in_order_kernel, [((SHARDS, length, width), BF)], (pos, d_input, input_c, input_x, input_xc), 2, tokens=(send_x, send_y)
    )
    (stats,) = gate([stats], [send_x])
    bit = 2
    while bit < dp_size:
        stats = hop(stats, "dp", bit)
        bit *= 2

    (a_kept,) = combine([kept(a_own, a_seg, a_x, a_y, (got_x, 0, a_seg.b), (got_y, 0, a_seg.a))], [patches_grad])
    a_parts = send_last(a_kept, a_seg)
    r_up, r_attn = summed(u_parts), summed(a_parts)

    count = dp_size * patches.shape[0] * length
    mean, square = stats[0] / count, stats[1] / count
    n_var = channels // SHARDS
    variance = lax.dynamic_slice_in_dim(square - mean * mean, me * n_var, n_var)
    tail = r_attn[:, 4 * cols + p_cols :]
    n_small = channels // dp_size

    def qkv_of(block, n):
        return jnp.stack([block[:, i * n : (i + 1) * n] for i in range(3)])

    return (
        predictions,
        patches_grad,
        variance,
        tail[:, 0],
        qkv_of(r_attn, cols),
        r_attn[:, 3 * cols : 4 * cols].T,
        tail[:, 1],
        r_up,
        r_down.T,
        r_attn[:, 4 * cols : 4 * cols + p_cols],
        tail[:n_small, 3],
        tail[:n_small, 2],
        qkv_of(r_pred, p_cols),
        r_pred[:, 3 * p_cols : 4 * p_cols].T,
        tail[n_small:, 2],
        r_pred[:, 4 * p_cols : 4 * p_cols + p_hid],
        r_pred[:, 4 * p_cols + p_hid :].T,
    )


def solution(mesh):
    placed = (
        P("dp", None, None), P("dp", None), P("dp", None), P(), P(None, None, "mp"), P("mp", None), P(),
        P(None, "mp"), P("mp", None), P(None, "mp"), P(), P(), P(None, None, "mp"), P("mp", None), P(),
        P(None, "mp"), P("mp", None), P("dp", None, None),
    )
    return jax.shard_map(
        body,
        mesh=mesh,
        in_specs=placed,
        out_specs=(
            P("dp", None, None), P("dp", None, None), P("mp"), P("dp"), P(None, "dp", "mp"), P("mp", "dp"),
            P("dp"), P("dp", "mp"), P("mp", "dp"), P("dp", "mp"), P("dp"), P("dp"), P(None, "dp", "mp"),
            P("mp", "dp"), P("dp"), P("dp", "mp"), P("mp", "dp"),
        ),
        check_vma=False,
    )
```

profile of v0, /device:TPU:0, one launch (start us, length us, event | category | flops | bytes accessed | tf_op | source)
XLA Modules:
  0.0 309.8 jit_solution(13284207519440516381)
XLA Ops:
  4.4 3.0 collective-permute-start.1
  7.4 13.4 %collective-permute-done.1.refs_7_.refs_1_.refs_13_ = bf16[384,768]{1,0:T(8,128)(2,1)} collective-permute-done((bf16[384,768]{1,0:T(8,128)(2,1)S(1)}, bf16[384,768]{1,0:T(8,128)(2,1)}, u32[]{:S(2)}, u32[]{:S(2)}) %collective-permute-start.1) | collective-permute-done | bytes 589856 | tf_op jit(solution)/shard_map/ppermute | solution.py:477
  22.6 2.2 shard_map.306
  28.1 7.6 %collective-permute-done.2.refs_8_.refs_14_ = bf16[384,768]{1,0:T(8,128)(2,1)} collective-permute-done((bf16[384,768]{1,0:T(8,128)(2,1)}, bf16[384,768]{1,0:T(8,128)(2,1)}, u32[]{:S(2)}, u32[]{:S(2)}) %collective-permute-start.2) | collective-permute-done | bytes 589856 | tf_op jit(solution)/shard_map/ppermute | solution.py:477
  41.8 9.6 %shard_map.307 = (f32[256,768]{1,0:T(8,128)S(1)}, bf16[2304,256]{1,0:T(8,128)(2,1)S(1)}, bf16[12,256,256]{2,1,0:T(8,128)(2,1)}, bf16[768,256]{1,0:T(8,128)(2,1)S(1)}) custom-call(s32[2]{0:T(128)S(1)} %pad_add_fusion.refs_0_, bf16[256,768]{1,0:T(8,128)(2,1)S(1)} %dynamic-slice_bitcast_fusion.refs_1_.refs_2_, ...), custom_call_target="tpu_custom_call" | custom-call | flops 89999998976 | bytes 9049096 | tf_op jit(solution)/shard_map/pallas_call | solution.py:113
  58.4 2.6 collective-permute-done.16.refs_11_
  66.1 6.2 %shard_map.311 = (bf16[256,3072]{1,0:T(8,128)(2,1)}, bf16[256,3072]{1,0:T(8,128)(2,1)}) custom-call(s32[2]{0:T(128)S(1)} %pad_add_fusion.refs_0_, f32[256,768]{1,0:T(8,128)S(1)} %copy-done.12, f32[1,768]{1,0:T(1,128)S(1)} %reshape.156.refs_2_.refs_4_, bf16[768,768]{1,0:T(8,128)(2,1)} %refs_6_.1, bf16[768,768]{1,0:T(8,128)(2,1)} %collective-permute-done.6.refs_4_.refs_7_, ...), custom_call_target="tpu_custom_call" | custom-call | flops 60000002048 | bytes 8653832 | tf_op jit(solution)/shard_map/pallas_call | solution.py:113
  73.4 3.4 %collective-permute-done.12.refs_0_ = bf16[384,768]{1,0:T(8,128)(2,1)S(1)} collective-permute-done((bf16[384,768]{1,0:T(8,128)(2,1)}, bf16[384,768]{1,0:T(8,128)(2,1)S(1)}, u32[]{:S(2)}, u32[]{:S(2)}) %collective-permute-start.12) | collective-permute-done | bytes 589856 | tf_op jit(solution)/shard_map/ppermute | solution.py:477
  82.3 3.7 %shard_map.314.refs_1_.refs_9_ = bf16[256,768]{1,0:T(8,128)(2,1)S(1)} custom-call(s32[2]{0:T(128)S(1)} %pad_add_fusion.refs_0_, f32[256,768]{1,0:T(8,128)S(1)} %copy-done.12, bf16[256,3072]{1,0:T(8,128)(2,1)} %get-tuple-element.78.refs_2_.refs_3_, bf16[768,768]{1,0:T(8,128)(2,1)S(1)} %copy-done.51, ...), custom_call_target="tpu_custom_call" | custom-call | flops 40000000000 | bytes 7471112 | tf_op jit(solution)/shard_map/pallas_call | solution.py:113
  86.8 6.6 %collective-permute-done.19.refs_0_ = bf16[2,2,192,384]{3,2,1,0:T(8,128)(2,1)S(1)} collective-permute-done((bf16[2,2,192,384]{3,2,1,0:T(8,128)(2,1)S(1)}, bf16[2,2,192,384]{3,2,1,0:T(8,128)(2,1)S(1)}, u32[]{:S(2)}, u32[]{:S(2)}) %collective-permute-start.19) | collective-permute-done | bytes 589856 | tf_op jit(solution)/shard_map/ppermute | solution.py:477
  100.7 20.0 %shard_map.316 = (bf16[768,128]{1,0:T(8,128)(2,1)S(1)}, f32[2,384]{1,0:T(2,128)S(1)}, bf16[6912,128]{1,0:T(8,128)(2,1)}, bf16[6912,128]{1,0:T(8,128)(2,1)}, bf16...) custom-call(s32[2]{0:T(128)S(1)} %pad_add_fusion.refs_0_, bf16[256,768]{1,0:T(8,128)(2,1)S(1)} %copy-done.39, ...), custom_call_target="tpu_custom_call" | custom-call | flops 299999985664 | bytes 9454088 | tf_op jit(solution)/shard_map/pallas_call | solution.py:113
  123.6 3.7 %shard_map.317 = (bf16[9216,128]{1,0:T(8,128)(2,1)S(1)}, bf16[9216,128]{1,0:T(8,128)(2,1)}) custom-call(s32[2]{0:T(128)S(1)} %pad_add_fusion.refs_0_, s32[768,1]{1,0:T(8,128)S(1)} %reshape.162.refs_1_, f32[256,768]{1,0:T(8,128)S(1)} %copy-done.81, bf16[256,3072]{1,0:T(8,128)(2,1)S(1)} %copy-done.5), custom_call_target="tpu_custom_call" | custom-call | flops 40000000000 | bytes 7080968 | tf_op jit(solution)/shard_map/pallas_call | solution.py:113
  135.1 3.1 shard_map.318
  143.0 12.2 %shard_map.320 = (bf16[9216,128]{1,0:T(8,128)(2,1)}, bf16[9216,128]{1,0:T(8,128)(2,1)}, f32[256,768]{1,0:T(8,128)}, f32[1,768]{1,0:T(1,128)S(1)}) custom-call(s32[2]{0:T(128)S(1)} %pad_add_fusion.refs_0_, s32[768,1]{1,0:T(8,128)S(1)} %copy-done.35, f32[256,768]{1,0:T(8,128)} %get-tuple-element.86.refs_2_, f32[256,768]{1,0:T(8,128)} %copy-done.11, ...), custom_call_target="tpu_custom_call" | custom-call | flops 140000002048 | bytes 18097160 | tf_op jit(solution)/shard_map/pallas_call | solution.py:113
  157.5 2.4 shard_map.321
  166.5 16.4 %shard_map.323 = (bf16[10752,128]{1,0:T(8,128)(2,1)}, bf16[10752,128]{1,0:T(8,128)(2,1)}, bf16[1536,128]{1,0:T(8,128)(2,1)S(1)}) custom-call(s32[2]{0:T(128)S(1)} %pad_add_fusion.refs_0_, s32[768,1]{1,0:T(8,128)S(1)} %copy-done.35, bf16[256,768]{1,0:T(8,128)(2,1)S(1)} %copy-done.37, f32[1,768]{1,0:T(1,128)S(1)} %copy-done.47, f32[256,768]{1,0:T(8,128)S(1)} %copy-done.85, ...), custom_call_target="tpu_custom_call" | custom-call | flops 140000002048 | bytes 15562760 | tf_op jit(solution)/shard_map/pallas_call | solution.py:113
  184.0 4.3 %shard_map.324 = (bf16[4992,128]{1,0:T(8,128)(2,1)}, bf16[3456,128]{1,0:T(8,128)(2,1)S(1)}, bf16[1728,128]{1,0:T(8,128)(2,1)S(1)}) custom-call(bf16[9216,128]{1,0:T(8,128)(2,1)} %get-tuple-element.97.refs_0_.refs_2_.refs_4_, bf16[9216,128]{1,0:T(8,128)(2,1)} %collective-permute-done.29.refs_1_.refs_3_.refs_5_, bf16[9216,128]{1,0:T(8,128)(2,1)} %copy-done.78, ...), custom_call_target="tpu_custom_call" | custom-call | flops 30000001024 | bytes 8896512 | tf_op jit(solution)/shard_map/pallas_call | solution.py:209
  191.6 4.9 %all-to-all-start = ((bf16[4,9,48,128]{3,2,1,0:T(8,128)(2,1)}), bf16[4,9,48,128]{3,2,1,0:T(8,128)(2,1)S(1)}, u32[]{:S(2)}, u32[]{:S(2)}) async-start(bf16[4,9,48,128]{3,2,1,0:T(8,128)(2,1)} %bitcast.83), calls=%async_computation | async-start | bytes 884736 | tf_op jit(solution)/shard_map/all_to_all | solution.py:488
  199.0 10.6 %all-to-all-done.refs_11_.refs_1_ = bf16[4,9,48,128]{3,2,1,0:T(8,128)(2,1)S(1)} async-done(((bf16[4,9,48,128]{3,2,1,0:T(8,128)(2,1)}), bf16[4,9,48,128]{3,2,1,0:T(8,128)(2,1)S(1)}, u32[]{:S(2)}, u32[]{:S(2)}) %all-to-all-start) | async-done | bytes 442400 | tf_op jit(solution)/shard_map/all_to_all | solution.py:488
  209.6 2.1 collective-permute-done.36.refs_4_.refs_7_
  211.8 7.1 %collective-permute-done.34.refs_5_.refs_6_ = bf16[4992,128]{1,0:T(8,128)(2,1)} collective-permute-done((bf16[4992,128]{1,0:T(8,128)(2,1)}, bf16[4992,128]{1,0:T(8,128)(2,1)}, u32[]{:S(2)}, u32[]{:S(2)}) %collective-permute-start.34) | collective-permute-done | bytes 1277984 | tf_op jit(solution)/shard_map/ppermute | solution.py:477
  222.3 4.0 %shard_map.327 = (bf16[3456,128]{1,0:T(8,128)(2,1)S(1)}, bf16[4224,128]{1,0:T(8,128)(2,1)}, bf16[2304,128]{1,0:T(8,128)(2,1)S(1)}) custom-call(bf16[10752,128]{1,0:T(8,128)(2,1)} %get-tuple-element.113.refs_0_, bf16[10752,128]{1,0:T(8,128)(2,1)} %collective-permute-done.35.refs_1_, bf16[9216,128]{1,0:T(8,128)(2,1)} %get-tuple-element.97.refs_0_.refs_2_.refs_4_, ...), custom_call_target="tpu_custom_call" | custom-call | flops 30000001024 | bytes 9437184 | tf_op jit(solution)/shard_map/pallas_call | solution.py:209
  232.5 4.9 %all-to-all-start.1 = ((bf16[4,6,96,128]{3,2,1,0:T(8,128)(2,1)}), bf16[4,6,96,128]{3,2,1,0:T(8,128)(2,1)S(1)}, u32[]{:S(2)}, u32[]{:S(2)}) async-start(bf16[4,6,96,128]{3,2,1,0:T(8,128)(2,1)} %bitcast.82), calls=%async_computation.1 | async-start | bytes 1179648 | tf_op jit(solution)/shard_map/all_to_all | solution.py:488
  239.4 9.5 %collective-permute-done.39.refs_3_.refs_2_ = bf16[3456,128]{1,0:T(8,128)(2,1)} collective-permute-done((bf16[3456,128]{1,0:T(8,128)(2,1)S(1)}, bf16[3456,128]{1,0:T(8,128)(2,1)}, u32[]{:S(2)}, u32[]{:S(2)}) %collective-permute-start.39) | collective-permute-done | bytes 884768 | tf_op jit(solution)/shard_map/ppermute | solution.py:477
  248.9 5.0 %all-to-all-done.1.refs_9_.refs_0_ = bf16[4,6,96,128]{3,2,1,0:T(8,128)(2,1)S(1)} async-done(((bf16[4,6,96,128]{3,2,1,0:T(8,128)(2,1)}), bf16[4,6,96,128]{3,2,1,0:T(8,128)(2,1)S(1)}, u32[]{:S(2)}, u32[]{:S(2)}) %all-to-all-start.1) | async-done | bytes 589856 | tf_op jit(solution)/shard_map/all_to_all | solution.py:488
  257.4 3.0 shard_map.329
  263.0 4.2 %all-to-all-start.3 = ((bf16[4,6,96,128]{3,2,1,0:T(8,128)(2,1)}), bf16[4,6,96,128]{3,2,1,0:T(8,128)(2,1)}, u32[]{:S(2)}, u32[]{:S(2)}) async-start(bf16[4,6,96,128]{3,2,1,0:T(8,128)(2,1)} %bitcast.81), calls=%async_computation.3 | async-start | bytes 1179648 | tf_op jit(solution)/shard_map/all_to_all | solution.py:488
  267.2 2.5 shard_map.330.refs_6_
  275.0 7.4 %all-to-all-done.3 = bf16[4,6,96,128]{3,2,1,0:T(8,128)(2,1)} async-done(((bf16[4,6,96,128]{3,2,1,0:T(8,128)(2,1)}), bf16[4,6,96,128]{3,2,1,0:T(8,128)(2,1)}, u32[]{:S(2)}, u32[]{:S(2)}) %all-to-all-start.3) | async-done | bytes 589856 | tf_op jit(solution)/shard_map/all_to_all | solution.py:488
  282.4 3.5 %all-to-all-start.2 = ((bf16[4,7,96,128]{3,2,1,0:T(8,128)(2,1)}), bf16[4,7,96,128]{3,2,1,0:T(8,128)(2,1)S(1)}, u32[]{:S(2)}, u32[]{:S(2)}) async-start(bf16[4,7,96,128]{3,2,1,0:T(8,128)(2,1)} %bitcast.73), calls=%async_computation.2 | async-start | bytes 1376256 | tf_op jit(solution)/shard_map/all_to_all | solution.py:488
  286.1 2.9 collective-permute-start.41
  289.7 13.8 %collective-permute-done.41 = f32[2,384]{1,0:T(2,128)S(1)} collective-permute-done((f32[2,384]{1,0:T(2,128)S(1)}, f32[2,384]{1,0:T(2,128)S(1)}, u32[]{:S(2)}, u32[]{:S(2)}) %collective-permute-start.41) | collective-permute-done | bytes 3104 | tf_op jit(solution)/shard_map/ppermute | solution.py:477
  (362 shorter events, 102.5 us)
Async XLA Ops:
  4.4 16.4 %collective-permute-start.1 = (bf16[384,768]{1,0:T(8,128)(2,1)S(1)}, bf16[384,768]{1,0:T(8,128)(2,1)}, u32[]{:S(2)}, u32[]{:S(2)}) collective-permute-start(bf16[384,768]{1,0:T(8,128)(2,1)S(1)} %get-tuple-element.71.refs_3_), channel_id=1, source_target_pairs={{0,2},{1,3},{2,0},{3,1},{4,6},{5,7},{6,4},{7,5},{8,10},{9,11},{10,... | collective-permute-start | bytes 1769480 | tf_op jit(solution)/shard_map/ppermute | solution.py:477
  7.4 54.7 %collective-permute-start.6 = (bf16[768,768]{1,0:T(8,128)(2,1)}, bf16[768,768]{1,0:T(8,128)(2,1)}, u32[]{:S(2)}, u32[]{:S(2)}) collective-permute-start(bf16[768,768]{1,0:T(8,128)(2,1)} %refs_6_.1), channel_id=1, source_target_pairs={{0,1},{1,0},{2,3},{3,2},{4,5},{5,4},{6,7},{7,6},{8,9},{9,8},{10,11... | collective-permute-start | bytes 3538952 | tf_op jit(solution)/shard_map/ppermute | solution.py:477
  20.8 14.8 %collective-permute-start.2 = (bf16[384,768]{1,0:T(8,128)(2,1)}, bf16[384,768]{1,0:T(8,128)(2,1)}, u32[]{:S(2)}, u32[]{:S(2)}) collective-permute-start(bf16[384,768]{1,0:T(8,128)(2,1)} %collective-permute-done.1.refs_7_.refs_1_.refs_13_), channel_id=1, source_target_pairs={{0,4},{4,0},{8,12},{12,8},{16,20},{20,16},{24,28},{28,24},{1,5},{5... | collective-permute-start | bytes 1769480 | tf_op jit(solution)/shard_map/ppermute | solution.py:477
  27.1 14.2 %collective-permute-start = (bf16[768,768]{1,0:T(8,128)(2,1)}, bf16[768,768]{1,0:T(8,128)(2,1)}, u32[]{:S(2)}, u32[]{:S(2)}) collective-permute-start(bf16[768,768]{1,0:T(8,128)(2,1)} %get-tuple-element.70.refs_5_.refs_11_), channel_id=1, source_target_pairs={{0,1},{1,0},{2,3},{3,2},{4,5},{5,4},{6,7},{7,6},{8,9},{9,8},{10,11... | collective-permute-start | bytes 3538952 | tf_op jit(solution)/shard_map/ppermute | solution.py:477
  39.8 14.3 %collective-permute-start.18 = (bf16[2,2,192,384]{3,2,1,0:T(8,128)(2,1)S(1)}, bf16[2,2,192,384]{3,2,1,0:T(8,128)(2,1)S(1)}, u32[]{:S(2)}, u32[]{:S(2)}) collective-permute-start(bf16[2,2,192,384]{3,2,1,0:T(8,128)(2,1)S(1)} %get-tuple-element.75.refs_2_), channel_id=1, source_target_pairs={{0,1},{1,0},{2,3},{3,2},{4,5},{5,4},{6,7},{7,6},{8,9},{9,8},{10,11... | collective-permute-start | bytes 1769480 | tf_op jit(solution)/shard_map/ppermute | solution.py:477
  39.8 16.0 %collective-permute-start.8 = (bf16[384,768]{1,0:T(8,128)(2,1)}, bf16[384,768]{1,0:T(8,128)(2,1)S(1)}, u32[]{:S(2)}, u32[]{:S(2)}) collective-permute-start(bf16[384,768]{1,0:T(8,128)(2,1)} %shard_map.308), channel_id=1, source_target_pairs={{0,2},{1,3},{2,0},{3,1},{4,6},{5,7},{6,4},{7,5},{8,10},{9,11},{10,... | collective-permute-start | bytes 1769480 | tf_op jit(solution)/shard_map/ppermute | solution.py:477
  41.3 15.7 %collective-permute-start.7 = (bf16[768,384]{1,0:T(8,128)(2,1)}, bf16[768,384]{1,0:T(8,128)(2,1)S(1)}, u32[]{:S(2)}, u32[]{:S(2)}) collective-permute-start(bf16[768,384]{1,0:T(8,128)(2,1)} %collective-permute-done.5.refs_11_.refs_5_.refs_1_.refs_8_), channel_id=1, source_target_pairs={{0,4},{4,0},{8,12},{12,8},{16,20},{20,16},{24,28},{28,24},{1,5},{5... | collective-permute-start | bytes 1769480 | tf_op jit(solution)/shard_map/ppermute | solution.py:477
  41.8 19.7 %collective-permute-start.9 = (bf16[768,384]{1,0:T(8,128)(2,1)}, bf16[768,384]{1,0:T(8,128)(2,1)}, u32[]{:S(2)}, u32[]{:S(2)}) collective-permute-start(bf16[768,384]{1,0:T(8,128)(2,1)} %collective-permute-done.5.refs_11_.refs_5_.refs_1_.refs_8_), channel_id=1, source_target_pairs={{0,1},{1,0},{2,3},{3,2},{4,5},{5,4},{6,7},{7,6},{8,9},{9,8},{10,11... | collective-permute-start | bytes 1769480 | tf_op jit(solution)/shard_map/ppermute | solution.py:477
  58.3 20.9 %collective-permute-start.11 = (bf16[768,768]{1,0:T(8,128)(2,1)}, bf16[768,768]{1,0:T(8,128)(2,1)}, u32[]{:S(2)}, u32[]{:S(2)}) collective-permute-start(bf16[768,768]{1,0:T(8,128)(2,1)} %refs_12_.1), channel_id=1, source_target_pairs={{0,1},{1,0},{2,3},{3,2},{4,5},{5,4},{6,7},{7,6},{8,9},{9,8},{10,11... | collective-permute-start | bytes 3538952 | tf_op jit(solution)/shard_map/ppermute | solution.py:477
  61.5 15.3 %collective-permute-start.12 = (bf16[384,768]{1,0:T(8,128)(2,1)}, bf16[384,768]{1,0:T(8,128)(2,1)S(1)}, u32[]{:S(2)}, u32[]{:S(2)}) collective-permute-start(bf16[384,768]{1,0:T(8,128)(2,1)} %get-tuple-element.77.refs_9_.refs_5_.refs_14_), channel_id=1, source_target_pairs={{0,4},{4,0},{8,12},{12,8},{16,20},{20,16},{24,28},{28,24},{1,5},{5... | collective-permute-start | bytes 1769480 | tf_op jit(solution)/shard_map/ppermute | solution.py:477
  62.1 17.1 %collective-permute-start.14 = (bf16[384,768]{1,0:T(8,128)(2,1)}, bf16[384,768]{1,0:T(8,128)(2,1)}, u32[]{:S(2)}, u32[]{:S(2)}) collective-permute-start(bf16[384,768]{1,0:T(8,128)(2,1)} %get-tuple-element.77.refs_9_.refs_5_.refs_14_), channel_id=1, source_target_pairs={{0,1},{1,0},{2,3},{3,2},{4,5},{5,4},{6,7},{7,6},{8,9},{9,8},{10,11... | collective-permute-start | bytes 1769480 | tf_op jit(solution)/shard_map/ppermute | solution.py:477
  77.6 15.8 %collective-permute-start.19 = (bf16[2,2,192,384]{3,2,1,0:T(8,128)(2,1)S(1)}, bf16[2,2,192,384]{3,2,1,0:T(8,128)(2,1)S(1)}, u32[]{:S(2)}, u32[]{:S(2)}) collective-permute-start(bf16[2,2,192,384]{3,2,1,0:T(8,128)(2,1)S(1)} %copy-done.15), channel_id=1, source_target_pairs={{0,2},{1,3},{2,0},{3,1},{4,6},{5,7},{6,4},{7,5},{8,10},{9,11},{10,... | collective-permute-start | bytes 1769480 | tf_op jit(solution)/shard_map/ppermute | solution.py:477
  128.7 28.8 %collective-permute-start.25 = (bf16[9216,128]{1,0:T(8,128)(2,1)}, bf16[9216,128]{1,0:T(8,128)(2,1)}, u32[]{:S(2)}, u32[]{:S(2)}) collective-permute-start(bf16[9216,128]{1,0:T(8,128)(2,1)} %get-tuple-element.87.refs_3_), channel_id=1, source_target_pairs={{0,1},{1,0},{2,3},{3,2},{4,5},{5,4},{6,7},{7,6},{8,9},{9,8},{10,11... | collective-permute-start | bytes 7077896 | tf_op jit(solution)/shard_map/ppermute | solution.py:477
  138.2 17.7 %collective-permute-start.22 = (bf16[2304,128]{1,0:T(8,128)(2,1)S(1)}, bf16[2304,128]{1,0:T(8,128)(2,1)}, u32[]{:S(2)}, u32[]{:S(2)}) collective-permute-start(bf16[2304,128]{1,0:T(8,128)(2,1)S(1)} %get-tuple-element.88.refs_1_.refs_18_), channel_id=1, source_target_pairs={{0,2},{1,3},{2,0},{3,1},{4,6},{5,7},{6,4},{7,5},{8,10},{9,11},{10,... | collective-permute-start | bytes 1769480 | tf_op jit(solution)/shard_map/ppermute | solution.py:477
  139.7 17.7 %collective-permute-start.26 = (bf16[1920,128]{1,0:T(8,128)(2,1)}, bf16[1920,128]{1,0:T(8,128)(2,1)}, u32[]{:S(2)}, u32[]{:S(2)}) collective-permute-start(bf16[1920,128]{1,0:T(8,128)(2,1)} %get-tuple-element.91.refs_19_), channel_id=1, source_target_pairs={{0,4},{4,0},{8,12},{12,8},{16,20},{20,16},{24,28},{28,24},{1,5},{5... | collective-permute-start | bytes 1474568 | tf_op jit(solution)/shard_map/ppermute | solution.py:477
  140.3 15.0 %collective-permute-start.24 = (f32[2,384]{1,0:T(2,128)}, f32[2,384]{1,0:T(2,128)S(1)}, u32[]{:S(2)}, u32[]{:S(2)}) collective-permute-start(f32[2,384]{1,0:T(2,128)} %shard_map.319), channel_id=1, source_target_pairs={{0,2},{1,3},{2,0},{3,1},{4,6},{5,7},{6,4},{7,5},{8,10},{9,11},{10,... | collective-permute-start | bytes 9224 | tf_op jit(solution)/shard_map/ppermute | solution.py:477
  162.6 21.3 %collective-permute-start.29 = (bf16[9216,128]{1,0:T(8,128)(2,1)}, bf16[9216,128]{1,0:T(8,128)(2,1)}, u32[]{:S(2)}, u32[]{:S(2)}) collective-permute-start(bf16[9216,128]{1,0:T(8,128)(2,1)} %get-tuple-element.93.refs_6_), channel_id=1, source_target_pairs={{0,1},{1,0},{2,3},{3,2},{4,5},{5,4},{6,7},{7,6},{8,9},{9,8},{10,11... | collective-permute-start | bytes 7077896 | tf_op jit(solution)/shard_map/ppermute | solution.py:477
  162.7 21.3 %collective-permute-start.31 = (bf16[3264,128]{1,0:T(8,128)(2,1)}, bf16[3264,128]{1,0:T(8,128)(2,1)S(1)}, u32[]{:S(2)}, u32[]{:S(2)}) collective-permute-start(bf16[3264,128]{1,0:T(8,128)(2,1)} %copy-done.10), channel_id=1, source_target_pairs={{0,2},{1,3},{2,0},{3,1},{4,6},{5,7},{6,4},{7,5},{8,10},{9,11},{10,... | collective-permute-start | bytes 2506760 | tf_op jit(solution)/shard_map/ppermute | solution.py:477
  164.3 19.6 %collective-permute-start.30 = (bf16[3072,128]{1,0:T(8,128)(2,1)S(1)}, bf16[3072,128]{1,0:T(8,128)(2,1)S(1)}, u32[]{:S(2)}, u32[]{:S(2)}) collective-permute-start(bf16[3072,128]{1,0:T(8,128)(2,1)S(1)} %get-tuple-element.98.refs_18_), channel_id=1, source_target_pairs={{0,4},{4,0},{8,12},{12,8},{16,20},{20,16},{24,28},{28,24},{1,5},{5... | collective-permute-start | bytes 2359304 | tf_op jit(solution)/shard_map/ppermute | solution.py:477
  164.8 18.7 %collective-permute-start.27 = (bf16[768,128]{1,0:T(8,128)(2,1)}, bf16[768,128]{1,0:T(8,128)(2,1)S(1)}, u32[]{:S(2)}, u32[]{:S(2)}) collective-permute-start(bf16[768,128]{1,0:T(8,128)(2,1)} %get-tuple-element.95.refs_1_), channel_id=1, source_target_pairs={{0,1},{1,0},{2,3},{3,2},{4,5},{5,4},{6,7},{7,6},{8,9},{9,8},{10,11... | collective-permute-start | bytes 589832 | tf_op jit(solution)/shard_map/ppermute | solution.py:477
  164.8 18.7 %collective-permute-start.28 = (bf16[768,128]{1,0:T(8,128)(2,1)}, bf16[768,128]{1,0:T(8,128)(2,1)S(1)}, u32[]{:S(2)}, u32[]{:S(2)}) collective-permute-start(bf16[768,128]{1,0:T(8,128)(2,1)} %get-tuple-element.96.refs_3_), channel_id=1, source_target_pairs={{0,1},{1,0},{2,3},{3,2},{4,5},{5,4},{6,7},{7,6},{8,9},{9,8},{10,11... | collective-permute-start | bytes 589832 | tf_op jit(solution)/shard_map/ppermute | solution.py:477
  183.5 28.3 %collective-permute-start.35 = (bf16[10752,128]{1,0:T(8,128)(2,1)}, bf16[10752,128]{1,0:T(8,128)(2,1)}, u32[]{:S(2)}, u32[]{:S(2)}) collective-permute-start(bf16[10752,128]{1,0:T(8,128)(2,1)} %get-tuple-element.107.refs_11_), channel_id=1, source_target_pairs={{0,1},{1,0},{2,3},{3,2},{4,5},{5,4},{6,7},{7,6},{8,9},{9,8},{10,11... | collective-permute-start | bytes 8257544 | tf_op jit(solution)/shard_map/ppermute | solution.py:477
  188.3 30.5 %collective-permute-start.34 = (bf16[4992,128]{1,0:T(8,128)(2,1)}, bf16[4992,128]{1,0:T(8,128)(2,1)}, u32[]{:S(2)}, u32[]{:S(2)}) collective-permute-start(bf16[4992,128]{1,0:T(8,128)(2,1)} %get-tuple-element.108.refs_5_.refs_2_), channel_id=1, source_target_pairs={{0,2},{1,3},{2,0},{3,1},{4,6},{5,7},{6,4},{7,5},{8,10},{9,11},{10,... | collective-permute-start | bytes 3833864 | tf_op jit(solution)/shard_map/ppermute | solution.py:477
  189.7 22.1 %collective-permute-start.36 = (bf16[3456,128]{1,0:T(8,128)(2,1)S(1)}, bf16[3456,128]{1,0:T(8,128)(2,1)S(1)}, u32[]{:S(2)}, u32[]{:S(2)}) collective-permute-start(bf16[3456,128]{1,0:T(8,128)(2,1)S(1)} %get-tuple-element.109.refs_6_), channel_id=1, source_target_pairs={{0,4},{4,0},{8,12},{12,8},{16,20},{20,16},{24,28},{28,24},{1,5},{5... | collective-permute-start | bytes 2654216 | tf_op jit(solution)/shard_map/ppermute | solution.py:477
  191.6 18.0 %all-to-all-start = ((bf16[4,9,48,128]{3,2,1,0:T(8,128)(2,1)}), bf16[4,9,48,128]{3,2,1,0:T(8,128)(2,1)S(1)}, u32[]{:S(2)}, u32[]{:S(2)}) async-start(bf16[4,9,48,128]{3,2,1,0:T(8,128)(2,1)} %bitcast.83), calls=%async_computation | async-start | bytes 884736 | tf_op jit(solution)/shard_map/all_to_all | solution.py:488
  226.3 27.7 %collective-permute-start.38 = (bf16[4224,128]{1,0:T(8,128)(2,1)}, bf16[4224,128]{1,0:T(8,128)(2,1)S(1)}, u32[]{:S(2)}, u32[]{:S(2)}) collective-permute-start(bf16[4224,128]{1,0:T(8,128)(2,1)} %get-tuple-element.116), channel_id=1, source_target_pairs={{0,4},{4,0},{8,12},{12,8},{16,20},{20,16},{24,28},{28,24},{1,5},{5... | collective-permute-start | bytes 3244040 | tf_op jit(solution)/shard_map/ppermute | solution.py:477
  227.8 21.0 %collective-permute-start.39 = (bf16[3456,128]{1,0:T(8,128)(2,1)S(1)}, bf16[3456,128]{1,0:T(8,128)(2,1)}, u32[]{:S(2)}, u32[]{:S(2)}) collective-permute-start(bf16[3456,128]{1,0:T(8,128)(2,1)S(1)} %get-tuple-element.114.refs_2_), channel_id=1, source_target_pairs={{0,2},{1,3},{2,0},{3,1},{4,6},{5,7},{6,4},{7,5},{8,10},{9,11},{10,... | collective-permute-start | bytes 2654216 | tf_op jit(solution)/shard_map/ppermute | solution.py:477
  232.5 21.4 %all-to-all-start.1 = ((bf16[4,6,96,128]{3,2,1,0:T(8,128)(2,1)}), bf16[4,6,96,128]{3,2,1,0:T(8,128)(2,1)S(1)}, u32[]{:S(2)}, u32[]{:S(2)}) async-start(bf16[4,6,96,128]{3,2,1,0:T(8,128)(2,1)} %bitcast.82), calls=%async_computation.1 | async-start | bytes 1179648 | tf_op jit(solution)/shard_map/all_to_all | solution.py:488
  262.1 23.9 %collective-permute-start.40 = (f32[2,384]{1,0:T(2,128)}, f32[2,384]{1,0:T(2,128)S(1)}, u32[]{:S(2)}, u32[]{:S(2)}) collective-permute-start(f32[2,384]{1,0:T(2,128)} %shard_map.331), channel_id=1, source_target_pairs={{0,8},{4,12},{8,0},{12,4},{16,24},{20,28},{24,16},{28,20},{1,9},{5... | collective-permute-start | bytes 9224 | tf_op jit(solution)/shard_map/ppermute | solution.py:477
  263.0 19.4 %all-to-all-start.3 = ((bf16[4,6,96,128]{3,2,1,0:T(8,128)(2,1)}), bf16[4,6,96,128]{3,2,1,0:T(8,128)(2,1)}, u32[]{:S(2)}, u32[]{:S(2)}) async-start(bf16[4,6,96,128]{3,2,1,0:T(8,128)(2,1)} %bitcast.81), calls=%async_computation.3 | async-start | bytes 1179648 | tf_op jit(solution)/shard_map/all_to_all | solution.py:488
  282.4 23.6 %all-to-all-start.2 = ((bf16[4,7,96,128]{3,2,1,0:T(8,128)(2,1)}), bf16[4,7,96,128]{3,2,1,0:T(8,128)(2,1)S(1)}, u32[]{:S(2)}, u32[]{:S(2)}) async-start(bf16[4,7,96,128]{3,2,1,0:T(8,128)(2,1)} %bitcast.73), calls=%async_computation.2 | async-start | bytes 1376256 | tf_op jit(solution)/shard_map/all_to_all | solution.py:488
  286.1 17.5 %collective-permute-start.41 = (f32[2,384]{1,0:T(2,128)S(1)}, f32[2,384]{1,0:T(2,128)S(1)}, u32[]{:S(2)}, u32[]{:S(2)}) collective-permute-start(f32[2,384]{1,0:T(2,128)S(1)} %add.43), channel_id=1, source_target_pairs={{0,16},{4,20},{8,24},{12,28},{16,0},{20,4},{24,8},{28,12},{1,17},{... | collective-permute-start | bytes 9224 | tf_op jit(solution)/shard_map/ppermute | solution.py:477
  (118 other events, 815.2 us)
where the time goes:
time: 312 us; the launch traced here: 310 us
  Pallas kernels  99.2 us (32%)
  waiting for transfers between devices  98.8 us (32%)
  local copies, waits for them, and re-layouts  56.3 us (18%)
  starting transfers between devices  47.4 us (15%)
  other arithmetic  6.48 us (2%)
    pallas_call x12, Pallas kernels, call(): pl.pallas_call(lambda *refs: kernel(*refs[:n_args], *refs[n_all:]), out_s...  80.7 us
    ppermute x44, waiting for transfers between devices, swap(): return lax.ppermute(value, axis, [(i, i ^ bit) for i in range(size)])  75.7 us
    unnamed x208, local copies, waits for them, and re-layouts  39.7 us
    ppermute x44, starting transfers between devices, swap(): return lax.ppermute(value, axis, [(i, i ^ bit) for i in range(size)])  29.9 us
    all_to_all x4, waiting for transfers between devices, send_last(): lax.all_to_all(jnp.swapaxes(kept, 0, 1), 'dp', 0, 0, axis_index_groups=gr...  23.1 us
    pallas_call x6, Pallas kernels, combine(): pl.pallas_call(kernel, out_shape=[jax.ShapeDtypeStruct((size, 128), BF) f...  18.4 us
    all_to_all x4, starting transfers between devices, send_last(): lax.all_to_all(jnp.swapaxes(kept, 0, 1), 'dp', 0, 0, axis_index_groups=gr...  17.4 us
  transfers between devices with their start and end apart: 48, of which 23 were waited for; matrix products, arithmetic and copies ran while one was open for 7% of the time, Pallas kernels for 22%

commit v1 on v0

--- a/solution.py
+++ b/solution.py
@@ -13,6 +13,7 @@
 EPS = 1e-06
 BF = jnp.bfloat16
 F32 = jnp.float32
+COST = 1.15e9
 VMEM_BYTES = 48 * 1024 * 1024
 
 
@@ -119,7 +120,7 @@
         out_specs=[pl.BlockSpec(memory_space=pltpu.VMEM)] * len(shapes),
         scratch_shapes=[pltpu.VMEM(shape, kind) for shape, kind in scratch],
         compiler_params=pltpu.CompilerParams(vmem_limit_bytes=VMEM_BYTES),
-        cost_estimate=pl.CostEstimate(flops=int(micros * 1e10), bytes_accessed=moved, transcendentals=0),
+        cost_estimate=pl.CostEstimate(flops=int(micros * COST), bytes_accessed=moved if micros else 0, transcendentals=0),
     )(*args, *tokens)
 
 
@@ -165,7 +166,7 @@
             ref[pl.ds(at, half), :] = value[side * half : (side + 1) * half].astype(BF)
 
 
-def combine(outs, tokens):
+def combine(outs, tokens, micros, sums=()):
     arrays, terms = [], []
     for segments in outs:
         for parts in segments:
@@ -173,17 +174,20 @@
                 if not any(array is known for known in arrays):
                     arrays.append(array)
                 terms.append((next(i for i, known in enumerate(arrays) if known is array), first, size))
-    n_in, n_out, n_terms = len(arrays) + len(tokens), len(outs), len(terms)
+    n_sums, n_arrays, n_out, n_terms = len(sums), len(arrays), len(outs), len(terms)
+    n_in = n_sums + n_arrays + len(tokens)
     sizes = [sum(parts[0][2] for parts in segments) for segments in outs]
 
     def kernel(*refs):
-        held, sem = refs[n_in + n_out : -1], refs[-1]
+        held, sem = refs[-1 - n_terms : -1], refs[-1]
         copies = [
-            pltpu.make_async_copy(refs[which].at[pl.ds(first, size), :], held[at], sem.at[at])
+            pltpu.make_async_copy(refs[n_sums + which].at[pl.ds(first, size), :], held[at], sem.at[at])
             for at, (which, first, size) in enumerate(terms)
         ]
         for copy in copies:
             copy.start()
+        if sums:
+            refs[n_in + n_out][...] = refs[0][...] + refs[1][...]
         at = 0
         for out, segments in zip(refs[n_in:], outs):
             row = 0
@@ -206,46 +210,38 @@
                 row += size
 
     moved = 256 * (sum(t[2] for t in terms) + sum(sizes))
+    in_vmem = pl.BlockSpec(memory_space=pltpu.VMEM)
     return pl.pallas_call(
         kernel,
-        out_shape=[jax.ShapeDtypeStruct((size, 128), BF) for size in sizes],
-        in_specs=[ANYWHERE] * n_in,
-        out_specs=[pl.BlockSpec(memory_space=pltpu.VMEM)] * n_out,
+        out_shape=[jax.ShapeDtypeStruct((size, 128), BF) for size in sizes]
+        + ([jax.ShapeDtypeStruct(sums[0].shape, F32)] if sums else []),
+        in_specs=[in_vmem] * n_sums + [ANYWHERE] * (n_in - n_sums),
+        out_specs=[in_vmem] * (n_out + (1 if sums else 0)),
         scratch_shapes=[pltpu.VMEM((size, 128), BF) for _, _, size in terms] + [pltpu.SemaphoreType.DMA((n_terms,))],
         compiler_params=pltpu.CompilerParams(vmem_limit_bytes=VMEM_BYTES),
-        cost_estimate=pl.CostEstimate(flops=int(3e10), bytes_accessed=moved, transcendentals=0),
-    )(*arrays, *tokens)
+        cost_estimate=pl.CostEstimate(flops=int(micros * COST), bytes_accessed=moved if micros else 0, transcendentals=0),
+    )(*sums, *arrays, *tokens)
 
 
 def pack_attn_kernel(pos, qkv, out, own, direct):
-    cols = qkv.shape[2]
+    cols = qkv.shape[1]
     for part in range(3):
-        own[part * cols : (part + 1) * cols, :] = qkv[part].T
+        own[part * cols : (part + 1) * cols, :] = qkv[part]
     own[3 * cols :, :] = out[...]
     half = direct.shape[0]
     direct[...] = own[pl.ds(pl.multiple_of(pos[1] * half, half), half), :]
 
 
-def pack_mlp_kernel(pos, up, down, up_direct, down_direct):
+def pack_rest_kernel(pos, up, down, qkv, out, embed, p_up, p_down, up_direct, down_direct, pred):
     half = up_direct.shape[1]
     at = pl.ds(pl.multiple_of(pos[1] * half, half), half)
     up_direct[...] = up[:, at]
     down_direct[...] = down[at, :]
-
-
-def pack_pred_kernel(pos, qkv, out, embed, up, down, attn, mlp):
-    cols, half_width = qkv.shape[2], attn.shape[2]
-    attn[0, :cols, :] = qkv[0].T
-    attn[0, cols : 2 * cols, :] = qkv[1].T
-    attn[0, 2 * cols :, :] = embed[:half_width, :].T
-    attn[1, :cols, :] = qkv[2].T
-    attn[1, cols : 2 * cols, :] = out[...]
-    attn[1, 2 * cols :, :] = embed[half_width:, :].T
-    half = mlp.shape[2]
-    turned_up = up[...].T
-    for side in range(2):
-        mlp[side, 0] = turned_up[side * half : (side + 1) * half, :]
-        mlp[side, 1] = down[side * half : (side + 1) * half, :]
+    width = pred.shape[1]
+    row = 0
+    for part in (qkv[0], qkv[1], qkv[2], out[...], embed[:, :width], embed[:, width:], p_up[...], p_down[...]):
+        pred[row : row + part.shape[0], :] = part
+        row += part.shape[0]
 
 
 def enc_attn_kernel(pos, x, seg_row, seg_col, gain, own, core, d_x, e_x, d_c, e_c, middle, qkv, probs, mixed, far):
@@ -305,30 +301,25 @@
 
 def pred_kernel(
     pos, enc, seg_row, seg_col, masked, token, gain_one, gain_two, cot, rows_at,
-    a_own, a_core, a_x, a_xc, m_own, m_core, m_x, m_xc,
+    p_own, p_core, p_x, p_xc,
     pred_out, stats, g_mine, g_theirs, d_embedded, d_enc, d_gains,
     w_qkv, w_out, w_embed, w_up, w_down, qkv, probs, mixed, d_mixed, d_qkv,
 ):
     me = pos[0]
     length = cot.shape[0]
     cols = w_out.shape[0] // SHARDS
-    segments = Segments(w_out.shape[0], 4 * cols + 4 * m_x.shape[2])
+    hid = w_down.shape[0] // SHARDS
+    segments = Segments(w_out.shape[0], 4 * cols + 2 * hid)
     per = cols // P_HEAD_DIM
-    half = m_x.shape[2]
-    hid = 2 * half
     width = w_out.shape[1]
-    for shard, pack in enumerate((a_own, a_core, a_x, a_xc)):
-        w_qkv[shard * 3 * cols : shard * 3 * cols + 2 * cols, :] = pack[0, : 2 * cols]
-        w_qkv[shard * 3 * cols + 2 * cols : (shard + 1) * 3 * cols, :] = pack[1, :cols]
-        w_out[shard * cols : (shard + 1) * cols, :] = pack[1, cols : 2 * cols]
+    for shard, pack in enumerate((p_own, p_core, p_x, p_xc)):
+        w_qkv[shard * 3 * cols : (shard + 1) * 3 * cols, :] = pack[: 3 * cols, :]
+        w_out[shard * cols : (shard + 1) * cols, :] = pack[3 * cols : 4 * cols, :]
         at = pl.ds(pl.multiple_of((me ^ shard) * cols, 16), cols)
-        w_embed[at, :width] = pack[0, 2 * cols :]
-        w_embed[at, width:] = pack[1, 2 * cols :]
-    for shard, pack in enumerate((m_own, m_core, m_x, m_xc)):
-        for which in range(2):
-            at = slice(shard * hid + which * half, shard * hid + (which + 1) * half)
-            w_up[at, :] = pack[which, 0]
-            w_down[at, :] = pack[which, 1]
+        w_embed[at, :width] = pack[4 * cols : 5 * cols, :]
+        w_embed[at, width:] = pack[5 * cols : 6 * cols, :]
+        w_up[:, shard * hid : (shard + 1) * hid] = pack[6 * cols : 6 * cols + width, :]
+        w_down[shard * hid : (shard + 1) * hid, :] = pack[6 * cols + width :, :]
 
     hidden_mask = masked[...] > 0.0
     start = jnp.where(hidden_mask, token[...], nt(enc[...], w_embed[...]))
@@ -339,11 +330,12 @@
     middle = start + tn(mixed[...], w_out[...])
     n_two, r_two = norm(middle)
     b = (n_two * gain_two[...]).astype(BF)
-    act, slope = gelu_parts(nt(b, w_up[...]))
+    act, slope = gelu_parts(nn(b, w_up[...]))
     act = act.astype(BF)
     predicted = middle + nn(act, w_down[...])
     for at, block in enumerate(units(predicted)):
         pred_out[at * length : (at + 1) * length, :] = block.astype(BF)
+    stats[...] = jnp.zeros_like(stats)
     stats[0:1, :] = jnp.sum(predicted, 0, keepdims=True)
     stats[1:2, :] = jnp.sum(predicted * predicted, 0, keepdims=True)
 
@@ -357,7 +349,7 @@
         blocks = units(nn(b_turned, d_pre[:, cut])) + units(nn(grad_turned, act[:, cut]))
         for block, value in enumerate(blocks):
             segments.put(home, at, 4 * cols // 128 + block, value)
-    d_middle, d_gain_two = norm_back(n_two, r_two, gain_two[...], nn(d_pre, w_up[...]))
+    d_middle, d_gain_two = norm_back(n_two, r_two, gain_two[...], nt(d_pre, w_up[...]))
     grad_mid = grad_low.astype(F32) + d_middle
     mid_low = grad_mid.astype(BF)
     d_mixed[...] = nt(w_out[...], mid_low).astype(BF)
@@ -370,6 +362,7 @@
             segments.put(home, at, block, value)
     d_value, d_gain_one = norm_back(n_one, r_one, gain_one[...], tn(d_qkv[...], w_qkv[...]))
     d_start = grad_mid + d_value
+    d_gains[...] = jnp.zeros_like(d_gains)
     d_gains[0:1, :] = d_gain_one
     d_gains[1:2, :] = d_gain_two
     d_gains[2:3, :] = jnp.sum(jnp.where(hidden_mask, d_start, 0.0), 0, keepdims=True)
@@ -413,7 +406,7 @@
 
 
 def enc_attn_back_kernel(
-    pos, rows_at, x, gain, grad, qkv, probs, mixed, d_embedded, enc, smalls, own, core, d_x, e_x, d_c, e_c,
+    pos, rows_at, x, gain, grad, qkv, probs, mixed, d_embedded, enc, d_gain_two, p_rows_at, p_d_gains, own, core, d_x, e_x, d_c, e_c,
     mine, theirs, d_input, far, d_mixed, d_qkv,
 ):
     me, side = pos[0], pos[1]
@@ -448,11 +441,13 @@
     within = column & 127
     one_hot = ((((column >> 7) ^ me) * e_cols + within == row) & (within < e_cols)).astype(BF)
     g_embed = nn(turned(source, enc[...]), nn(d_embedded[...], one_hot).astype(BF))
-    which = lax.broadcasted_iota(jnp.int32, smalls.shape, 0)
-    lines = jnp.where(which == 0, d_gain_one, smalls[...]).astype(BF)
-    lane = lax.broadcasted_iota(jnp.int32, (smalls.shape[0], 128), 1)
-    line = lax.broadcasted_iota(jnp.int32, (smalls.shape[0], 128), 0)
-    g_small = nn(turned(source, lines), (lane == line + e_cols).astype(BF))
+    line = lax.broadcasted_iota(jnp.int32, (8, width), 0)
+    lines = jnp.where(line == 0, d_gain_one, jnp.where(line == 1, d_gain_two[...], 0.0)).astype(BF)
+    lane = lax.broadcasted_iota(jnp.int32, (8, 128), 1) - lax.broadcasted_iota(jnp.int32, (8, 128), 0)
+    p_one_hot = (lax.broadcasted_iota(jnp.int32, (width, channels), 1) == p_rows_at[...]).astype(BF)
+    g_small = nn(turned(source, lines), (lane == e_cols).astype(BF)) + nn(
+        nt(p_one_hot, p_d_gains[...].astype(BF)).astype(BF), (lane == e_cols + 2).astype(BF)
+    )
 
     segments = Segments(width, 4 * cols + 128)
     homes = ((mine, 0), (theirs, 0), (mine, 1), (theirs, 1))
@@ -516,28 +511,27 @@
     pos = jnp.stack([me, side]).astype(jnp.int32)
 
     attn_own, attn_direct = call(
-        pack_attn_kernel, [((4 * cols, width), BF), ((2 * cols, width), BF)], (pos, qkv_weight, out_weight), 1
-    )
-    up_direct, down_direct = call(
-        pack_mlp_kernel, [((width, hid // 2), BF), ((hid // 2, width), BF)],
-        (pos, up_weight, down_weight), 1, tokens=(attn_direct,),
-    )
-    p_attn_own, p_mlp_own = call(
-        pack_pred_kernel,
-        [((2, 3 * p_cols, channels), BF), ((2, 2, p_hid // 2, channels), BF)],
-        (pos, pred_qkv, pred_out, embed_weight, pred_up, pred_down), 2, tokens=(up_direct,),
+        pack_attn_kernel, [((4 * cols, width), BF), ((2 * cols, width), BF)],
+        (pos, jnp.swapaxes(qkv_weight, 1, 2), out_weight), 1,
+    )
+    up_direct, down_direct, p_own = call(
+        pack_rest_kernel,
+        [((width, hid // 2), BF), ((hid // 2, width), BF), ((6 * p_cols + channels + p_hid, channels), BF)],
+        (pos, up_weight, down_weight, jnp.swapaxes(pred_qkv, 1, 2), pred_out, embed_weight.T, pred_up, pred_down), 3,
+        tokens=(attn_direct,),
     )
 
     attn_core, up_core, down_core = swap(attn_own, "mp", 1), swap(up_weight, "mp", 1), swap(down_weight, "mp", 1)
-    p_attn_core, p_mlp_core = swap(p_attn_own, "mp", 1), swap(p_mlp_own, "mp", 1)
+    p_core = swap(p_own, "mp", 1)
     attn_x = swap(attn_direct, "mp", 2)
+    attn_x, up_direct = gate([attn_x, up_direct], [p_own])
     up_x = swap(up_direct, "mp", 2)
     attn_y = swap(attn_x, "dp", 1)
-    (down_direct,) = gate([down_direct], [attn_x])
+    (down_direct,) = gate([down_direct], [up_x])
     down_x = swap(down_direct, "mp", 2)
     up_y = swap(up_x, "dp", 1)
-    (p_attn_own,) = gate([p_attn_own], [up_x])
-    p_attn_x = swap(p_attn_own, "mp", 2)
+    (p_send,) = gate([p_own], [down_x])
+    p_x = swap(p_send, "mp", 2)
     attn = (attn_own, attn_core, attn_x, attn_y, swap(attn_x, "mp", 1), swap(attn_y, "mp", 1))
 
     x = pick(patches, me)
@@ -548,148 +542,123 @@
     cot = pick(cotangent, me)
     row = lambda gain: gain.astype(F32)[None, :]
     rows_at, p_rows_at = source_rows(width, side), source_rows(channels, side)
+    n_rows, n_small = width // dp_size, channels // dp_size
+    small_rows_at = rows_at // n_rows * n_small + rows_at % n_small
 
     middle, qkv, probs, mixed = call(
         enc_attn_kernel,
         [((length, width), F32), ((3 * width, length), BF), ((heads, length, length), BF), ((width, length), BF)],
         (pos, x, seg_row, seg_col, row(gain_attn)) + attn, 9,
-        [((2, 4 * cols, width), BF)], tokens=(up_x,),
-    )
-    up_y, down_x, p_mlp_own = gate([up_y, down_x, p_mlp_own], [middle])
+        [((2, 4 * cols, width), BF)],
+    )
+    (up_y,) = gate([up_y], [middle])
     up = (up_weight, up_core, up_x, up_y, swap(up_x, "mp", 1), swap(up_y, "mp", 1))
     down_y = swap(down_x, "dp", 1)
-    p_mlp_x = swap(p_mlp_own, "mp", 2)
     hidden, slope = call(
         enc_up_forward_kernel, [((length, SHARDS * hid), BF), ((length, SHARDS * hid), BF)],
-        (pos, middle, row(gain_mlp)) + up, 6, tokens=(down_x,),
-    )
-    down_y, p_attn_x = gate([down_y, p_attn_x], [hidden])
+        (pos, middle, row(gain_mlp)) + up, 6,
+    )
+    (down_y,) = gate([down_y], [hidden])
     down = (down_weight, down_core, down_x, down_y, swap(down_x, "mp", 1), swap(down_y, "mp", 1))
-    p_attn = (p_attn_own, p_attn_core, p_attn_x, swap(p_attn_x, "mp", 1))
     (enc,) = call(enc_down_forward_kernel, [((length, width), BF)], (pos, middle, hidden) + down, 4)
-    (p_mlp_x,) = gate([p_mlp_x], [enc])
-    p_mlp = (p_mlp_own, p_mlp_core, p_mlp_x, swap(p_mlp_x, "mp", 1))
+    p_packs = (p_send, p_core, p_x, swap(p_x, "mp", 1))
     p_seg, d_seg = Segments(channels, 4 * p_cols + 2 * p_hid), Segments(width, hid)
     u_seg, a_seg = Segments(width, hid), Segments(width, 4 * cols + 128)
     p_blocks, x_blocks = channels // 128, width // 128
     predicted, stats, p_mine, p_theirs, d_embedded, d_enc, p_d_gains = call(
         pred_kernel,
-        [((p_blocks * length, 128), BF), ((2, channels), F32), (p_seg.shape, BF), (p_seg.shape, BF), ((length, channels), BF),
-         ((length, width), F32), ((3, channels), F32)],
+        [((p_blocks * length, 128), BF), ((8, channels), F32), (p_seg.shape, BF), (p_seg.shape, BF), ((length, channels), BF),
+         ((length, width), F32), ((8, channels), F32)],
         (pos, enc, seg_row, seg_col, masked, row(mask_token), row(pred_gain_attn), row(pred_gain_mlp), cot, p_rows_at)
-        + p_attn + p_mlp, 30,
+        + p_packs, 30,
         [((3 * channels, channels), BF), ((channels, channels), BF), ((channels, width), BF),
-         ((SHARDS * p_hid, channels), BF), ((SHARDS * p_hid, channels), BF), ((3 * channels, length), BF),
+         ((channels, SHARDS * p_hid), BF), ((SHARDS * p_hid, channels), BF), ((3 * channels, length), BF),
          ((p_heads, length, length), BF), ((channels, length), BF), ((channels, length), BF),
          ((3 * channels, length), BF)],
     )
 
-    def hop(value, axis, bit):
-        return value + swap(value, axis, bit)
-
-    p_away, stats = swap(p_theirs, "mp", 1), hop(stats, "mp", 1)
-    d_mine, d_theirs = call(enc_down_kernel, [(d_seg.shape, BF)] * 2, (pos, rows_at, d_enc, hidden), 4)
-
-    p_own = (p_mine, p_away)
-    send_x, send_y = combine(
-        [[[(g, *p_seg.over_x) for g in p_own], [(predicted, 0, predicted.shape[0])]], [[(g, *p_seg.over_y) for g in p_own]]],
-        [d_theirs],
-    )
-    (stats,) = gate([stats], [send_x])
-    d_away, got_x, got_y, stats = swap(d_theirs, "mp", 1), swap(send_x, "mp", 2), swap(send_y, "dp", 1), hop(stats, "mp", 2)
-    p_x, p_y = (got_x, 0, 2 * p_seg.a), (got_y, 0, 2 * p_seg.b)
+    def first(own, seg):
+        return [(g, *seg.over_x) for g in own], [(g, *seg.over_y) for g in own]
+
+    def second(own, seg, got):
+        return [(g, *seg.then_x) for g in own] + [(got[1][0], got[1][1] + seg.b, seg.b)], [
+            (g, *seg.then_y) for g in own
+        ] + [(got[0][0], got[0][1] + seg.a, seg.a)]
+
+    def kept(own, seg, got, then):
+        return [[(g, *seg.keep_left) for g in own] + [(*got[0], seg.a), (*then[1], seg.a)],
+                [(g, *seg.keep_right) for g in own] + [(*got[1], seg.b), (*then[0], seg.b)]]
+
+    def stage(parts, tokens, micros, sums=()):
+        send = combine([[x for x, _ in parts], [y for _, y in parts]], tokens, micros, sums)
+        got, at = (swap(send[0], "mp", 2), swap(send[1], "dp", 1)), [0, 0]
+        places = []
+        for x, y in parts:
+            places.append(((got[0], at[0]), (got[1], at[1])))
+            at = [at[0] + x[0][2], at[1] + y[0][2]]
+        return send[:2], got, places, send[2] if sums else None
+
+    p_away, stats_got = swap(p_theirs, "mp", 1), swap(stats, "mp", 1)
+    d_mine, d_theirs = call(enc_down_kernel, [(d_seg.shape, BF)] * 2, (pos, rows_at, d_enc, hidden), 30)
+    d_away, p_own = swap(d_theirs, "mp", 1), (p_mine, p_away)
+    send, p_arrived, p_got, stats = stage([first(p_own, p_seg)], [d_theirs], 30, (stats, stats_got))
+    (predicted,) = gate([predicted], send)
+    d_own, p_got = (d_mine, d_away), p_got[0]
+    stats_got, predicted_x = swap(stats, "dp", 2), swap(predicted, "mp", 2)
     u_mine, u_theirs, grad_mid, d_gain_two = call(
         enc_up_kernel,
         [(u_seg.shape, BF), (u_seg.shape, BF), ((length, width), F32), ((1, width), F32)],
-        (pos, rows_at, d_enc, middle, row(gain_mlp), slope) + up + down, 14, tokens=(send_x, send_y),
-    )
-
-    def first(terms, part):
-        return (terms[0], terms[1], part)
-
-    def second(terms, part):
-        return (terms[0], terms[1] + part, part)
-
+        (pos, rows_at, d_enc, middle, row(gain_mlp), slope) + up + down, 100, tokens=send,
+    )
+    u_away = swap(u_theirs, "mp", 1)
+    predicted_x, d_away = gate([predicted_x, d_away], [u_theirs])
     d_own = (d_mine, d_away)
-    predicted_x = lax.slice_in_dim(got_x, 2 * p_seg.a, got_x.shape[0])
-    send_x, send_y = combine(
-        [[[(g, *d_seg.over_x) for g in d_own], [(g, *p_seg.then_x) for g in p_own] + [second(p_y, p_seg.b)]],
-         [[(g, *d_seg.over_y) for g in d_own], [(g, *p_seg.then_y) for g in p_own] + [second(p_x, p_seg.a)]]],
-        [u_theirs],
-    )
-    predicted, predicted_x, stats = gate([predicted, predicted_x, stats], [send_x])
-    u_away, got_x, got_y, stats = swap(u_theirs, "mp", 1), swap(send_x, "mp", 2), swap(send_y, "dp", 1), hop(stats, "dp", 1)
-    predicted_c, predicted_xc = swap(predicted, "mp", 1), swap(predicted_x, "mp", 1)
-    d_x, p_then_x = (got_x, 0, 2 * d_seg.a), (got_x, 2 * d_seg.a, p_seg.b)
-    d_y, p_then_y = (got_y, 0, 2 * d_seg.b), (got_y, 2 * d_seg.b, p_seg.a)
-    by_block = lambda left, right: jnp.concatenate([left.reshape(dp_size, -1), right.reshape(dp_size, -1)], 1).reshape(1, width)
-    zeros = jnp.zeros((channels,), F32)
-    smalls = jnp.concatenate(
-        [jnp.zeros((1, width), F32), d_gain_two, by_block(p_d_gains[0], p_d_gains[1]), by_block(p_d_gains[2], zeros),
-         jnp.zeros((4, width), F32)]
-    )
+    send, d_arrived, (d_got, p_then), stats = stage(
+        [first(d_own, d_seg), second(p_own, p_seg, p_got)], [u_theirs], 30, (stats, stats_got)
+    )
+    predicted, predicted_x = gate([predicted, predicted_x], send)
+    stats_got, predicted_c, predicted_xc = swap(stats, "dp", dp_size // 2), swap(predicted, "mp", 1), swap(predicted_x, "mp", 1)
     a_mine, a_theirs, d_input = call(
         enc_attn_back_kernel,
         [(a_seg.shape, BF), (a_seg.shape, BF), ((x_blocks * length, 128), BF)],
-        (pos, rows_at, x, row(gain_attn), grad_mid, qkv, probs, mixed, d_embedded, enc, smalls) + attn, 14,
-        [((2, 4 * cols, width), BF), ((width, length), BF), ((3 * width, length), BF)], tokens=(send_x, send_y),
-    )
-
-    def kept(own, seg, over_x, over_y, then_x, then_y):
-        return [[(g, *seg.keep_left) for g in own] + [first(over_x, seg.a), then_y],
-                [(g, *seg.keep_right) for g in own] + [first(over_y, seg.b), then_x]]
-
-    u_own = (u_mine, u_away)
-    send_x, send_y, p_kept = combine(
-        [[[(g, *u_seg.over_x) for g in u_own], [(g, *d_seg.then_x) for g in d_own] + [second(d_y, d_seg.b)],
-          [(d_input, 0, d_input.shape[0])]],
-         [[(g, *u_seg.over_y) for g in u_own], [(g, *d_seg.then_y) for g in d_own] + [second(d_x, d_seg.a)]],
-         kept(p_own, p_seg, p_x, p_y, p_then_x, p_then_y)],
-        [a_theirs, predicted_c, predicted_xc],
-    )
-    stats, d_input = gate([stats, d_input], [send_x])
-    a_away, got_x, got_y = swap(a_theirs, "mp", 1), swap(send_x, "mp", 2), swap(send_y, "dp", 1)
-    p_parts, input_c = send_last(p_kept, p_seg), swap(d_input, "mp", 1)
-    u_x, d_then_x = (got_x, 0, 2 * u_seg.a), (got_x, 2 * u_seg.a, d_seg.b)
-    u_y, d_then_y = (got_y, 0, 2 * u_seg.b), (got_y, 2 * u_seg.b, d_seg.a)
+        (pos, rows_at, x, row(gain_attn), grad_mid, qkv, probs, mixed, d_embedded, enc, d_gain_two, small_rows_at, p_d_gains)
+        + attn, 100,
+        [((2, 4 * cols, width), BF), ((width, length), BF), ((3 * width, length), BF)], tokens=send,
+    )
+
+    a_away = swap(a_theirs, "mp", 1)
+    u_away, predicted_c, predicted_xc = gate([u_away, predicted_c, predicted_xc], [a_theirs])
+    u_own, a_own = (u_mine, u_away), (a_mine, a_away)
+    ud_send, _, (u_got, d_then), stats = stage(
+        [first(u_own, u_seg), second(d_own, d_seg, d_got)], [a_theirs, predicted_c, predicted_xc], 60, (stats, stats_got)
+    )
+    (p_kept,) = combine([kept(p_own, p_seg, p_got, p_then)], ud_send, 30)
     (predictions,) = call(
-        in_order_kernel, [((SHARDS, length, channels), BF)], (pos, predicted, predicted_c, predicted_x, predicted_xc), 2,
-        tokens=(send_x, send_y),
-    )
-
-    a_own = (a_mine, a_away)
-    input_x = lax.slice_in_dim(got_x, 2 * u_seg.a + d_seg.b, got_x.shape[0])
-    send_x, send_y, d_kept = combine(
-        [[[(g, *a_seg.over_x) for g in a_own], [(g, *u_seg.then_x) for g in u_own] + [second(u_y, u_seg.b)]],
-         [[(g, *a_seg.over_y) for g in a_own], [(g, *u_seg.then_y) for g in u_own] + [second(u_x, u_seg.a)]],
-         kept(d_own, d_seg, d_x, d_y, d_then_x, d_then_y)],
-        [predictions, p_parts, input_c],
-    )
-    input_x, p_parts = gate([input_x, p_parts], [send_x])
-    got_x, got_y, d_parts, input_xc = swap(send_x, "mp", 2), swap(send_y, "dp", 1), send_last(d_kept, d_seg), swap(input_x, "mp", 1)
-    a_x, u_then_x = (got_x, 0, 2 * a_seg.a), (got_x, 2 * a_seg.a, u_seg.b)
-    a_y, u_then_y = (got_y, 0, 2 * a_seg.b), (got_y, 2 * a_seg.b, u_seg.a)
+        in_order_kernel, [((SHARDS, length, channels), BF)], (pos, predicted, predicted_c, predicted_x, predicted_xc), 30,
+        tokens=[p_kept],
+    )
+    stats_got = swap(stats, "mp", 2)
+    a_send, _, (a_got,), _ = stage([first(a_own, a_seg)], [*ud_send, predictions], 1)
+    p_parts = send_last(p_kept, p_seg)
+    u_send, _, (u_then,), stats = stage([second(u_own, u_seg, u_got)], a_send, 1, (stats, stats_got))
+    (d_kept,) = combine([kept(d_own, d_seg, d_got, d_then)], u_send, 1)
+    p_parts, d_input = gate([p_parts, d_input], u_send)
+    stats_got = swap(stats, "dp", 1)
+    d_parts = send_last(d_kept, d_seg)
     r_pred = summed(p_parts)
-
-    send_x, send_y, u_kept = combine(
-        [[[(g, *a_seg.then_x) for g in a_own] + [second(a_y, a_seg.b)]], [[(g, *a_seg.then_y) for g in a_own] + [second(a_x, a_seg.a)]],
-         kept(u_own, u_seg, u_x, u_y, u_then_x, u_then_y)],
-        [r_pred, d_parts, input_xc],
-    )
-    (d_parts,) = gate([d_parts], [send_x])
-    got_x, got_y, u_parts = swap(send_x, "mp", 2), swap(send_y, "dp", 1), send_last(u_kept, u_seg)
+    a_send, _, (a_then,), stats = stage([second(a_own, a_seg, a_got)], [*u_send, r_pred], 1, (stats, stats_got))
+    input_x, input_c = swap(d_input, "mp", 2), swap(d_input, "mp", 1)
+    (u_kept,) = combine([kept(u_own, u_seg, u_got, u_then)], a_send, 1)
+    (d_parts,) = gate([d_parts], a_send)
+    for at in range(2, dp_size.bit_length() - 2):
+        stats = stats + swap(stats, "dp", 1 << at)
+    u_parts = send_last(u_kept, u_seg)
     r_down = summed(d_parts)
+    (a_kept,) = combine([kept(a_own, a_seg, a_got, a_then)], [u_kept], 1)
+    a_parts = send_last(a_kept, a_seg)
     (patches_grad,) = call(
-        in_order_kernel, [((SHARDS, length, width), BF)], (pos, d_input, input_c, input_x, input_xc), 2, tokens=(send_x, send_y)
-    )
-    (stats,) = gate([stats], [send_x])
-    bit = 2
-    while bit < dp_size:
-        stats = hop(stats, "dp", bit)
-        bit *= 2
-
-    (a_kept,) = combine([kept(a_own, a_seg, a_x, a_y, (got_x, 0, a_seg.b), (got_y, 0, a_seg.a))], [patches_grad])
-    a_parts = send_last(a_kept, a_seg)
+        in_order_kernel, [((SHARDS, length, width), BF)], (pos, d_input, input_c, input_x, swap(input_x, "mp", 1)), 2,
+    )
     r_up, r_attn = summed(u_parts), summed(a_parts)
 
     count = dp_size * patches.shape[0] * length
@@ -697,7 +666,6 @@
     n_var = channels // SHARDS
     variance = lax.dynamic_slice_in_dim(square - mean * mean, me * n_var, n_var)
     tail = r_attn[:, 4 * cols + p_cols :]
-    n_small = channels // dp_size
 
     def qkv_of(block, n):
         return jnp.stack([block[:, i * n : (i + 1) * n] for i in range(3)])
@@ -713,11 +681,11 @@
         r_up,
         r_down.T,
         r_attn[:, 4 * cols : 4 * cols + p_cols],
-        tail[:n_small, 3],
+        tail[:n_small, 4],
         tail[:n_small, 2],
         qkv_of(r_pred, p_cols),
         r_pred[:, 3 * p_cols : 4 * p_cols].T,
-        tail[n_small:, 2],
+        tail[:n_small, 3],
         r_pred[:, 4 * p_cols : 4 * p_cols + p_hid],
         r_pred[:, 4 * p_cols + p_hid :].T,
     )

time: 312 us -> 280 us (0.90)
  waiting for transfers between devices: 98.8 us -> 64.4 us
  starting transfers between devices: 47.4 us -> 53.8 us
  local copies, waits for them, and re-layouts: 56.3 us -> 51 us
    ppermute x44 -> x45, waiting for transfers between devices: 75.7 us -> 57.8 us  [swap(): return lax.ppermute(value, axis, [(i, i ^ bit) for i in range(size)])]
    all_to_all x4, waiting for transfers between devices: 23.1 us -> 6.53 us  [send_last(): lax.all_to_all(jnp.swapaxes(kept, 0, 1), 'dp', 0, 0, axis_index_groups=gr...]
    ppermute x44 -> x45, starting transfers between devices: 29.9 us -> 35.2 us  [swap(): return lax.ppermute(value, axis, [(i, i ^ bit) for i in range(size)])]
    pallas_call x6 -> x10, Pallas kernels: 18.4 us -> 23.3 us  [combine(): pl.pallas_call(kernel, out_shape=[jax.ShapeDtypeStruct((size, 128), BF) f...]
    slice x4 -> x1, local copies, waits for them, and re-layouts: 4.71 us -> 0.73 us  [body(): tail[:n_small, 3]]
    unnamed x208 -> x179, local copies, waits for them, and re-layouts: 39.7 us -> 36.8 us
    pallas_call x12 -> x11, Pallas kernels: 80.7 us -> 78.2 us  [call(): pl.pallas_call(lambda *refs: kernel(*refs[:n_args], *refs[n_all:]), out_s...]
  transfers between devices with their start and end apart: 48 -> 49, of which waited for: 23 -> 11; matrix products, arithmetic and copies ran while one was open for 7% -> 6% of each run, Pallas kernels for 22% -> 27%
where the time goes in v1:
time: 280 us; the launch traced here: 278 us
  Pallas kernels  101 us (36%)
  waiting for transfers between devices  64.4 us (23%)
  starting transfers between devices  53.8 us (19%)
  local copies, waits for them, and re-layouts  51 us (18%)
  other arithmetic  6.1 us (2%)
    pallas_call x11, Pallas kernels, call(): pl.pallas_call(lambda *refs: kernel(*refs[:n_args], *refs[n_all:]), out_s...  78.2 us
    ppermute x45, waiting for transfers between devices, swap(): return lax.ppermute(value, axis, [(i, i ^ bit) for i in range(size)])  57.8 us
    unnamed x179, local copies, waits for them, and re-layouts  36.8 us
    ppermute x45, starting transfers between devices, swap(): return lax.ppermute(value, axis, [(i, i ^ bit) for i in range(size)])  35.2 us
    pallas_call x10, Pallas kernels, combine(): pl.pallas_call(kernel, out_shape=[jax.ShapeDtypeStruct((size, 128), BF) f...  23.3 us
    all_to_all x4, starting transfers between devices, send_last(): lax.all_to_all(jnp.swapaxes(kept, 0, 1), 'dp', 0, 0, axis_index_groups=gr...  18.6 us
    all_to_all x4, waiting for transfers between devices, send_last(): lax.all_to_all(jnp.swapaxes(kept, 0, 1), 'dp', 0, 0, axis_index_groups=gr...  6.53 us
  transfers between devices with their start and end apart: 49, of which 11 were waited for; matrix products, arithmetic and copies ran while one was open for 6% of the time, Pallas kernels for 27%

profile of v1, /device:TPU:0, one launch (start us, length us, event | category | flops | bytes accessed | tf_op | source)
XLA Modules:
  0.0 278.5 jit_solution(16126108111748799760)
XLA Ops:
  4.7 2.9 %collective-permute-start.1 = (bf16[384,768]{1,0:T(8,128)(2,1)S(1)}, bf16[384,768]{1,0:T(8,128)(2,1)S(1)}, u32[]{:S(2)}, u32[]{:S(2)}) collective-permute-start(bf16[384,768]{1,0:T(8,128)(2,1)S(1)} %get-tuple-element.73.refs_8_), channel_id=1, source_target_pairs={{0,2},{1,3},{2,0},{3,1},{4,6},{5,7},{6,4},{7,5},{8,10},{9,11},{10,... | collective-permute-start | bytes 1769480 | tf_op jit(solution)/shard_map/ppermute | solution.py:472
  11.1 9.9 %collective-permute-done.1.refs_0_ = bf16[384,768]{1,0:T(8,128)(2,1)S(1)} collective-permute-done((bf16[384,768]{1,0:T(8,128)(2,1)S(1)}, bf16[384,768]{1,0:T(8,128)(2,1)S(1)}, u32[]{:S(2)}, u32[]{:S(2)}) %collective-permute-start.1) | collective-permute-done | bytes 589856 | tf_op jit(solution)/shard_map/ppermute | solution.py:472
  21.8 1.8 collective-permute-start.2
  25.0 11.6 %collective-permute-done.2.refs_8_.refs_16_ = bf16[384,768]{1,0:T(8,128)(2,1)} collective-permute-done((bf16[384,768]{1,0:T(8,128)(2,1)}, bf16[384,768]{1,0:T(8,128)(2,1)}, u32[]{:S(2)}, u32[]{:S(2)}) %collective-permute-start.2) | collective-permute-done | bytes 589856 | tf_op jit(solution)/shard_map/ppermute | solution.py:472
  41.9 9.6 %shard_map.308 = (f32[256,768]{1,0:T(8,128)S(1)}, bf16[2304,256]{1,0:T(8,128)(2,1)S(1)}, bf16[12,256,256]{2,1,0:T(8,128)(2,1)}, bf16[768,256]{1,0:T(8,128)(2,1)S(1)}) custom-call(s32[2]{0:T(128)S(1)} %pad_add_fusion.refs_0_, bf16[256,768]{1,0:T(8,128)(2,1)S(1)} %copy-done.44, s32[1,256]{1,0:T(1,128)S(1)} %constant_dynamic-slice_fusion.3.refs_2_, ...), custom_call_target="tpu_custom_call" | custom-call | flops 10350000128 | bytes 9049096 | tf_op jit(solution)/shard_map/pallas_call | solution.py:114
  61.2 5.8 %shard_map.310 = (bf16[256,3072]{1,0:T(8,128)(2,1)}, bf16[256,3072]{1,0:T(8,128)(2,1)}) custom-call(s32[2]{0:T(128)S(1)} %pad_add_fusion.refs_0_, f32[256,768]{1,0:T(8,128)S(1)} %copy-done.23, f32[1,768]{1,0:T(1,128)S(1)} %reshape.243.refs_2_.refs_4_, bf16[768,768]{1,0:T(8,128)(2,1)S(1)} %copy-done.61, ...), custom_call_target="tpu_custom_call" | custom-call | flops 6899999744 | bytes 8653832 | tf_op jit(solution)/shard_map/pallas_call | solution.py:114
  67.0 6.7 %collective-permute-done.12.refs_0_ = bf16[384,768]{1,0:T(8,128)(2,1)S(1)} collective-permute-done((bf16[384,768]{1,0:T(8,128)(2,1)}, bf16[384,768]{1,0:T(8,128)(2,1)S(1)}, u32[]{:S(2)}, u32[]{:S(2)}) %collective-permute-start.12) | collective-permute-done | bytes 589856 | tf_op jit(solution)/shard_map/ppermute | solution.py:472
  74.6 7.6 %collective-permute-done.16.refs_12_ = bf16[1344,384]{1,0:T(8,128)(2,1)} collective-permute-done((bf16[1344,384]{1,0:T(8,128)(2,1)}, bf16[1344,384]{1,0:T(8,128)(2,1)}, u32[]{:S(2)}, u32[]{:S(2)}) %collective-permute-start.16) | collective-permute-done | bytes 1032224 | tf_op jit(solution)/shard_map/ppermute | solution.py:472
  87.0 3.9 %shard_map.313.refs_1_.refs_9_ = bf16[256,768]{1,0:T(8,128)(2,1)S(1)} custom-call(s32[2]{0:T(128)S(1)} %pad_add_fusion.refs_0_, f32[256,768]{1,0:T(8,128)S(1)} %copy-done.23, bf16[256,3072]{1,0:T(8,128)(2,1)} %get-tuple-element.79.refs_1_.refs_2_.refs_3_, bf16[768,768]{1,0:T(8,128)(2,1)S(1)} %copy-done.63, ...), custom_call_target="tpu_custom_call" | custom-call | flops 4600000000 | bytes 7471112 | tf_op jit(solution)/shard_map/pallas_call | solution.py:114
  91.0 20.4 %shard_map.315 = (bf16[768,128]{1,0:T(8,128)(2,1)S(1)}, f32[8,384]{1,0:T(8,128)S(1)}, bf16[6912,128]{1,0:T(8,128)(2,1)}, bf16[6912,128]{1,0:T(8,128)(2,1)}, bf16...) custom-call(s32[2]{0:T(128)S(1)} %pad_add_fusion.refs_0_, ...), custom_call_target="tpu_custom_call" | custom-call | flops 34500001792 | bytes 9470984 | tf_op jit(solution)/shard_map/pallas_call | solution.py:114
  112.5 3.7 %shard_map.316 = (bf16[9216,128]{1,0:T(8,128)(2,1)S(1)}, bf16[9216,128]{1,0:T(8,128)(2,1)}) custom-call(s32[2]{0:T(128)S(1)} %pad_add_fusion.refs_0_, s32[768,1]{1,0:T(8,128)S(1)} %copy.115.refs_1_, f32[256,768]{1,0:T(8,128)S(1)} %get-tuple-element.85.refs_2_, bf16[256,3072]{1,0:T(8,128)(2,1)S(1)} %copy-done.15), custom_call_target="tpu_custom_call" | custom-call | flops 34500001792 | bytes 7080968 | tf_op jit(solution)/shard_map/pallas_call | solution.py:114
  118.1 2.1 shard_map.317
  126.5 12.0 %shard_map.319 = (bf16[9216,128]{1,0:T(8,128)(2,1)}, bf16[9216,128]{1,0:T(8,128)(2,1)}, f32[256,768]{1,0:T(8,128)}, f32[1,768]{1,0:T(1,128)S(1)}) custom-call(s32[2]{0:T(128)S(1)} %pad_add_fusion.refs_0_, s32[768,1]{1,0:T(8,128)S(1)} %copy.115.refs_1_, f32[256,768]{1,0:T(8,128)} %copy-done.78, f32[256,768]{1,0:T(8,128)} %copy-done.22, ...), custom_call_target="tpu_custom_call" | custom-call | flops 115000000512 | bytes 18097160 | tf_op jit(solution)/shard_map/pallas_call | solution.py:114
  142.1 3.6 %shard_map.321 = (bf16[3264,128]{1,0:T(8,128)(2,1)}, bf16[3072,128]{1,0:T(8,128)(2,1)}, f32[8,384]{1,0:T(8,128)S(1)}) custom-call(f32[8,384]{1,0:T(8,128)S(1)} %get-tuple-element.92.refs_0_, f32[8,384]{1,0:T(8,128)S(1)} %collective-permute-done.22.refs_1_, bf16[9216,128]{1,0:T(8,128)(2,1)} %copy-done.12, ...), custom_call_target="tpu_custom_call" | custom-call | flops 34500001792 | bytes 5308416 | tf_op jit(solution)/shard_map/pallas_call | solution.py:214
  148.2 2.7 collective-permute-start.30
  153.0 16.4 %shard_map.323 = (bf16[10752,128]{1,0:T(8,128)(2,1)}, bf16[10752,128]{1,0:T(8,128)(2,1)}, bf16[1536,128]{1,0:T(8,128)(2,1)S(1)}) custom-call(s32[2]{0:T(128)S(1)} %pad_add_fusion.refs_0_, s32[768,1]{1,0:T(8,128)S(1)} %copy.115.refs_1_, bf16[256,768]{1,0:T(8,128)(2,1)S(1)} %copy-done.45, f32[1,768]{1,0:T(1,128)S(1)} %copy-done.57, f32[256,768]{1,0:T(8,128)S(1)} %copy-done.81, ...), custom_call_target="tpu_custom_call" | custom-call | flops 115000000512 | bytes 15556616 | tf_op jit(solution)/shard_map/pallas_call | solution.py:114
  171.0 1.8 copy-done.3
  174.6 3.3 %shard_map.325 = (bf16[3456,128]{1,0:T(8,128)(2,1)}, bf16[3456,128]{1,0:T(8,128)(2,1)}, f32[8,384]{1,0:T(8,128)S(1)}) custom-call(f32[8,384]{1,0:T(8,128)S(1)} %get-tuple-element.109.refs_0_, f32[8,384]{1,0:T(8,128)S(1)} %collective-permute-done.30.refs_1_, bf16[9216,128]{1,0:T(8,128)(2,1)S(1)} %copy-done.3, ...), custom_call_target="tpu_custom_call" | custom-call | flops 69000003584 | bytes 5898240 | tf_op jit(solution)/shard_map/pallas_call | solution.py:214
  185.4 4.1 %all-to-all-start = ((bf16[4,9,48,128]{3,2,1,0:T(8,128)(2,1)}), bf16[4,9,48,128]{3,2,1,0:T(8,128)(2,1)}, u32[]{:S(2)}, u32[]{:S(2)}) async-start(bf16[4,9,48,128]{3,2,1,0:T(8,128)(2,1)} %bitcast.89), calls=%async_computation | async-start | bytes 884736 | tf_op jit(solution)/shard_map/all_to_all | solution.py:483
  196.6 3.0 %shard_map.328 = (bf16[2304,128]{1,0:T(8,128)(2,1)S(1)}, bf16[3072,128]{1,0:T(8,128)(2,1)}) custom-call(bf16[10752,128]{1,0:T(8,128)(2,1)} %get-tuple-element.116.refs_0_.refs_2_, bf16[10752,128]{1,0:T(8,128)(2,1)} %collective-permute-done.34.refs_1_.refs_3_, bf16[3456,128]{1,0:T(8,128)(2,1)} %get-tuple-element.112.refs_6_.refs_2_, ...), custom_call_target="tpu_custom_call" | custom-call | flops 1150000000 | bytes 4128768 | tf_op jit(solution)/shard_map/pallas_call | solution.py:214
  201.5 2.5 shard_map.329
  204.0 1.8 shard_map.335
  206.8 4.4 %all-to-all-start.3 = ((bf16[4,6,96,128]{3,2,1,0:T(8,128)(2,1)}), bf16[4,6,96,128]{3,2,1,0:T(8,128)(2,1)}, u32[]{:S(2)}, u32[]{:S(2)}) async-start(bf16[4,6,96,128]{3,2,1,0:T(8,128)(2,1)} %bitcast.87), calls=%async_computation.3 | async-start | bytes 1179648 | tf_op jit(solution)/shard_map/all_to_all | solution.py:483
  216.4 8.9 %collective-permute-done.38.refs_1_ = f32[8,384]{1,0:T(8,128)S(1)} collective-permute-done((f32[8,384]{1,0:T(8,128)S(1)}, f32[8,384]{1,0:T(8,128)S(1)}, u32[]{:S(2)}, u32[]{:S(2)}) %collective-permute-start.38) | collective-permute-done | bytes 12320 | tf_op jit(solution)/shard_map/ppermute | solution.py:472
  227.9 1.8 shard_map.332
  229.7 4.4 %collective-permute-done.44.refs_5_ = bf16[1152,128]{1,0:T(8,128)(2,1)} collective-permute-done((bf16[1152,128]{1,0:T(8,128)(2,1)S(1)}, bf16[1152,128]{1,0:T(8,128)(2,1)}, u32[]{:S(2)}, u32[]{:S(2)}) %collective-permute-start.44) | collective-permute-done | bytes 294944 | tf_op jit(solution)/shard_map/ppermute | solution.py:472
  236.7 5.0 %all-to-all-start.2 = ((bf16[4,6,96,128]{3,2,1,0:T(8,128)(2,1)}), bf16[4,6,96,128]{3,2,1,0:T(8,128)(2,1)}, u32[]{:S(2)}, u32[]{:S(2)}) async-start(bf16[4,6,96,128]{3,2,1,0:T(8,128)(2,1)} %bitcast.88), calls=%async_computation.2 | async-start | bytes 1179648 | tf_op jit(solution)/shard_map/all_to_all | solution.py:483
  248.2 5.1 %collective-permute-done.41.refs_3_ = bf16[1152,128]{1,0:T(8,128)(2,1)S(1)} collective-permute-done((bf16[1152,128]{1,0:T(8,128)(2,1)}, bf16[1152,128]{1,0:T(8,128)(2,1)S(1)}, u32[]{:S(2)}, u32[]{:S(2)}) %collective-permute-start.41) | collective-permute-done | bytes 294944 | tf_op jit(solution)/shard_map/ppermute | solution.py:472
  253.3 1.8 shard_map.334
  256.0 5.1 %all-to-all-start.1 = ((bf16[4,7,96,128]{3,2,1,0:T(8,128)(2,1)}), bf16[4,7,96,128]{3,2,1,0:T(8,128)(2,1)S(1)}, u32[]{:S(2)}, u32[]{:S(2)}) async-start(bf16[4,7,96,128]{3,2,1,0:T(8,128)(2,1)} %bitcast.76), calls=%async_computation.1 | async-start | bytes 1376256 | tf_op jit(solution)/shard_map/all_to_all | solution.py:483
  261.7 2.7 shard_map.331
  268.2 6.5 %all-to-all-done.1 = bf16[4,7,96,128]{3,2,1,0:T(8,128)(2,1)S(1)} async-done(((bf16[4,7,96,128]{3,2,1,0:T(8,128)(2,1)}), bf16[4,7,96,128]{3,2,1,0:T(8,128)(2,1)S(1)}, u32[]{:S(2)}, u32[]{:S(2)}) %all-to-all-start.1) | async-done | bytes 688160 | tf_op jit(solution)/shard_map/all_to_all | solution.py:483
  (324 shorter events, 94.2 us)
Async XLA Ops:
  4.7 16.3 %collective-permute-start.1 = (bf16[384,768]{1,0:T(8,128)(2,1)S(1)}, bf16[384,768]{1,0:T(8,128)(2,1)S(1)}, u32[]{:S(2)}, u32[]{:S(2)}) collective-permute-start(bf16[384,768]{1,0:T(8,128)(2,1)S(1)} %get-tuple-element.73.refs_8_), channel_id=1, source_target_pairs={{0,2},{1,3},{2,0},{3,1},{4,6},{5,7},{6,4},{7,5},{8,10},{9,11},{10,... | collective-permute-start | bytes 1769480 | tf_op jit(solution)/shard_map/ppermute | solution.py:472
  7.6 32.7 %collective-permute-start = (bf16[768,768]{1,0:T(8,128)(2,1)}, bf16[768,768]{1,0:T(8,128)(2,1)}, u32[]{:S(2)}, u32[]{:S(2)}) collective-permute-start(bf16[768,768]{1,0:T(8,128)(2,1)} %get-tuple-element.72.refs_5_.refs_13_), channel_id=1, source_target_pairs={{0,1},{1,0},{2,3},{3,2},{4,5},{5,4},{6,7},{7,6},{8,9},{9,8},{10,11... | collective-permute-start | bytes 3538952 | tf_op jit(solution)/shard_map/ppermute | solution.py:472
  36.6 21.8 %collective-permute-start.5 = (bf16[768,768]{1,0:T(8,128)(2,1)}, bf16[768,768]{1,0:T(8,128)(2,1)}, u32[]{:S(2)}, u32[]{:S(2)}) collective-permute-start(bf16[768,768]{1,0:T(8,128)(2,1)} %refs_6_.3), channel_id=1, source_target_pairs={{0,1},{1,0},{2,3},{3,2},{4,5},{5,4},{6,7},{7,6},{8,9},{9,8},{10,11... | collective-permute-start | bytes 3538952 | tf_op jit(solution)/shard_map/ppermute | solution.py:472
  38.1 18.3 %collective-permute-start.15 = (bf16[1344,384]{1,0:T(8,128)(2,1)S(1)}, bf16[1344,384]{1,0:T(8,128)(2,1)}, u32[]{:S(2)}, u32[]{:S(2)}) collective-permute-start(bf16[1344,384]{1,0:T(8,128)(2,1)S(1)} %copy-done.8), channel_id=1, source_target_pairs={{0,1},{1,0},{2,3},{3,2},{4,5},{5,4},{6,7},{7,6},{8,9},{9,8},{10,11... | collective-permute-start | bytes 3096584 | tf_op jit(solution)/shard_map/ppermute | solution.py:472
  38.9 18.1 %collective-permute-start.11 = (bf16[384,768]{1,0:T(8,128)(2,1)}, bf16[384,768]{1,0:T(8,128)(2,1)}, u32[]{:S(2)}, u32[]{:S(2)}) collective-permute-start(bf16[384,768]{1,0:T(8,128)(2,1)} %shard_map.311), channel_id=1, source_target_pairs={{0,2},{1,3},{2,0},{3,1},{4,6},{5,7},{6,4},{7,5},{8,10},{9,11},{10,... | collective-permute-start | bytes 1769480 | tf_op jit(solution)/shard_map/ppermute | solution.py:472
  41.9 18.0 %collective-permute-start.8 = (bf16[768,384]{1,0:T(8,128)(2,1)}, bf16[768,384]{1,0:T(8,128)(2,1)}, u32[]{:S(2)}, u32[]{:S(2)}) collective-permute-start(bf16[768,384]{1,0:T(8,128)(2,1)} %copy-done.28), channel_id=1, source_target_pairs={{0,1},{1,0},{2,3},{3,2},{4,5},{5,4},{6,7},{7,6},{8,9},{9,8},{10,11... | collective-permute-start | bytes 1769480 | tf_op jit(solution)/shard_map/ppermute | solution.py:472
  56.5 28.2 %collective-permute-start.10 = (bf16[768,768]{1,0:T(8,128)(2,1)}, bf16[768,768]{1,0:T(8,128)(2,1)}, u32[]{:S(2)}, u32[]{:S(2)}) collective-permute-start(bf16[768,768]{1,0:T(8,128)(2,1)} %refs_12_.1), channel_id=1, source_target_pairs={{0,1},{1,0},{2,3},{3,2},{4,5},{5,4},{6,7},{7,6},{8,9},{9,8},{10,11... | collective-permute-start | bytes 3538952 | tf_op jit(solution)/shard_map/ppermute | solution.py:472
  57.0 25.1 %collective-permute-start.16 = (bf16[1344,384]{1,0:T(8,128)(2,1)}, bf16[1344,384]{1,0:T(8,128)(2,1)}, u32[]{:S(2)}, u32[]{:S(2)}) collective-permute-start(bf16[1344,384]{1,0:T(8,128)(2,1)} %shard_map.314.refs_10_), channel_id=1, source_target_pairs={{0,2},{1,3},{2,0},{3,1},{4,6},{5,7},{6,4},{7,5},{8,10},{9,11},{10,... | collective-permute-start | bytes 3096584 | tf_op jit(solution)/shard_map/ppermute | solution.py:472
  58.4 15.3 %collective-permute-start.12 = (bf16[384,768]{1,0:T(8,128)(2,1)}, bf16[384,768]{1,0:T(8,128)(2,1)S(1)}, u32[]{:S(2)}, u32[]{:S(2)}) collective-permute-start(bf16[384,768]{1,0:T(8,128)(2,1)} %collective-permute-done.11.refs_5_.refs_1_.refs_14_), channel_id=1, source_target_pairs={{0,4},{4,0},{8,12},{12,8},{16,20},{20,16},{24,28},{28,24},{1,5},{5... | collective-permute-start | bytes 1769480 | tf_op jit(solution)/shard_map/ppermute | solution.py:472
  59.9 24.7 %collective-permute-start.13 = (bf16[384,768]{1,0:T(8,128)(2,1)}, bf16[384,768]{1,0:T(8,128)(2,1)}, u32[]{:S(2)}, u32[]{:S(2)}) collective-permute-start(bf16[384,768]{1,0:T(8,128)(2,1)} %collective-permute-done.11.refs_5_.refs_1_.refs_14_), channel_id=1, source_target_pairs={{0,1},{1,0},{2,3},{3,2},{4,5},{5,4},{6,7},{7,6},{8,9},{9,8},{10,11... | collective-permute-start | bytes 1769480 | tf_op jit(solution)/shard_map/ppermute | solution.py:472
  117.6 20.9 %collective-permute-start.21 = (bf16[9216,128]{1,0:T(8,128)(2,1)}, bf16[9216,128]{1,0:T(8,128)(2,1)}, u32[]{:S(2)}, u32[]{:S(2)}) collective-permute-start(bf16[9216,128]{1,0:T(8,128)(2,1)} %get-tuple-element.86.refs_4_), channel_id=1, source_target_pairs={{0,1},{1,0},{2,3},{3,2},{4,5},{5,4},{6,7},{7,6},{8,9},{9,8},{10,11... | collective-permute-start | bytes 7077896 | tf_op jit(solution)/shard_map/ppermute | solution.py:472
  120.3 18.9 %collective-permute-start.23 = (bf16[1920,128]{1,0:T(8,128)(2,1)S(1)}, bf16[1920,128]{1,0:T(8,128)(2,1)}, u32[]{:S(2)}, u32[]{:S(2)}) collective-permute-start(bf16[1920,128]{1,0:T(8,128)(2,1)S(1)} %get-tuple-element.88.refs_2_.refs_19_), channel_id=1, source_target_pairs={{0,4},{4,0},{8,12},{12,8},{16,20},{20,16},{24,28},{28,24},{1,5},{5... | collective-permute-start | bytes 1474568 | tf_op jit(solution)/shard_map/ppermute | solution.py:472
  121.9 17.3 %collective-permute-start.24 = (bf16[1536,128]{1,0:T(8,128)(2,1)}, bf16[1536,128]{1,0:T(8,128)(2,1)}, u32[]{:S(2)}, u32[]{:S(2)}) collective-permute-start(bf16[1536,128]{1,0:T(8,128)(2,1)} %get-tuple-element.87.refs_1_.refs_18_), channel_id=1, source_target_pairs={{0,2},{1,3},{2,0},{3,1},{4,6},{5,7},{6,4},{7,5},{8,10},{9,11},{10,... | collective-permute-start | bytes 1179656 | tf_op jit(solution)/shard_map/ppermute | solution.py:472
  122.4 16.1 %collective-permute-start.20 = (bf16[768,128]{1,0:T(8,128)(2,1)}, bf16[768,128]{1,0:T(8,128)(2,1)S(1)}, u32[]{:S(2)}, u32[]{:S(2)}) collective-permute-start(bf16[768,128]{1,0:T(8,128)(2,1)} %shard_map.318.refs_0_), channel_id=1, source_target_pairs={{0,2},{1,3},{2,0},{3,1},{4,6},{5,7},{6,4},{7,5},{8,10},{9,11},{10,... | collective-permute-start | bytes 589832 | tf_op jit(solution)/shard_map/ppermute | solution.py:472
  147.0 24.0 %collective-permute-start.25 = (bf16[9216,128]{1,0:T(8,128)(2,1)}, bf16[9216,128]{1,0:T(8,128)(2,1)}, u32[]{:S(2)}, u32[]{:S(2)}) collective-permute-start(bf16[9216,128]{1,0:T(8,128)(2,1)} %get-tuple-element.90.refs_2_.refs_8_), channel_id=1, source_target_pairs={{0,1},{1,0},{2,3},{3,2},{4,5},{5,4},{6,7},{7,6},{8,9},{9,8},{10,11... | collective-permute-start | bytes 7077896 | tf_op jit(solution)/shard_map/ppermute | solution.py:472
  147.1 23.9 %collective-permute-start.29 = (bf16[3264,128]{1,0:T(8,128)(2,1)}, bf16[3264,128]{1,0:T(8,128)(2,1)S(1)}, u32[]{:S(2)}, u32[]{:S(2)}) collective-permute-start(bf16[3264,128]{1,0:T(8,128)(2,1)} %get-tuple-element.95.refs_2_.refs_19_), channel_id=1, source_target_pairs={{0,2},{1,3},{2,0},{3,1},{4,6},{5,7},{6,4},{7,5},{8,10},{9,11},{10,... | collective-permute-start | bytes 2506760 | tf_op jit(solution)/shard_map/ppermute | solution.py:472
  147.7 23.3 %collective-permute-start.28 = (bf16[3072,128]{1,0:T(8,128)(2,1)}, bf16[3072,128]{1,0:T(8,128)(2,1)}, u32[]{:S(2)}, u32[]{:S(2)}) collective-permute-start(bf16[3072,128]{1,0:T(8,128)(2,1)} %get-tuple-element.96.refs_3_.refs_20_), channel_id=1, source_target_pairs={{0,4},{4,0},{8,12},{12,8},{16,20},{20,16},{24,28},{28,24},{1,5},{5... | collective-permute-start | bytes 2359304 | tf_op jit(solution)/shard_map/ppermute | solution.py:472
  148.2 21.9 %collective-permute-start.27 = (bf16[768,128]{1,0:T(8,128)(2,1)}, bf16[768,128]{1,0:T(8,128)(2,1)S(1)}, u32[]{:S(2)}, u32[]{:S(2)}) collective-permute-start(bf16[768,128]{1,0:T(8,128)(2,1)} %get-tuple-element.98.refs_3_), channel_id=1, source_target_pairs={{0,1},{1,0},{2,3},{3,2},{4,5},{5,4},{6,7},{7,6},{8,9},{9,8},{10,11... | collective-permute-start | bytes 589832 | tf_op jit(solution)/shard_map/ppermute | solution.py:472
  148.2 22.8 %collective-permute-start.30 = (f32[8,384]{1,0:T(8,128)S(1)}, f32[8,384]{1,0:T(8,128)S(1)}, u32[]{:S(2)}, u32[]{:S(2)}) collective-permute-start(f32[8,384]{1,0:T(8,128)S(1)} %get-tuple-element.109.refs_0_), channel_id=1, source_target_pairs={{0,16},{4,20},{8,24},{12,28},{16,0},{20,4},{24,8},{28,12},{1,17},{... | collective-permute-start | bytes 36872 | tf_op jit(solution)/shard_map/ppermute | solution.py:472
  170.8 24.7 %collective-permute-start.34 = (bf16[10752,128]{1,0:T(8,128)(2,1)}, bf16[10752,128]{1,0:T(8,128)(2,1)}, u32[]{:S(2)}, u32[]{:S(2)}) collective-permute-start(bf16[10752,128]{1,0:T(8,128)(2,1)} %get-tuple-element.106.refs_3_.refs_8_), channel_id=1, source_target_pairs={{0,1},{1,0},{2,3},{3,2},{4,5},{5,4},{6,7},{7,6},{8,9},{9,8},{10,11... | collective-permute-start | bytes 8257544 | tf_op jit(solution)/shard_map/ppermute | solution.py:472
  178.0 23.5 %collective-permute-start.32 = (bf16[3456,128]{1,0:T(8,128)(2,1)}, bf16[3456,128]{1,0:T(8,128)(2,1)S(1)}, u32[]{:S(2)}, u32[]{:S(2)}) collective-permute-start(bf16[3456,128]{1,0:T(8,128)(2,1)} %get-tuple-element.113.refs_7_.refs_3_), channel_id=1, source_target_pairs={{0,4},{4,0},{8,12},{12,8},{16,20},{20,16},{24,28},{28,24},{1,5},{5... | collective-permute-start | bytes 2654216 | tf_op jit(solution)/shard_map/ppermute | solution.py:472
  179.6 21.9 %collective-permute-start.33 = (bf16[3456,128]{1,0:T(8,128)(2,1)}, bf16[3456,128]{1,0:T(8,128)(2,1)}, u32[]{:S(2)}, u32[]{:S(2)}) collective-permute-start(bf16[3456,128]{1,0:T(8,128)(2,1)} %get-tuple-element.112.refs_6_.refs_2_), channel_id=1, source_target_pairs={{0,2},{1,3},{2,0},{3,1},{4,6},{5,7},{6,4},{7,5},{8,10},{9,11},{10,... | collective-permute-start | bytes 2654216 | tf_op jit(solution)/shard_map/ppermute | solution.py:472
  185.4 21.3 %all-to-all-start = ((bf16[4,9,48,128]{3,2,1,0:T(8,128)(2,1)}), bf16[4,9,48,128]{3,2,1,0:T(8,128)(2,1)}, u32[]{:S(2)}, u32[]{:S(2)}) async-start(bf16[4,9,48,128]{3,2,1,0:T(8,128)(2,1)} %bitcast.89), calls=%async_computation | async-start | bytes 884736 | tf_op jit(solution)/shard_map/all_to_all | solution.py:483
  199.7 28.2 %collective-permute-start.39 = (bf16[3072,128]{1,0:T(8,128)(2,1)}, bf16[3072,128]{1,0:T(8,128)(2,1)}, u32[]{:S(2)}, u32[]{:S(2)}) collective-permute-start(bf16[3072,128]{1,0:T(8,128)(2,1)} %get-tuple-element.118.refs_7_), channel_id=1, source_target_pairs={{0,4},{4,0},{8,12},{12,8},{16,20},{20,16},{24,28},{28,24},{1,5},{5... | collective-permute-start | bytes 2359304 | tf_op jit(solution)/shard_map/ppermute | solution.py:472
  206.8 30.0 %all-to-all-start.3 = ((bf16[4,6,96,128]{3,2,1,0:T(8,128)(2,1)}), bf16[4,6,96,128]{3,2,1,0:T(8,128)(2,1)}, u32[]{:S(2)}, u32[]{:S(2)}) async-start(bf16[4,6,96,128]{3,2,1,0:T(8,128)(2,1)} %bitcast.87), calls=%async_computation.3 | async-start | bytes 1179648 | tf_op jit(solution)/shard_map/all_to_all | solution.py:483
  211.2 16.6 %collective-permute-start.40 = (bf16[2304,128]{1,0:T(8,128)(2,1)}, bf16[2304,128]{1,0:T(8,128)(2,1)}, u32[]{:S(2)}, u32[]{:S(2)}) collective-permute-start(bf16[2304,128]{1,0:T(8,128)(2,1)} %copy-done.27), channel_id=1, source_target_pairs={{0,2},{1,3},{2,0},{3,1},{4,6},{5,7},{6,4},{7,5},{8,10},{9,11},{10,... | collective-permute-start | bytes 1769480 | tf_op jit(solution)/shard_map/ppermute | solution.py:472
  212.7 17.0 %collective-permute-start.43 = (bf16[1152,128]{1,0:T(8,128)(2,1)}, bf16[1152,128]{1,0:T(8,128)(2,1)}, u32[]{:S(2)}, u32[]{:S(2)}) collective-permute-start(bf16[1152,128]{1,0:T(8,128)(2,1)} %get-tuple-element.120.refs_3_.refs_7_), channel_id=1, source_target_pairs={{0,4},{4,0},{8,12},{12,8},{16,20},{20,16},{24,28},{28,24},{1,5},{5... | collective-permute-start | bytes 884744 | tf_op jit(solution)/shard_map/ppermute | solution.py:472
  213.8 20.3 %collective-permute-start.44 = (bf16[1152,128]{1,0:T(8,128)(2,1)S(1)}, bf16[1152,128]{1,0:T(8,128)(2,1)}, u32[]{:S(2)}, u32[]{:S(2)}) collective-permute-start(bf16[1152,128]{1,0:T(8,128)(2,1)S(1)} %get-tuple-element.119.refs_2_.refs_6_), channel_id=1, source_target_pairs={{0,2},{1,3},{2,0},{3,1},{4,6},{5,7},{6,4},{7,5},{8,10},{9,11},{10,... | collective-permute-start | bytes 884744 | tf_op jit(solution)/shard_map/ppermute | solution.py:472
  225.3 22.9 %collective-permute-start.36 = (bf16[1536,128]{1,0:T(8,128)(2,1)}, bf16[1536,128]{1,0:T(8,128)(2,1)}, u32[]{:S(2)}, u32[]{:S(2)}) collective-permute-start(bf16[1536,128]{1,0:T(8,128)(2,1)} %get-tuple-element.121.refs_1_), channel_id=1, source_target_pairs={{0,2},{1,3},{2,0},{3,1},{4,6},{5,7},{6,4},{7,5},{8,10},{9,11},{10,... | collective-permute-start | bytes 1179656 | tf_op jit(solution)/shard_map/ppermute | solution.py:472
  227.8 33.8 %collective-permute-start.35 = (bf16[1536,128]{1,0:T(8,128)(2,1)}, bf16[1536,128]{1,0:T(8,128)(2,1)}, u32[]{:S(2)}, u32[]{:S(2)}) collective-permute-start(bf16[1536,128]{1,0:T(8,128)(2,1)} %get-tuple-element.121.refs_1_), channel_id=1, source_target_pairs={{0,1},{1,0},{2,3},{3,2},{4,5},{5,4},{6,7},{7,6},{8,9},{9,8},{10,11... | collective-permute-start | bytes 1179656 | tf_op jit(solution)/shard_map/ppermute | solution.py:472
  236.7 19.3 %all-to-all-start.2 = ((bf16[4,6,96,128]{3,2,1,0:T(8,128)(2,1)}), bf16[4,6,96,128]{3,2,1,0:T(8,128)(2,1)}, u32[]{:S(2)}, u32[]{:S(2)}) async-start(bf16[4,6,96,128]{3,2,1,0:T(8,128)(2,1)} %bitcast.88), calls=%async_computation.2 | async-start | bytes 1179648 | tf_op jit(solution)/shard_map/all_to_all | solution.py:483
  256.0 18.7 %all-to-all-start.1 = ((bf16[4,7,96,128]{3,2,1,0:T(8,128)(2,1)}), bf16[4,7,96,128]{3,2,1,0:T(8,128)(2,1)S(1)}, u32[]{:S(2)}, u32[]{:S(2)}) async-start(bf16[4,7,96,128]{3,2,1,0:T(8,128)(2,1)} %bitcast.76), calls=%async_computation.1 | async-start | bytes 1376256 | tf_op jit(solution)/shard_map/all_to_all | solution.py:483
  (106 other events, 678.6 us)

commit v2 on v1

--- a/solution.py
+++ b/solution.py
@@ -104,7 +104,23 @@
 ANYWHERE = pl.BlockSpec(memory_space=pl.ANY)
 
 
+def in_hbm(arrays):
+    return [pltpu.with_memory_space_constraint(a, pltpu.HBM) if n_bytes(a) >= 256 * 1700 else a for a in arrays]
+
+
+def n_bytes(array):
+    return math.prod(array.shape) * array.dtype.itemsize
+
+
 ANYWHERE = pl.BlockSpec(memory_space=pl.ANY)
+
+
+def in_hbm(arrays):
+    return [pltpu.with_memory_space_constraint(a, pltpu.HBM) if n_bytes(a) >= 256 * 1700 else a for a in arrays]
+
+
+def n_bytes(array):
+    return math.prod(array.shape) * array.dtype.itemsize
 
 
 def call(kernel, outs, args, micros, scratch=(), tokens=()):
@@ -121,7 +137,7 @@
         scratch_shapes=[pltpu.VMEM(shape, kind) for shape, kind in scratch],
         compiler_params=pltpu.CompilerParams(vmem_limit_bytes=VMEM_BYTES),
         cost_estimate=pl.CostEstimate(flops=int(micros * COST), bytes_accessed=moved if micros else 0, transcendentals=0),
-    )(*args, *tokens)
+    )(*args, *in_hbm(tokens))
 
 
 def gate(values, tokens):
@@ -131,7 +147,7 @@
         in_specs=[ANYWHERE] * (len(values) + len(tokens)),
         out_specs=[ANYWHERE] * len(values),
         input_output_aliases={at: at for at in range(len(values))},
-    )(*values, *tokens)
+    )(*in_hbm(values), *in_hbm(tokens))
 
 
 def units(value):
@@ -140,33 +156,39 @@
 
 class Segments:
     def __init__(self, rows, cols):
-        self.half, blocks = rows // 2, cols // 128
+        self.eighth, blocks = rows // 8, cols // 128
         self.left, self.right = blocks // 2, blocks - blocks // 2
-        a, b = self.half * self.left, self.half * self.right
+        a, b = 4 * self.eighth * self.left, 4 * self.eighth * self.right
         self.over_x, self.over_y = (0, 2 * a), (2 * a, 2 * b)
         self.then_y, self.then_x = (2 * a + 2 * b, a), (3 * a + 2 * b, b)
         self.keep_left, self.keep_right = (3 * a + 3 * b, a), (4 * a + 3 * b, b)
         self.shape = (4 * (a + b), 128)
         self.a, self.b = a, b
 
-    def put(self, ref, shard, block, value):
-        half, a, b = self.half, self.a, self.b
+    def put(self, refs, shard, block, value):
+        a, b, size = self.a, self.b, self.eighth
         if shard:
             starts_left = (self.over_x[0], self.over_x[0] + a)
             starts_right = (self.then_x[0], self.over_y[0] + b)
         else:
             starts_left = (self.keep_left[0], self.then_y[0])
             starts_right = (self.keep_right[0], self.over_y[0])
-        for side in range(2):
-            if isinstance(block, int):
-                at = starts_left[side] + block * half if block < self.left else starts_right[side] + (block - self.left) * half
-            else:
-                at = jnp.where(block < self.left, starts_left[side], starts_right[side] - self.left * half) + block * half
-                at = pl.multiple_of(at, half)
-            ref[pl.ds(at, half), :] = value[side * half : (side + 1) * half].astype(BF)
-
-
-def combine(outs, tokens, micros, sums=()):
+        is_left = block < self.left
+        count, index = (self.left, block) if is_left else (self.right, block - self.left)
+        for number in range(8):
+            start = (starts_left if is_left else starts_right)[number // 4]
+            at = start + (number % 4 * count + index) * size
+            for ref in refs:
+                if at < ref.shape[0]:
+                    ref[at : at + size, :] = value[number * size : (number + 1) * size].astype(BF)
+                    break
+                at -= ref.shape[0]
+
+    def parts(self):
+        return [((size, 128), BF) for size in (self.over_x[1], self.over_y[1], 2 * (self.a + self.b))]
+
+
+def combine(outs, tokens, micros, sums=(), kind=BF):
     arrays, terms = [], []
     for segments in outs:
         for parts in segments:
@@ -198,14 +220,14 @@
                     copies[term].wait()
 
                 def add(step, carry, row=row, mine=mine, out=out):
-                    here = pl.ds(pl.multiple_of(step * 64, 64), 64)
+                    here = pl.ds(pl.multiple_of(step * 48, 48), 48)
                     total = held[mine[0]][here, :].astype(F32)
                     for term in mine[1:]:
                         total = total + held[term][here, :].astype(F32)
-                    out[pl.ds(pl.multiple_of(row + step * 64, 64), 64), :] = total.astype(BF)
+                    out[pl.ds(pl.multiple_of(row + step * 48, 16), 48), :] = total.astype(kind)
                     return carry
 
-                lax.fori_loop(0, size // 64, add, 0, unroll=2)
+                lax.fori_loop(0, size // 48, add, 0, unroll=2)
                 at += len(parts)
                 row += size
 
@@ -213,14 +235,14 @@
     in_vmem = pl.BlockSpec(memory_space=pltpu.VMEM)
     return pl.pallas_call(
         kernel,
-        out_shape=[jax.ShapeDtypeStruct((size, 128), BF) for size in sizes]
+        out_shape=[jax.ShapeDtypeStruct((size, 128), kind) for size in sizes]
         + ([jax.ShapeDtypeStruct(sums[0].shape, F32)] if sums else []),
         in_specs=[in_vmem] * n_sums + [ANYWHERE] * (n_in - n_sums),
         out_specs=[in_vmem] * (n_out + (1 if sums else 0)),
         scratch_shapes=[pltpu.VMEM((size, 128), BF) for _, _, size in terms] + [pltpu.SemaphoreType.DMA((n_terms,))],
         compiler_params=pltpu.CompilerParams(vmem_limit_bytes=VMEM_BYTES),
         cost_estimate=pl.CostEstimate(flops=int(micros * COST), bytes_accessed=moved if micros else 0, transcendentals=0),
-    )(*sums, *arrays, *tokens)
+    )(*sums, *in_hbm(arrays), *in_hbm(tokens))
 
 
 def pack_attn_kernel(pos, qkv, out, own, direct):
@@ -339,7 +361,7 @@
     stats[0:1, :] = jnp.sum(predicted, 0, keepdims=True)
     stats[1:2, :] = jnp.sum(predicted * predicted, 0, keepdims=True)
 
-    homes = ((g_mine, 0), (g_theirs, 0), (g_mine, 1), (g_theirs, 1))
+    homes = (((g_mine,), 0), ((g_theirs,), 0), ((g_mine,), 1), ((g_theirs,), 1))
     grad_low = cot[...]
     d_pre = (nt(grad_low, w_down[...]) * slope).astype(BF)
     source = rows_at[...]
@@ -371,45 +393,53 @@
     d_enc[...] = nn(d_low, w_embed[...])
 
 
-def enc_down_kernel(pos, rows_at, grad, hidden, mine, theirs):
+def enc_down_kernel(pos, rows_at, grad, hidden, mine, *theirs):
     width = hidden.shape[1] // SHARDS
     segments = Segments(grad.shape[1], width)
     grad_turned = turned(rows_at[...], grad[...].astype(BF))
-    for shard, (home, at) in ((1, (theirs, 0)), (3, (theirs, 1)), (0, (mine, 0)), (2, (mine, 1))):
+    for shard, (home, at) in ((1, (theirs, 0)), (3, (theirs, 1)), (0, ((mine,), 0)), (2, ((mine,), 1))):
         for block, value in enumerate(units(nn(grad_turned, hidden[:, shard * width : (shard + 1) * width]))):
             segments.put(home, at, block, value)
 
 
 def enc_up_kernel(pos, rows_at, grad, middle, gain, slope, *refs):
-    ups, downs, (mine, theirs, grad_mid, d_gain) = refs[:6], refs[6:12], refs[12:]
+    ups, downs, (grad_mid, d_gain, mine), theirs = refs[:6], refs[6:12], refs[12:15], refs[15:]
+    side = pos[1]
     width = ups[0].shape[1]
     value = middle[...]
     segments = Segments(value.shape[1], width)
     n_two, r_two = norm(value)
     b_turned = turned(rows_at[...], (n_two * gain[...]).astype(BF))
-    homes = ((mine, 0), (theirs, 0), (mine, 1), (theirs, 1))
+    homes = (((mine,), 0), (theirs, 0), ((mine,), 1), (theirs, 1))
     low = grad[...].astype(BF)
     d_b = jnp.zeros_like(value)
-    pieces = hidden_pieces(pos[1], ups, width)
+    pieces = hidden_pieces(side, ups, width)
     for piece in (1, 4, 5, 0, 2, 3):
         up, first, size = pieces[piece]
-        shard = (0, 1, 2, 2, 3, 3)[piece]
+        home, at = homes[(0, 1, 2, 2, 3, 3)[piece]]
         d_pre = (nt(low, downs[piece][...]) * slope[:, columns(first, size)].astype(F32)).astype(BF)
         d_b = d_b + nt(d_pre, up[...])
-        home, at = homes[shard]
-        first_block = (first - shard * width) // 128
-        for block, part in enumerate(units(nn(b_turned, d_pre))):
-            segments.put(home, at, first_block + block, part)
+        blocks = units(nn(b_turned, d_pre))
+
+        def put(first_block, home=home, at=at, blocks=blocks):
+            for block, part in enumerate(blocks):
+                segments.put(home, at, first_block + block, part)
+
+        if piece < 2:
+            put(0)
+        else:
+            second_half = side if piece in (2, 4) else 1 - side
+            pl.when(second_half == 0)(lambda put=put: put(0))
+            pl.when(second_half == 1)(lambda put=put, blocks=blocks: put(len(blocks)))
     d_middle, d_gain_two = norm_back(n_two, r_two, gain[...], d_b)
     grad_mid[...] = grad[...] + d_middle
     d_gain[...] = d_gain_two
 
 
 def enc_attn_back_kernel(
-    pos, rows_at, x, gain, grad, qkv, probs, mixed, d_embedded, enc, d_gain_two, p_rows_at, p_d_gains, own, core, d_x, e_x, d_c, e_c,
-    mine, theirs, d_input, far, d_mixed, d_qkv,
+    pos, x, gain, grad, qkv, probs, own, core, d_x, e_x, d_c, e_c, d_qkv, d_input, d_gain, far, d_mixed
 ):
-    me, side = pos[0], pos[1]
+    side = pos[1]
     half = d_x.shape[0]
     per = own.shape[0] // 4 // HEAD_DIM
     cols = per * HEAD_DIM
@@ -422,18 +452,28 @@
         d_mixed[shard * cols : (shard + 1) * cols, :] = nt(pack[3 * cols :, :], low).astype(BF)
     attend_back(qkv, probs, d_mixed, d_qkv, per, HEAD_DIM)
     value = x[...].astype(F32)
-    length, width = value.shape
+    length = value.shape[0]
     normed, inverse = norm(value)
     d_a = jnp.zeros_like(value)
     for shard in range(SHARDS):
         d_a = d_a + tn(d_qkv[shard * 3 * cols : (shard + 1) * 3 * cols, :], packs[shard][: 3 * cols, :])
     d_value, d_gain_one = norm_back(normed, inverse, gain[...], d_a)
+    d_gain[...] = d_gain_one
     for at, block in enumerate(units(grad[...] + d_value)):
         d_input[at * length : (at + 1) * length, :] = block.astype(BF)
 
+
+def enc_attn_weights_kernel(
+    pos, rows_at, x, gain, grad, mixed, d_qkv, d_embedded, enc, d_gain_one, d_gain_two, p_d_gains, mine, *theirs
+):
+    me = pos[0]
+    value = x[...].astype(F32)
+    width = value.shape[1]
+    cols = width // SHARDS
+    normed, _ = norm(value)
     source = rows_at[...]
     a_turned = turned(source, (normed * gain[...]).astype(BF))
-    mid_turned = turned(source, low)
+    mid_turned = turned(source, grad[...].astype(BF))
     channels = d_embedded.shape[1]
     e_cols = channels // SHARDS
     row = lax.broadcasted_iota(jnp.int32, (channels, SHARDS * 128), 0)
@@ -442,15 +482,19 @@
     one_hot = ((((column >> 7) ^ me) * e_cols + within == row) & (within < e_cols)).astype(BF)
     g_embed = nn(turned(source, enc[...]), nn(d_embedded[...], one_hot).astype(BF))
     line = lax.broadcasted_iota(jnp.int32, (8, width), 0)
-    lines = jnp.where(line == 0, d_gain_one, jnp.where(line == 1, d_gain_two[...], 0.0)).astype(BF)
+    lines = jnp.where(line == 0, d_gain_one[...], jnp.where(line == 1, d_gain_two[...], 0.0)).astype(BF)
     lane = lax.broadcasted_iota(jnp.int32, (8, 128), 1) - lax.broadcasted_iota(jnp.int32, (8, 128), 0)
-    p_one_hot = (lax.broadcasted_iota(jnp.int32, (width, channels), 1) == p_rows_at[...]).astype(BF)
+    n_rows, n_small = pos[2], pos[3]
+    device = ((source.astype(F32) + 0.5) / n_rows.astype(F32)).astype(jnp.int32)
+    within_device = source - device * n_rows
+    p_source = device * n_small + jnp.where(within_device >= n_small, within_device - n_small, within_device)
+    p_one_hot = (lax.broadcasted_iota(jnp.int32, (width, channels), 1) == p_source).astype(BF)
     g_small = nn(turned(source, lines), (lane == e_cols).astype(BF)) + nn(
         nt(p_one_hot, p_d_gains[...].astype(BF)).astype(BF), (lane == e_cols + 2).astype(BF)
     )
 
     segments = Segments(width, 4 * cols + 128)
-    homes = ((mine, 0), (theirs, 0), (mine, 1), (theirs, 1))
+    homes = (((mine,), 0), (theirs, 0), ((mine,), 1), (theirs, 1))
     for shard in (1, 3, 0, 2):
         home, at = homes[shard]
         g_qkv = nt(a_turned, d_qkv[shard * 3 * cols : (shard + 1) * 3 * cols, :])
@@ -476,23 +520,14 @@
     return lax.dynamic_index_in_dim(value, index, axis, keepdims=False)
 
 
-def send_last(kept, segments):
+def source_rows(width):
     size = lax.axis_size("dp")
-    groups = [[i for i in range(size) if i % 2 == side] for side in range(2)]
-    kept = kept.reshape(segments.left + segments.right, size // 2, -1, 128)
-    return lax.all_to_all(jnp.swapaxes(kept, 0, 1), "dp", 0, 0, axis_index_groups=groups, tiled=True)
-
-
-def summed(parts):
-    total = jnp.sum(parts.astype(F32), 0)
-    return jnp.swapaxes(total, 0, 1).reshape(total.shape[1], -1)
-
-
-def source_rows(width, side):
-    size = lax.axis_size("dp")
-    blocks = jnp.arange(width, dtype=jnp.int32).reshape(size // 2, 2, width // size)
-    order = jnp.where(side == 0, blocks, blocks[:, ::-1])
-    return jnp.swapaxes(order, 0, 1).reshape(width, 1)
+    number = jnp.arange(8, dtype=jnp.int32)
+    owner = (lax.axis_index("dp") & 7) ^ (number >> 2 | number & 2 | (number & 1) << 2)
+    inner = jnp.arange(width // 8, dtype=jnp.int32).reshape(1, size // 8, width // size)
+    high = jnp.arange(size // 8, dtype=jnp.int32)[None, :, None]
+    rows = (high * 8 + owner[:, None, None]) * (width // size) + inner % (width // size)
+    return rows.reshape(width, 1)
 
 
 def body(
@@ -508,7 +543,7 @@
     p_cols, p_hid = pred_qkv.shape[2], pred_up.shape[1]
     heads = SHARDS * cols // HEAD_DIM
     p_heads = SHARDS * p_cols // P_HEAD_DIM
-    pos = jnp.stack([me, side]).astype(jnp.int32)
+    pos = jnp.stack([me, side, width // dp_size, channels // dp_size]).astype(jnp.int32)
 
     attn_own, attn_direct = call(
         pack_attn_kernel, [((4 * cols, width), BF), ((2 * cols, width), BF)],
@@ -541,9 +576,8 @@
     masked = jnp.any(jnp.arange(length, dtype=jnp.int32)[:, None] == slots[None, :], -1, keepdims=True).astype(F32)
     cot = pick(cotangent, me)
     row = lambda gain: gain.astype(F32)[None, :]
-    rows_at, p_rows_at = source_rows(width, side), source_rows(channels, side)
+    rows_at, p_rows_at = source_rows(width), source_rows(channels)
     n_rows, n_small = width // dp_size, channels // dp_size
-    small_rows_at = rows_at // n_rows * n_small + rows_at % n_small
 
     middle, qkv, probs, mixed = call(
         enc_attn_kernel,
@@ -577,89 +611,164 @@
          ((3 * channels, length), BF)],
     )
 
+    def from_core(theirs):
+        return [swap(part, "mp", 1) for part in theirs]
+
+    def both(own, at, size):
+        mine, away = own
+        segments, start = [], 0
+        for part in away:
+            low, high = max(at, start), min(at + size, start + part.shape[0])
+            if low < high:
+                segments.append([(mine, low, high - low), (part, low - start, high - low)])
+            start += part.shape[0]
+        return segments
+
+    def with_term(segments, array, at):
+        result = []
+        for parts in segments:
+            result.append(parts + [(array, at, parts[0][2])])
+            at += parts[0][2]
+        return result
+
     def first(own, seg):
-        return [(g, *seg.over_x) for g in own], [(g, *seg.over_y) for g in own]
+        return both(own, *seg.over_x), both(own, *seg.over_y)
 
     def second(own, seg, got):
-        return [(g, *seg.then_x) for g in own] + [(got[1][0], got[1][1] + seg.b, seg.b)], [
-            (g, *seg.then_y) for g in own
-        ] + [(got[0][0], got[0][1] + seg.a, seg.a)]
-
-    def kept(own, seg, got, then):
-        return [[(g, *seg.keep_left) for g in own] + [(*got[0], seg.a), (*then[1], seg.a)],
-                [(g, *seg.keep_right) for g in own] + [(*got[1], seg.b), (*then[0], seg.b)]]
-
-    def stage(parts, tokens, micros, sums=()):
-        send = combine([[x for x, _ in parts], [y for _, y in parts]], tokens, micros, sums)
-        got, at = (swap(send[0], "mp", 2), swap(send[1], "dp", 1)), [0, 0]
+        (x, x_at), (y, y_at) = got
+        return with_term(both(own, *seg.then_x), y, y_at + seg.b), with_term(both(own, *seg.then_y), x, x_at + seg.a)
+
+    def kept(own, seg, got, then, low, high, extra=()):
+        segments = []
+        for (start, size), over, after, right in (
+            (seg.keep_left, got[0], then[1], 0), (seg.keep_right, got[1], then[0], 1)
+        ):
+            at, rows = low * size // 4, (high - low) * size // 4
+            part = both(own, start + at, rows)
+            for array, array_at in (over, after):
+                part = with_term(part, array, array_at + at)
+            for array, array_at in extra:
+                part = with_term(part, array, array_at + right * seg.a * (high - low) // 4)
+            segments += part
+        return segments
+
+    def stage(parts, tokens, micros, sums=(), z=()):
+        outs = [sum((x for x, _ in parts), []), sum((y for _, y in parts), [])] if parts else []
+        send = combine(outs + list(z), tokens, micros, sums)
+        got, at = ((swap(send[0], "mp", 2), swap(send[1], "dp", 1)) if parts else ()), [0, 0]
         places = []
         for x, y in parts:
             places.append(((got[0], at[0]), (got[1], at[1])))
-            at = [at[0] + x[0][2], at[1] + y[0][2]]
-        return send[:2], got, places, send[2] if sums else None
-
-    p_away, stats_got = swap(p_theirs, "mp", 1), swap(stats, "mp", 1)
-    d_mine, d_theirs = call(enc_down_kernel, [(d_seg.shape, BF)] * 2, (pos, rows_at, d_enc, hidden), 30)
-    d_away, p_own = swap(d_theirs, "mp", 1), (p_mine, p_away)
-    send, p_arrived, p_got, stats = stage([first(p_own, p_seg)], [d_theirs], 30, (stats, stats_got))
-    (predicted,) = gate([predicted], send)
-    d_own, p_got = (d_mine, d_away), p_got[0]
-    stats_got, predicted_x = swap(stats, "dp", 2), swap(predicted, "mp", 2)
-    u_mine, u_theirs, grad_mid, d_gain_two = call(
+            at = [at[0] + sum(p[0][2] for p in x), at[1] + sum(p[0][2] for p in y)]
+        return send, got, places
+
+    p_away = swap(p_theirs, "mp", 1)
+    d_mine, *d_theirs = call(enc_down_kernel, [(d_seg.shape, BF)] + d_seg.parts(), (pos, rows_at, d_enc, hidden), 30)
+    p_own, d_own = (p_mine, [p_away]), (d_mine, from_core(d_theirs))
+    send, p_arrived, (p_got, d_got, at_predicted) = stage(
+        [first(p_own, p_seg), first(d_own, d_seg), ([[(predicted, 0, predicted.shape[0])]], [])], [], 30
+    )
+    grad_mid, d_gain_two, u_mine, *u_theirs = call(
         enc_up_kernel,
-        [(u_seg.shape, BF), (u_seg.shape, BF), ((length, width), F32), ((1, width), F32)],
+        [((length, width), F32), ((1, width), F32), (u_seg.shape, BF)] + u_seg.parts(),
         (pos, rows_at, d_enc, middle, row(gain_mlp), slope) + up + down, 100, tokens=send,
     )
-    u_away = swap(u_theirs, "mp", 1)
-    predicted_x, d_away = gate([predicted_x, d_away], [u_theirs])
-    d_own = (d_mine, d_away)
-    send, d_arrived, (d_got, p_then), stats = stage(
-        [first(d_own, d_seg), second(p_own, p_seg, p_got)], [u_theirs], 30, (stats, stats_got)
-    )
-    predicted, predicted_x = gate([predicted, predicted_x], send)
-    stats_got, predicted_c, predicted_xc = swap(stats, "dp", dp_size // 2), swap(predicted, "mp", 1), swap(predicted_x, "mp", 1)
-    a_mine, a_theirs, d_input = call(
+    u_away = from_core(u_theirs)
+    d_qkv, d_input, d_gain_one = call(
         enc_attn_back_kernel,
-        [(a_seg.shape, BF), (a_seg.shape, BF), ((x_blocks * length, 128), BF)],
-        (pos, rows_at, x, row(gain_attn), grad_mid, qkv, probs, mixed, d_embedded, enc, d_gain_two, small_rows_at, p_d_gains)
-        + attn, 100,
-        [((2, 4 * cols, width), BF), ((width, length), BF), ((3 * width, length), BF)], tokens=send,
-    )
-
-    a_away = swap(a_theirs, "mp", 1)
-    u_away, predicted_c, predicted_xc = gate([u_away, predicted_c, predicted_xc], [a_theirs])
-    u_own, a_own = (u_mine, u_away), (a_mine, a_away)
-    ud_send, _, (u_got, d_then), stats = stage(
-        [first(u_own, u_seg), second(d_own, d_seg, d_got)], [a_theirs, predicted_c, predicted_xc], 60, (stats, stats_got)
-    )
-    (p_kept,) = combine([kept(p_own, p_seg, p_got, p_then)], ud_send, 30)
+        [((3 * width, length), BF), ((x_blocks * length, 128), BF), ((1, width), F32)],
+        (pos, x, row(gain_attn), grad_mid, qkv, probs) + attn, 1,
+        [((2, 4 * cols, width), BF), ((width, length), BF)],
+    )
+    got_x, got_y, *u_away[:2] = gate([*p_arrived, *u_away[:2]], [d_gain_one])
+    moved = lambda places: ((got_x, places[0][1]), (got_y, places[1][1]))
+    p_got, d_got, u_own = moved(p_got), moved(d_got), (u_mine, u_away)
+    predicted_x = lax.slice_in_dim(got_x, at_predicted[0][1], got_x.shape[0])
+    filler = [[(d_input, 0, p_seg.b - p_seg.a)]]
+    send, _, (u_got, d_then, p_then, _) = stage(
+        [first(u_own, u_seg), second(d_own, d_seg, d_got), second(p_own, p_seg, p_got), ([], filler)], [], 30
+    )
+    predicted, predicted_x, d_input = gate([predicted, predicted_x, d_input], send)
+    a_mine, *a_theirs = call(
+        enc_attn_weights_kernel, [(a_seg.shape, BF)] + a_seg.parts(),
+        (pos, rows_at, x, row(gain_attn), grad_mid, mixed, d_qkv, d_embedded, enc, d_gain_one, d_gain_two, p_d_gains), 100, tokens=send,
+    )
+    a_own = (a_mine, from_core(a_theirs))
+    a_send, _, (a_got,) = stage([first(a_own, a_seg)], [], 0)
+    p_z = (p_own, p_seg, p_got, p_then)
+    d_z = (d_own, d_seg, d_got, d_then)
+    (*u_send, z_send), _, (u_then,) = stage(
+        [second(u_own, u_seg, u_got)], a_send, 3, (), [kept(*p_z, 2, 4) + kept(*d_z, 2, 4)]
+    )
+    (stats,) = gate([stats], u_send)
+    u_z = (u_own, u_seg, u_got, u_then)
+    stats_got, z_got = swap(stats, "mp", 1), swap(z_send, "dp", 2)
+    p_rows, d_rows, u_rows = ((seg.a + seg.b) // 4 for seg in (p_seg, d_seg, u_seg))
+    p_one, d_one = (z_got, 0), (z_got, 2 * p_rows)
+
+    def later(one, seg, quarter):
+        array, at = one
+        return [(array, at + quarter * seg.a // 4), (array, at + seg.a // 2 + quarter * seg.b // 4)]
+
+    def last(z, one, quarter, two=None):
+        own, seg, got, then = z
+        segments = []
+        lefts_rights = later(one, seg, quarter)
+        for part, (start, size), over, after, (array, at), shift in (
+            (0, seg.keep_left, got[0], then[1], lefts_rights[0], 0), (1, seg.keep_right, got[1], then[0], lefts_rights[1], seg.a // 4)
+        ):
+            begin, rows = quarter * size // 4, size // 4
+            terms = both(own, start + begin, rows)
+            for more, more_at in (over, after):
+                terms = with_term(terms, more, more_at + begin)
+            terms = with_term(terms, array, at)
+            if two is not None:
+                terms = with_term(terms, two[0], two[1] + shift)
+            segments += terms
+        return segments
+
+    (*a_send, z_send, stats), _, (a_then,) = stage(
+        [second(a_own, a_seg, a_got)], u_send, 3, (stats, stats_got), [last(p_z, p_one, 1) + last(d_z, d_one, 1)]
+    )
+    a_z = (a_own, a_seg, a_got, a_then)
+    z_got = swap(z_send, "dp", 4)
+    (z_send,) = combine([kept(*u_z, 2, 4)], a_send, 3)
+    u_one, stats_got = (swap(z_send, "dp", 2), 0), swap(stats, "dp", 2)
+    predicted, predicted_x = gate([predicted, predicted_x], [z_send])
+    predicted_c, predicted_xc = swap(predicted, "mp", 1), swap(predicted_x, "mp", 1)
+    z_send, z_send_u, stats = combine([kept(*a_z, 2, 4), last(u_z, u_one, 1)], [z_send], 3, (stats, stats_got))
+    a_one, u_two = (swap(z_send, "dp", 2), 0), (swap(z_send_u, "dp", 4), 0)
+    d_input, stats, p_two_array = gate([d_input, stats, z_got], [z_send])
+    p_two, d_two = (p_two_array, 0), (p_two_array, p_rows)
+    stats_got, input_x, input_c = swap(stats, "dp", 4), swap(d_input, "mp", 2), swap(d_input, "mp", 1)
+    p_sum, d_sum = combine([last(p_z, p_one, 0, p_two), last(d_z, d_one, 0, d_two)], [z_send], 3, kind=F32)
     (predictions,) = call(
-        in_order_kernel, [((SHARDS, length, channels), BF)], (pos, predicted, predicted_c, predicted_x, predicted_xc), 30,
-        tokens=[p_kept],
-    )
-    stats_got = swap(stats, "mp", 2)
-    a_send, _, (a_got,), _ = stage([first(a_own, a_seg)], [*ud_send, predictions], 1)
-    p_parts = send_last(p_kept, p_seg)
-    u_send, _, (u_then,), stats = stage([second(u_own, u_seg, u_got)], a_send, 1, (stats, stats_got))
-    (d_kept,) = combine([kept(d_own, d_seg, d_got, d_then)], u_send, 1)
-    p_parts, d_input = gate([p_parts, d_input], u_send)
+        in_order_kernel, [((SHARDS, length, channels), BF)], (pos, predicted, predicted_c, predicted_x, predicted_xc), 3,
+        tokens=(p_sum,),
+    )
+    z_send, stats = combine([last(a_z, a_one, 1)], [predictions], 3, (stats, stats_got))
+    a_two = (swap(z_send, "dp", 4), 0)
+    (input_x,) = gate([input_x], [z_send])
+    u_sum, stats = combine([last(u_z, u_one, 0, u_two)], [z_send], 3, (stats, swap(stats, "mp", 2)), kind=F32)
     stats_got = swap(stats, "dp", 1)
-    d_parts = send_last(d_kept, d_seg)
-    r_pred = summed(p_parts)
-    a_send, _, (a_then,), stats = stage([second(a_own, a_seg, a_got)], [*u_send, r_pred], 1, (stats, stats_got))
-    input_x, input_c = swap(d_input, "mp", 2), swap(d_input, "mp", 1)
-    (u_kept,) = combine([kept(u_own, u_seg, u_got, u_then)], a_send, 1)
-    (d_parts,) = gate([d_parts], a_send)
-    for at in range(2, dp_size.bit_length() - 2):
-        stats = stats + swap(stats, "dp", 1 << at)
-    u_parts = send_last(u_kept, u_seg)
-    r_down = summed(d_parts)
-    (a_kept,) = combine([kept(a_own, a_seg, a_got, a_then)], [u_kept], 1)
-    a_parts = send_last(a_kept, a_seg)
     (patches_grad,) = call(
         in_order_kernel, [((SHARDS, length, width), BF)], (pos, d_input, input_c, input_x, swap(input_x, "mp", 1)), 2,
-    )
-    r_up, r_attn = summed(u_parts), summed(a_parts)
+        tokens=(u_sum,),
+    )
+    a_sum, stats = combine([last(a_z, a_one, 0, a_two)], [patches_grad], 3, (stats, stats_got), kind=F32)
+    for at in range(3, dp_size.bit_length() - 1):
+        stats = stats + swap(stats, "dp", 1 << at)
+
+    def own_rows(total, seg):
+        total = total.reshape(seg.left + seg.right, -1, 128)
+        if dp_size > 8:
+            groups = [[high * 8 + low for high in range(dp_size // 8)] for low in range(8)]
+            total = lax.psum_scatter(total, "dp", scatter_dimension=1, axis_index_groups=groups, tiled=True)
+        return jnp.swapaxes(total, 0, 1).reshape(total.shape[1], -1)
+
+    r_pred, r_down, r_up, r_attn = (
+        own_rows(total, seg) for total, seg in ((p_sum, p_seg), (d_sum, d_seg), (u_sum, u_seg), (a_sum, a_seg))
+    )
 
     count = dp_size * patches.shape[0] * length
     mean, square = stats[0] / count, stats[1] / count

time: 280 us -> 268 us (0.957)
  starting transfers between devices: 53.8 us -> 39.9 us
  local copies, waits for them, and re-layouts: 51 us -> 39.6 us
  waiting for transfers between devices: 64.4 us -> 74.4 us
  Pallas kernels: 101 us -> 106 us
  other arithmetic: 6.1 us -> 2.29 us
    all_to_all x4 -> x0, starting transfers between devices: 18.6 us -> none  [send_last(): lax.all_to_all(jnp.swapaxes(kept, 0, 1), 'dp', 0, 0, axis_index_groups=gr...]
    ppermute x45 -> x54, waiting for transfers between devices: 57.8 us -> 74.4 us  [swap(): return lax.ppermute(value, axis, [(i, i ^ bit) for i in range(size)])]
    unnamed x179 -> x191, local copies, waits for them, and re-layouts: 36.8 us -> 29.9 us
    all_to_all x4 -> x0, waiting for transfers between devices: 6.53 us -> none  [send_last(): lax.all_to_all(jnp.swapaxes(kept, 0, 1), 'dp', 0, 0, axis_index_groups=gr...]
    ppermute x45 -> x54, starting transfers between devices: 35.2 us -> 39.9 us  [swap(): return lax.ppermute(value, axis, [(i, i ^ bit) for i in range(size)])]
    pallas_call x11 -> x12, Pallas kernels: 78.2 us -> 82.3 us  [call(): pl.pallas_call(lambda *refs: kernel(*refs[:n_args], *refs[n_all:]), out_s...]
    reshape x10 -> x4, local copies, waits for them, and re-layouts: 4.63 us -> 0.66 us  [own_rows(): total = total.reshape(seg.left + seg.right, -1, 128)]
    reduce_sum x4 -> x0, other arithmetic: 3.53 us -> none  [summed(): total = jnp.sum(parts.astype(F32), 0)]
  transfers between devices with their start and end apart: 49 -> 54, of which waited for: 11 -> 18; matrix products, arithmetic and copies ran while one was open for 6% -> 4% of each run, Pallas kernels for 27% -> 31%
where the time goes in v2:
time: 268 us; the launch traced here: 264 us
  Pallas kernels  106 us (40%)
  waiting for transfers between devices  74.4 us (28%)
  starting transfers between devices  39.9 us (15%)
  local copies, waits for them, and re-layouts  39.6 us (15%)
    pallas_call x12, Pallas kernels, call(): pl.pallas_call(lambda *refs: kernel(*refs[:n_args], *refs[n_all:]), out_s...  82.3 us
    ppermute x54, waiting for transfers between devices, swap(): return lax.ppermute(value, axis, [(i, i ^ bit) for i in range(size)])  74.4 us
    ppermute x54, starting transfers between devices, swap(): return lax.ppermute(value, axis, [(i, i ^ bit) for i in range(size)])  39.9 us
    unnamed x191, local copies, waits for them, and re-layouts  29.9 us
    pallas_call x11, Pallas kernels, combine(): pl.pallas_call(kernel, out_shape=[jax.ShapeDtypeStruct((size, 128), kind)...  23.8 us
  transfers between devices with their start and end apart: 54, of which 18 were waited for; matrix products, arithmetic and copies ran while one was open for 4% of the time, Pallas kernels for 31%

profile of v2, /device:TPU:0, one launch (start us, length us, event | category | flops | bytes accessed | tf_op | source)
XLA Modules:
  0.0 264.2 jit_solution(13902389597601653835)
XLA Ops:
  3.0 1.7 shard_map.305
  4.8 2.9 %collective-permute-start.1 = (bf16[384,768]{1,0:T(8,128)(2,1)S(1)}, bf16[384,768]{1,0:T(8,128)(2,1)S(1)}, u32[]{:S(2)}, u32[]{:S(2)}) collective-permute-start(bf16[384,768]{1,0:T(8,128)(2,1)S(1)} %get-tuple-element.91.refs_8_), channel_id=1, source_target_pairs={{0,2},{1,3},{2,0},{3,1},{4,6},{5,7},{6,4},{7,5},{8,10},{9,11},{10,... | collective-permute-start | bytes 1769480 | tf_op jit(solution)/shard_map/ppermute | solution.py:516
  10.3 10.7 %collective-permute-done.1.refs_0_ = bf16[384,768]{1,0:T(8,128)(2,1)S(1)} collective-permute-done((bf16[384,768]{1,0:T(8,128)(2,1)S(1)}, bf16[384,768]{1,0:T(8,128)(2,1)S(1)}, u32[]{:S(2)}, u32[]{:S(2)}) %collective-permute-start.1) | collective-permute-done | bytes 589856 | tf_op jit(solution)/shard_map/ppermute | solution.py:516
  21.8 1.8 collective-permute-start.2
  25.1 11.6 %collective-permute-done.2.refs_8_.refs_9_ = bf16[384,768]{1,0:T(8,128)(2,1)} collective-permute-done((bf16[384,768]{1,0:T(8,128)(2,1)}, bf16[384,768]{1,0:T(8,128)(2,1)}, u32[]{:S(2)}, u32[]{:S(2)}) %collective-permute-start.2) | collective-permute-done | bytes 589856 | tf_op jit(solution)/shard_map/ppermute | solution.py:516
  41.5 9.6 %shard_map.308 = (f32[256,768]{1,0:T(8,128)S(1)}, bf16[2304,256]{1,0:T(8,128)(2,1)S(1)}, bf16[12,256,256]{2,1,0:T(8,128)(2,1)}, bf16[768,256]{1,0:T(8,128)(2,1)S(1)}) custom-call(s32[4]{0:T(128)S(1)} %pad_add_fusion.refs_0_, bf16[256,768]{1,0:T(8,128)(2,1)S(1)} %copy-done.11, s32[1,256]{1,0:T(1,128)S(1)} %constant_dynamic-slice_fusion.3.refs_2_, ...), custom_call_target="tpu_custom_call" | custom-call | flops 10350000128 | bytes 9049104 | tf_op jit(solution)/shard_map/pallas_call | solution.py:130
  52.7 3.1 %collective-permute-done.7.refs_0_ = bf16[768,384]{1,0:T(8,128)(2,1)} collective-permute-done((bf16[768,384]{1,0:T(8,128)(2,1)}, bf16[768,384]{1,0:T(8,128)(2,1)}, u32[]{:S(2)}, u32[]{:S(2)}) %collective-permute-start.7) | collective-permute-done | bytes 589856 | tf_op jit(solution)/shard_map/ppermute | solution.py:516
  60.7 6.1 %shard_map.310 = (bf16[256,3072]{1,0:T(8,128)(2,1)}, bf16[256,3072]{1,0:T(8,128)(2,1)}) custom-call(s32[4]{0:T(128)S(1)} %pad_add_fusion.refs_0_, f32[256,768]{1,0:T(8,128)S(1)} %copy-done.26, f32[1,768]{1,0:T(1,128)S(1)} %reshape.183.refs_2_.refs_4_, bf16[768,768]{1,0:T(8,128)(2,1)S(1)} %copy-done.53, ...), custom_call_target="tpu_custom_call" | custom-call | flops 6899999744 | bytes 8653840 | tf_op jit(solution)/shard_map/pallas_call | solution.py:130
  66.8 6.9 %collective-permute-done.12.refs_0_ = bf16[384,768]{1,0:T(8,128)(2,1)} collective-permute-done((bf16[384,768]{1,0:T(8,128)(2,1)}, bf16[384,768]{1,0:T(8,128)(2,1)}, u32[]{:S(2)}, u32[]{:S(2)}) %collective-permute-start.12) | collective-permute-done | bytes 589856 | tf_op jit(solution)/shard_map/ppermute | solution.py:516
  73.8 7.7 %collective-permute-done.16.refs_12_ = bf16[1344,384]{1,0:T(8,128)(2,1)} collective-permute-done((bf16[1344,384]{1,0:T(8,128)(2,1)}, bf16[1344,384]{1,0:T(8,128)(2,1)}, u32[]{:S(2)}, u32[]{:S(2)}) %collective-permute-start.16) | collective-permute-done | bytes 1032224 | tf_op jit(solution)/shard_map/ppermute | solution.py:516
  85.3 4.0 %shard_map.313.refs_1_.refs_8_ = bf16[256,768]{1,0:T(8,128)(2,1)S(1)} custom-call(s32[4]{0:T(128)S(1)} %pad_add_fusion.refs_0_, f32[256,768]{1,0:T(8,128)S(1)} %copy-done.26, bf16[256,3072]{1,0:T(8,128)(2,1)} %get-tuple-element.97.refs_1_.refs_2_.refs_3_, bf16[768,768]{1,0:T(8,128)(2,1)S(1)} %copy-done.55, ...), custom_call_target="tpu_custom_call" | custom-call | flops 4600000000 | bytes 7471120 | tf_op jit(solution)/shard_map/pallas_call | solution.py:130
  89.4 20.5 %shard_map.315 = (bf16[768,128]{1,0:T(8,128)(2,1)S(1)}, f32[8,384]{1,0:T(8,128)S(1)}, bf16[6912,128]{1,0:T(8,128)(2,1)}, bf16[6912,128]{1,0:T(8,128)(2,1)}, bf16...) custom-call(s32[4]{0:T(128)S(1)} %pad_add_fusion.refs_0_, ...), custom_call_target="tpu_custom_call" | custom-call | flops 34500001792 | bytes 9470992 | tf_op jit(solution)/shard_map/pallas_call | solution.py:130
  111.1 4.4 %shard_map.316 = (bf16[9216,128]{1,0:T(8,128)(2,1)}, bf16[2304,128]{1,0:T(8,128)(2,1)S(1)}, bf16[2304,128]{1,0:T(8,128)(2,1)S(1)}, bf16[4608,128]{1,0:T(8,128)(2,1)}) custom-call(s32[4]{0:T(128)S(1)} %pad_add_fusion.refs_0_, s32[768,1]{1,0:T(8,128)S(1)} %copy-done.31, f32[256,768]{1,0:T(8,128)S(1)} %get-tuple-element.102.refs_2_, ...), custom_call_target="tpu_custom_call" | custom-call | flops 34500001792 | bytes 7080976 | tf_op jit(solution)/shard_map/pallas_call | solution.py:130
  120.6 2.5 shard_map.317
  125.3 13.5 %shard_map.318 = (f32[256,768]{1,0:T(8,128)}, f32[1,768]{1,0:T(1,128)S(1)}, bf16[9216,128]{1,0:T(8,128)(2,1)}, bf16[2304,128]{1,0:T(8,128)(2,1)S(1)}, bf16[2304,...) custom-call(s32[4]{0:T(128)S(1)} %pad_add_fusion.refs_0_, s32[768,1]{1,0:T(8,128)S(1)} %copy-done.31, ...), custom_call_target="tpu_custom_call" | custom-call | flops 115000000512 | bytes 18097168 | tf_op jit(solution)/shard_map/pallas_call | solution.py:130
  140.4 10.8 %shard_map.319 = (bf16[2304,256]{1,0:T(8,128)(2,1)S(1)}, bf16[1536,128]{1,0:T(8,128)(2,1)S(1)}, f32[1,768]{1,0:T(1,128)S(1)}) custom-call(s32[4]{0:T(128)S(1)} %pad_add_fusion.refs_0_, bf16[256,768]{1,0:T(8,128)(2,1)S(1)} %copy-done.12, f32[1,768]{1,0:T(1,128)S(1)} %copy-done.49, f32[256,768]{1,0:T(8,128)S(1)} %copy-done.27, bf16[2304,256]{1,0:T(8,128)(2,1)} %copy-done.15, ...), custom_call_target="tpu_custom_call" | custom-call | flops 1150000000 | bytes 10229776 | tf_op jit(solution)/shard_map/pallas_call | solution.py:130
  154.4 3.0 %shard_map.321 = (bf16[4416,128]{1,0:T(8,128)(2,1)S(1)}, bf16[4416,128]{1,0:T(8,128)(2,1)S(1)}) custom-call(bf16[9216,128]{1,0:T(8,128)(2,1)} %get-tuple-element.117.refs_0_.refs_8_.refs_2_, bf16[2304,128]{1,0:T(8,128)(2,1)} %get-tuple-element.118.refs_1_, bf16[9216,128]{1,0:T(8,128)(2,1)} %get-tuple-element.103.refs_2_.refs_8_.refs_13_, ...), custom_call_target="tpu_custom_call" | custom-call | flops 34500001792 | bytes 7766016 | tf_op jit(solution)/shard_map/pallas_call | solution.py:236
  159.5 6.3 %shard_map.323 = (bf16[10752,128]{1,0:T(8,128)(2,1)}, bf16[2304,128]{1,0:T(8,128)(2,1)S(1)}, bf16[3072,128]{1,0:T(8,128)(2,1)S(1)}, bf16[5376,128]{1,0:T(8,128)(2,1)}) custom-call(s32[4]{0:T(128)S(1)} %pad_add_fusion.refs_0_, s32[768,1]{1,0:T(8,128)S(1)} %copy-done.32, bf16[256,768]{1,0:T(8,128)(2,1)S(1)} %copy-done.12, f32[1,768]{1,0:T(1,128)S(1)} %copy-done.49, ...), custom_call_target="tpu_custom_call" | custom-call | flops 115000000512 | bytes 8871952 | tf_op jit(solution)/shard_map/pallas_call | solution.py:130
  169.8 2.9 %shard_map.324 = (bf16[2304,128]{1,0:T(8,128)(2,1)}, bf16[3072,128]{1,0:T(8,128)(2,1)S(1)}) custom-call(bf16[10752,128]{1,0:T(8,128)(2,1)} %get-tuple-element.132.refs_0_.refs_2_, bf16[2304,128]{1,0:T(8,128)(2,1)} %copy-done.83, bf16[3072,128]{1,0:T(8,128)(2,1)} %copy-done.80), custom_call_target="tpu_custom_call" | custom-call | tf_op jit(solution)/shard_map/pallas_call | solution.py:236
  174.9 10.3 %collective-permute-done.27.refs_3_.refs_12_.refs_2_.refs_10_.refs_7_.refs_4_ = bf16[4416,128]{1,0:T(8,128)(2,1)S(1)} collective-permute-done((bf16[4416,128]{1,0:T(8,128)(2,1)S(1)}, bf16[4416,128]{1,0:T(8,128)(2,1)S(1)}, u32[]{:S(2)}, u32[]{:S(2)}) %collective-permute-start.27) | collective-permute-done | bytes 1130528 | tf_op jit(solution)/shard_map/ppermute | solution.py:516
  187.8 2.3 shard_map.325
  197.3 6.4 %collective-permute-done.35.refs_4_.refs_6_.refs_7_.refs_8_ = bf16[3072,128]{1,0:T(8,128)(2,1)} collective-permute-done((bf16[3072,128]{1,0:T(8,128)(2,1)S(1)}, bf16[3072,128]{1,0:T(8,128)(2,1)}, u32[]{:S(2)}, u32[]{:S(2)}) %collective-permute-start.35) | collective-permute-done | bytes 786464 | tf_op jit(solution)/shard_map/ppermute | solution.py:516
  207.1 2.9 %shard_map.327 = (bf16[1536,128]{1,0:T(8,128)(2,1)}, bf16[1152,128]{1,0:T(8,128)(2,1)S(1)}, bf16[1008,128]{1,0:T(8,128)(2,1)S(1)}, f32[8,384]{1,0:T(8,128)S(1)}) custom-call(f32[8,384]{1,0:T(8,128)S(1)} %copy-done.45, f32[8,384]{1,0:T(8,128)S(1)} %collective-permute-done.33.refs_1_, bf16[10752,128]{1,0:T(8,128)(2,1)} %get-tuple-element.132.refs_0_.refs_2_, ...), custom_call_target="tpu_custom_call" | custom-call | flops 3449999872 | bytes 4300800 | tf_op jit(solution)/shard_map/pallas_call | solution.py:236
  218.1 2.6 collective-permute-start.44
  223.8 2.5 shard_map.330
  227.5 2.2 collective-permute-done.44.refs_2_
  232.3 1.7 shard_map.332
  237.0 2.4 collective-permute-start.51
  239.5 2.0 shard_map.333.refs_9_
  246.4 2.4 collective-permute-start.53
  251.8 2.5 shard_map.337.refs_10_
  254.3 3.5 %collective-permute-done.53.refs_7_ = bf16[672,128]{1,0:T(8,128)(2,1)S(1)} collective-permute-done((bf16[672,128]{1,0:T(8,128)(2,1)S(1)}, bf16[672,128]{1,0:T(8,128)(2,1)S(1)}, u32[]{:S(2)}, u32[]{:S(2)}) %collective-permute-start.53) | collective-permute-done | bytes 172064 | tf_op jit(solution)/shard_map/ppermute | solution.py:516
  (336 shorter events, 88.3 us)
Async XLA Ops:
  4.8 16.3 %collective-permute-start.1 = (bf16[384,768]{1,0:T(8,128)(2,1)S(1)}, bf16[384,768]{1,0:T(8,128)(2,1)S(1)}, u32[]{:S(2)}, u32[]{:S(2)}) collective-permute-start(bf16[384,768]{1,0:T(8,128)(2,1)S(1)} %get-tuple-element.91.refs_8_), channel_id=1, source_target_pairs={{0,2},{1,3},{2,0},{3,1},{4,6},{5,7},{6,4},{7,5},{8,10},{9,11},{10,... | collective-permute-start | bytes 1769480 | tf_op jit(solution)/shard_map/ppermute | solution.py:516
  7.7 30.6 %collective-permute-start = (bf16[768,768]{1,0:T(8,128)(2,1)}, bf16[768,768]{1,0:T(8,128)(2,1)}, u32[]{:S(2)}, u32[]{:S(2)}) collective-permute-start(bf16[768,768]{1,0:T(8,128)(2,1)} %get-tuple-element.90.refs_5_.refs_6_), channel_id=1, source_target_pairs={{0,1},{1,0},{2,3},{3,2},{4,5},{5,4},{6,7},{7,6},{8,9},{9,8},{10,11... | collective-permute-start | bytes 3538952 | tf_op jit(solution)/shard_map/ppermute | solution.py:516
  21.8 14.8 %collective-permute-start.2 = (bf16[384,768]{1,0:T(8,128)(2,1)}, bf16[384,768]{1,0:T(8,128)(2,1)}, u32[]{:S(2)}, u32[]{:S(2)}) collective-permute-start(bf16[384,768]{1,0:T(8,128)(2,1)} %get-tuple-element.94.refs_7_.refs_8_), channel_id=1, source_target_pairs={{0,4},{4,0},{8,12},{12,8},{16,20},{20,16},{24,28},{28,24},{1,5},{5... | collective-permute-start | bytes 1769480 | tf_op jit(solution)/shard_map/ppermute | solution.py:516
  23.6 14.6 %collective-permute-start.6 = (bf16[768,384]{1,0:T(8,128)(2,1)}, bf16[768,384]{1,0:T(8,128)(2,1)}, u32[]{:S(2)}, u32[]{:S(2)}) collective-permute-start(bf16[768,384]{1,0:T(8,128)(2,1)} %get-tuple-element.96), channel_id=1, source_target_pairs={{0,2},{1,3},{2,0},{3,1},{4,6},{5,7},{6,4},{7,5},{8,10},{9,11},{10,... | collective-permute-start | bytes 1769480 | tf_op jit(solution)/shard_map/ppermute | solution.py:516
  25.1 14.7 %collective-permute-start.3 = (bf16[384,768]{1,0:T(8,128)(2,1)}, bf16[384,768]{1,0:T(8,128)(2,1)}, u32[]{:S(2)}, u32[]{:S(2)}) collective-permute-start(bf16[384,768]{1,0:T(8,128)(2,1)} %get-tuple-element.94.refs_7_.refs_8_), channel_id=1, source_target_pairs={{0,1},{1,0},{2,3},{3,2},{4,5},{5,4},{6,7},{7,6},{8,9},{9,8},{10,11... | collective-permute-start | bytes 1769480 | tf_op jit(solution)/shard_map/ppermute | solution.py:516
  36.7 20.9 %collective-permute-start.5 = (bf16[768,768]{1,0:T(8,128)(2,1)}, bf16[768,768]{1,0:T(8,128)(2,1)}, u32[]{:S(2)}, u32[]{:S(2)}) collective-permute-start(bf16[768,768]{1,0:T(8,128)(2,1)} %refs_6_.3), channel_id=1, source_target_pairs={{0,1},{1,0},{2,3},{3,2},{4,5},{5,4},{6,7},{7,6},{8,9},{9,8},{10,11... | collective-permute-start | bytes 3538952 | tf_op jit(solution)/shard_map/ppermute | solution.py:516
  38.2 17.7 %collective-permute-start.15 = (bf16[1344,384]{1,0:T(8,128)(2,1)S(1)}, bf16[1344,384]{1,0:T(8,128)(2,1)}, u32[]{:S(2)}, u32[]{:S(2)}) collective-permute-start(bf16[1344,384]{1,0:T(8,128)(2,1)S(1)} %copy-done.3), channel_id=1, source_target_pairs={{0,1},{1,0},{2,3},{3,2},{4,5},{5,4},{6,7},{7,6},{8,9},{9,8},{10,11... | collective-permute-start | bytes 3096584 | tf_op jit(solution)/shard_map/ppermute | solution.py:516
  38.3 17.6 %collective-permute-start.11 = (bf16[384,768]{1,0:T(8,128)(2,1)}, bf16[384,768]{1,0:T(8,128)(2,1)}, u32[]{:S(2)}, u32[]{:S(2)}) collective-permute-start(bf16[384,768]{1,0:T(8,128)(2,1)} %shard_map.311), channel_id=1, source_target_pairs={{0,2},{1,3},{2,0},{3,1},{4,6},{5,7},{6,4},{7,5},{8,10},{9,11},{10,... | collective-permute-start | bytes 1769480 | tf_op jit(solution)/shard_map/ppermute | solution.py:516
  39.8 18.2 %collective-permute-start.8 = (bf16[768,384]{1,0:T(8,128)(2,1)}, bf16[768,384]{1,0:T(8,128)(2,1)}, u32[]{:S(2)}, u32[]{:S(2)}) collective-permute-start(bf16[768,384]{1,0:T(8,128)(2,1)} %collective-permute-done.6.refs_5_.refs_1_.refs_8_), channel_id=1, source_target_pairs={{0,1},{1,0},{2,3},{3,2},{4,5},{5,4},{6,7},{7,6},{8,9},{9,8},{10,11... | collective-permute-start | bytes 1769480 | tf_op jit(solution)/shard_map/ppermute | solution.py:516
  39.9 15.9 %collective-permute-start.7 = (bf16[768,384]{1,0:T(8,128)(2,1)}, bf16[768,384]{1,0:T(8,128)(2,1)}, u32[]{:S(2)}, u32[]{:S(2)}) collective-permute-start(bf16[768,384]{1,0:T(8,128)(2,1)} %collective-permute-done.6.refs_5_.refs_1_.refs_8_), channel_id=1, source_target_pairs={{0,4},{4,0},{8,12},{12,8},{16,20},{20,16},{24,28},{28,24},{1,5},{5... | collective-permute-start | bytes 1769480 | tf_op jit(solution)/shard_map/ppermute | solution.py:516
  55.9 25.6 %collective-permute-start.16 = (bf16[1344,384]{1,0:T(8,128)(2,1)}, bf16[1344,384]{1,0:T(8,128)(2,1)}, u32[]{:S(2)}, u32[]{:S(2)}) collective-permute-start(bf16[1344,384]{1,0:T(8,128)(2,1)} %shard_map.314.refs_10_), channel_id=1, source_target_pairs={{0,2},{1,3},{2,0},{3,1},{4,6},{5,7},{6,4},{7,5},{8,10},{9,11},{10,... | collective-permute-start | bytes 3096584 | tf_op jit(solution)/shard_map/ppermute | solution.py:516
  56.6 27.4 %collective-permute-start.10 = (bf16[768,768]{1,0:T(8,128)(2,1)}, bf16[768,768]{1,0:T(8,128)(2,1)}, u32[]{:S(2)}, u32[]{:S(2)}) collective-permute-start(bf16[768,768]{1,0:T(8,128)(2,1)} %refs_12_.1), channel_id=1, source_target_pairs={{0,1},{1,0},{2,3},{3,2},{4,5},{5,4},{6,7},{7,6},{8,9},{9,8},{10,11... | collective-permute-start | bytes 3538952 | tf_op jit(solution)/shard_map/ppermute | solution.py:516
  57.6 26.4 %collective-permute-start.13 = (bf16[384,768]{1,0:T(8,128)(2,1)}, bf16[384,768]{1,0:T(8,128)(2,1)}, u32[]{:S(2)}, u32[]{:S(2)}) collective-permute-start(bf16[384,768]{1,0:T(8,128)(2,1)} %collective-permute-done.11.refs_5_.refs_1_.refs_14_), channel_id=1, source_target_pairs={{0,1},{1,0},{2,3},{3,2},{4,5},{5,4},{6,7},{7,6},{8,9},{9,8},{10,11... | collective-permute-start | bytes 1769480 | tf_op jit(solution)/shard_map/ppermute | solution.py:516
  57.9 15.8 %collective-permute-start.12 = (bf16[384,768]{1,0:T(8,128)(2,1)}, bf16[384,768]{1,0:T(8,128)(2,1)}, u32[]{:S(2)}, u32[]{:S(2)}) collective-permute-start(bf16[384,768]{1,0:T(8,128)(2,1)} %collective-permute-done.11.refs_5_.refs_1_.refs_14_), channel_id=1, source_target_pairs={{0,4},{4,0},{8,12},{12,8},{16,20},{20,16},{24,28},{28,24},{1,5},{5... | collective-permute-start | bytes 1769480 | tf_op jit(solution)/shard_map/ppermute | solution.py:516
  116.0 38.3 %collective-permute-start.25 = (bf16[4608,128]{1,0:T(8,128)(2,1)}, bf16[4608,128]{1,0:T(8,128)(2,1)}, u32[]{:S(2)}, u32[]{:S(2)}) collective-permute-start(bf16[4608,128]{1,0:T(8,128)(2,1)} %get-tuple-element.119), channel_id=1, source_target_pairs={{0,1},{1,0},{2,3},{3,2},{4,5},{5,4},{6,7},{7,6},{8,9},{9,8},{10,11... | collective-permute-start | bytes 3538952 | tf_op jit(solution)/shard_map/ppermute | solution.py:516
  123.2 28.8 %collective-permute-start.22 = (bf16[4224,128]{1,0:T(8,128)(2,1)S(1)}, bf16[4224,128]{1,0:T(8,128)(2,1)S(1)}, u32[]{:S(2)}, u32[]{:S(2)}) collective-permute-start(bf16[4224,128]{1,0:T(8,128)(2,1)S(1)} %get-tuple-element.107.refs_19_), channel_id=1, source_target_pairs={{0,4},{4,0},{8,12},{12,8},{16,20},{20,16},{24,28},{28,24},{1,5},{5... | collective-permute-start | bytes 3244040 | tf_op jit(solution)/shard_map/ppermute | solution.py:516
  124.7 27.7 %collective-permute-start.21 = (bf16[4608,128]{1,0:T(8,128)(2,1)S(1)}, bf16[4608,128]{1,0:T(8,128)(2,1)S(1)}, u32[]{:S(2)}, u32[]{:S(2)}) collective-permute-start(bf16[4608,128]{1,0:T(8,128)(2,1)S(1)} %get-tuple-element.106.refs_18_), channel_id=1, source_target_pairs={{0,2},{1,3},{2,0},{3,1},{4,6},{5,7},{6,4},{7,5},{8,10},{9,11},{10,... | collective-permute-start | bytes 3538952 | tf_op jit(solution)/shard_map/ppermute | solution.py:516
  138.8 13.1 %collective-permute-start.23 = (bf16[2304,128]{1,0:T(8,128)(2,1)S(1)}, bf16[2304,128]{1,0:T(8,128)(2,1)S(1)}, u32[]{:S(2)}, u32[]{:S(2)}) collective-permute-start(bf16[2304,128]{1,0:T(8,128)(2,1)S(1)} %get-tuple-element.109), channel_id=1, source_target_pairs={{0,1},{1,0},{2,3},{3,2},{4,5},{5,4},{6,7},{7,6},{8,9},{9,8},{10,11... | collective-permute-start | bytes 1769480 | tf_op jit(solution)/shard_map/ppermute | solution.py:516
  138.8 13.1 %collective-permute-start.24 = (bf16[2304,128]{1,0:T(8,128)(2,1)S(1)}, bf16[2304,128]{1,0:T(8,128)(2,1)S(1)}, u32[]{:S(2)}, u32[]{:S(2)}) collective-permute-start(bf16[2304,128]{1,0:T(8,128)(2,1)S(1)} %get-tuple-element.110), channel_id=1, source_target_pairs={{0,1},{1,0},{2,3},{3,2},{4,5},{5,4},{6,7},{7,6},{8,9},{9,8},{10,11... | collective-permute-start | bytes 1769480 | tf_op jit(solution)/shard_map/ppermute | solution.py:516
  151.8 21.9 %collective-permute-start.26 = (bf16[4608,128]{1,0:T(8,128)(2,1)}, bf16[4608,128]{1,0:T(8,128)(2,1)}, u32[]{:S(2)}, u32[]{:S(2)}) collective-permute-start(bf16[4608,128]{1,0:T(8,128)(2,1)} %get-tuple-element.126), channel_id=1, source_target_pairs={{0,1},{1,0},{2,3},{3,2},{4,5},{5,4},{6,7},{7,6},{8,9},{9,8},{10,11... | collective-permute-start | bytes 3538952 | tf_op jit(solution)/shard_map/ppermute | solution.py:516
  157.4 27.8 %collective-permute-start.27 = (bf16[4416,128]{1,0:T(8,128)(2,1)S(1)}, bf16[4416,128]{1,0:T(8,128)(2,1)S(1)}, u32[]{:S(2)}, u32[]{:S(2)}) collective-permute-start(bf16[4416,128]{1,0:T(8,128)(2,1)S(1)} %get-tuple-element.122.refs_3_.refs_12_), channel_id=1, source_target_pairs={{0,2},{1,3},{2,0},{3,1},{4,6},{5,7},{6,4},{7,5},{8,10},{9,11},{10,... | collective-permute-start | bytes 3391496 | tf_op jit(solution)/shard_map/ppermute | solution.py:516
  158.9 27.8 %collective-permute-start.28 = (bf16[4416,128]{1,0:T(8,128)(2,1)S(1)}, bf16[4416,128]{1,0:T(8,128)(2,1)S(1)}, u32[]{:S(2)}, u32[]{:S(2)}) collective-permute-start(bf16[4416,128]{1,0:T(8,128)(2,1)S(1)} %get-tuple-element.123.refs_4_.refs_13_), channel_id=1, source_target_pairs={{0,4},{4,0},{8,12},{12,8},{16,20},{20,16},{24,28},{28,24},{1,5},{5... | collective-permute-start | bytes 3391496 | tf_op jit(solution)/shard_map/ppermute | solution.py:516
  167.8 27.1 %collective-permute-start.34 = (bf16[5376,128]{1,0:T(8,128)(2,1)}, bf16[5376,128]{1,0:T(8,128)(2,1)}, u32[]{:S(2)}, u32[]{:S(2)}) collective-permute-start(bf16[5376,128]{1,0:T(8,128)(2,1)} %get-tuple-element.140), channel_id=1, source_target_pairs={{0,1},{1,0},{2,3},{3,2},{4,5},{5,4},{6,7},{7,6},{8,9},{9,8},{10,11... | collective-permute-start | bytes 4128776 | tf_op jit(solution)/shard_map/ppermute | solution.py:516
  172.8 24.5 %collective-permute-start.36 = (bf16[2304,128]{1,0:T(8,128)(2,1)}, bf16[2304,128]{1,0:T(8,128)(2,1)}, u32[]{:S(2)}, u32[]{:S(2)}) collective-permute-start(bf16[2304,128]{1,0:T(8,128)(2,1)} %get-tuple-element.135.refs_10_), channel_id=1, source_target_pairs={{0,2},{1,3},{2,0},{3,1},{4,6},{5,7},{6,4},{7,5},{8,10},{9,11},{10,... | collective-permute-start | bytes 1769480 | tf_op jit(solution)/shard_map/ppermute | solution.py:516
  173.7 30.0 %collective-permute-start.35 = (bf16[3072,128]{1,0:T(8,128)(2,1)S(1)}, bf16[3072,128]{1,0:T(8,128)(2,1)}, u32[]{:S(2)}, u32[]{:S(2)}) collective-permute-start(bf16[3072,128]{1,0:T(8,128)(2,1)S(1)} %get-tuple-element.136.refs_11_), channel_id=1, source_target_pairs={{0,4},{4,0},{8,12},{12,8},{16,20},{20,16},{24,28},{28,24},{1,5},{5... | collective-permute-start | bytes 2359304 | tf_op jit(solution)/shard_map/ppermute | solution.py:516
  194.5 16.9 %collective-permute-start.31 = (bf16[1152,128]{1,0:T(8,128)(2,1)}, bf16[1152,128]{1,0:T(8,128)(2,1)S(1)}, u32[]{:S(2)}, u32[]{:S(2)}) collective-permute-start(bf16[1152,128]{1,0:T(8,128)(2,1)} %copy-done.18), channel_id=1, source_target_pairs={{0,4},{4,0},{8,12},{12,8},{16,20},{20,16},{24,28},{28,24},{1,5},{5... | collective-permute-start | bytes 884744 | tf_op jit(solution)/shard_map/ppermute | solution.py:516
  195.0 16.4 %collective-permute-start.32 = (bf16[1152,128]{1,0:T(8,128)(2,1)}, bf16[1152,128]{1,0:T(8,128)(2,1)S(1)}, u32[]{:S(2)}, u32[]{:S(2)}) collective-permute-start(bf16[1152,128]{1,0:T(8,128)(2,1)} %copy-done.16), channel_id=1, source_target_pairs={{0,2},{1,3},{2,0},{3,1},{4,6},{5,7},{6,4},{7,5},{8,10},{9,11},{10,... | collective-permute-start | bytes 884744 | tf_op jit(solution)/shard_map/ppermute | solution.py:516
  210.0 12.8 %collective-permute-start.42 = (bf16[1536,128]{1,0:T(8,128)(2,1)}, bf16[1536,128]{1,0:T(8,128)(2,1)S(1)}, u32[]{:S(2)}, u32[]{:S(2)}) collective-permute-start(bf16[1536,128]{1,0:T(8,128)(2,1)} %get-tuple-element.142.refs_6_), channel_id=1, source_target_pairs={{0,2},{1,3},{2,0},{3,1},{4,6},{5,7},{6,4},{7,5},{8,10},{9,11},{10,... | collective-permute-start | bytes 1179656 | tf_op jit(solution)/shard_map/ppermute | solution.py:516
  222.3 14.1 %collective-permute-start.38 = (bf16[768,128]{1,0:T(8,128)(2,1)}, bf16[768,128]{1,0:T(8,128)(2,1)}, u32[]{:S(2)}, u32[]{:S(2)}) collective-permute-start(bf16[768,128]{1,0:T(8,128)(2,1)} %get-tuple-element.144.refs_1_), channel_id=1, source_target_pairs={{0,1},{1,0},{2,3},{3,2},{4,5},{5,4},{6,7},{7,6},{8,9},{9,8},{10,11... | collective-permute-start | bytes 589832 | tf_op jit(solution)/shard_map/ppermute | solution.py:516
  222.3 14.7 %collective-permute-start.39 = (bf16[768,128]{1,0:T(8,128)(2,1)}, bf16[768,128]{1,0:T(8,128)(2,1)}, u32[]{:S(2)}, u32[]{:S(2)}) collective-permute-start(bf16[768,128]{1,0:T(8,128)(2,1)} %get-tuple-element.145.refs_3_), channel_id=1, source_target_pairs={{0,1},{1,0},{2,3},{3,2},{4,5},{5,4},{6,7},{7,6},{8,9},{9,8},{10,11... | collective-permute-start | bytes 589832 | tf_op jit(solution)/shard_map/ppermute | solution.py:516
  227.0 14.5 %collective-permute-start.48 = (bf16[1344,128]{1,0:T(8,128)(2,1)S(1)}, bf16[1344,128]{1,0:T(8,128)(2,1)}, u32[]{:S(2)}, u32[]{:S(2)}) collective-permute-start(bf16[1344,128]{1,0:T(8,128)(2,1)S(1)} %get-tuple-element.150.refs_3_.refs_10_), channel_id=1, source_target_pairs={{0,8},{4,12},{8,0},{12,4},{16,24},{20,28},{24,16},{28,20},{1,9},{5... | collective-permute-start | bytes 1032200 | tf_op jit(solution)/shard_map/ppermute | solution.py:516
  236.5 15.3 %collective-permute-start.45 = (bf16[1536,128]{1,0:T(8,128)(2,1)S(1)}, bf16[1536,128]{1,0:T(8,128)(2,1)}, u32[]{:S(2)}, u32[]{:S(2)}) collective-permute-start(bf16[1536,128]{1,0:T(8,128)(2,1)S(1)} %copy-done.9), channel_id=1, source_target_pairs={{0,1},{1,0},{2,3},{3,2},{4,5},{5,4},{6,7},{7,6},{8,9},{9,8},{10,11... | collective-permute-start | bytes 1179656 | tf_op jit(solution)/shard_map/ppermute | solution.py:516
  (115 other events, 600.6 us)

commit v3 on v2

--- a/solution.py
+++ b/solution.py
@@ -1,4 +1,5 @@
 import math
+from functools import partial
 
 import jax
 import jax.numpy as jnp
@@ -78,7 +79,7 @@
         mixed_ref[at, :] = nn(qkv_ref[u_at, :], probs).astype(BF)
         return carry
 
-    lax.fori_loop(0, SHARDS * per, one_head, 0, unroll=2)
+    lax.fori_loop(0, SHARDS * per, one_head, 0, unroll=4)
 
 
 def attend_back(qkv_ref, probs_ref, d_mixed_ref, d_qkv_ref, per, head_dim):
@@ -98,14 +99,14 @@
         d_qkv_ref[u_at, :] = nt(d_mixed, low).astype(BF)
         return carry
 
-    lax.fori_loop(0, SHARDS * per, one_head, 0, unroll=2)
+    lax.fori_loop(0, SHARDS * per, one_head, 0, unroll=4)
 
 
 ANYWHERE = pl.BlockSpec(memory_space=pl.ANY)
 
 
-def in_hbm(arrays):
-    return [pltpu.with_memory_space_constraint(a, pltpu.HBM) if n_bytes(a) >= 256 * 1700 else a for a in arrays]
+def in_hbm(arrays, least=256 * 1700):
+    return [pltpu.with_memory_space_constraint(a, pltpu.HBM) if n_bytes(a) >= least else a for a in arrays]
 
 
 def n_bytes(array):
@@ -115,8 +116,8 @@
 ANYWHERE = pl.BlockSpec(memory_space=pl.ANY)
 
 
-def in_hbm(arrays):
-    return [pltpu.with_memory_space_constraint(a, pltpu.HBM) if n_bytes(a) >= 256 * 1700 else a for a in arrays]
+def in_hbm(arrays, least=256 * 1700):
+    return [pltpu.with_memory_space_constraint(a, pltpu.HBM) if n_bytes(a) >= least else a for a in arrays]
 
 
 def n_bytes(array):
@@ -137,7 +138,7 @@
         scratch_shapes=[pltpu.VMEM(shape, kind) for shape, kind in scratch],
         compiler_params=pltpu.CompilerParams(vmem_limit_bytes=VMEM_BYTES),
         cost_estimate=pl.CostEstimate(flops=int(micros * COST), bytes_accessed=moved if micros else 0, transcendentals=0),
-    )(*args, *in_hbm(tokens))
+    )(*args, *in_hbm(tokens, 0))
 
 
 def gate(values, tokens):
@@ -147,7 +148,7 @@
         in_specs=[ANYWHERE] * (len(values) + len(tokens)),
         out_specs=[ANYWHERE] * len(values),
         input_output_aliases={at: at for at in range(len(values))},
-    )(*in_hbm(values), *in_hbm(tokens))
+    )(*in_hbm(values), *in_hbm(tokens, 0))
 
 
 def units(value):
@@ -188,7 +189,7 @@
         return [((size, 128), BF) for size in (self.over_x[1], self.over_y[1], 2 * (self.a + self.b))]
 
 
-def combine(outs, tokens, micros, sums=(), kind=BF):
+def combine(outs, tokens, micros, sums=(), kind=BF, cuts=None):
     arrays, terms = [], []
     for segments in outs:
         for parts in segments:
@@ -199,9 +200,19 @@
     n_sums, n_arrays, n_out, n_terms = len(sums), len(arrays), len(outs), len(terms)
     n_in = n_sums + n_arrays + len(tokens)
     sizes = [sum(parts[0][2] for parts in segments) for segments in outs]
+    shapes = [jax.ShapeDtypeStruct((size, 128), kind) for size in sizes]
+    n_results = n_out
+    if cuts:
+        shapes = []
+        for (rows, cut) in cuts:
+            for first, size, count, is_turned in cut:
+                shape = (count, rows, size) if count > 1 else (size, rows) if is_turned else (rows, size)
+                shapes.append(jax.ShapeDtypeStruct(shape, F32))
+        n_results = len(shapes)
 
     def kernel(*refs):
         held, sem = refs[-1 - n_terms : -1], refs[-1]
+        totals = refs[n_in : n_in + n_out] if not cuts else refs[n_in + n_results + bool(sums) : -1 - n_terms]
         copies = [
             pltpu.make_async_copy(refs[n_sums + which].at[pl.ds(first, size), :], held[at], sem.at[at])
             for at, (which, first, size) in enumerate(terms)
@@ -209,9 +220,9 @@
         for copy in copies:
             copy.start()
         if sums:
-            refs[n_in + n_out][...] = refs[0][...] + refs[1][...]
+            refs[n_in + n_results][...] = refs[0][...] + refs[1][...]
         at = 0
-        for out, segments in zip(refs[n_in:], outs):
+        for out, segments in zip(totals, outs):
             row = 0
             for parts in segments:
                 size = parts[0][2]
@@ -230,19 +241,26 @@
                 lax.fori_loop(0, size // 48, add, 0, unroll=2)
                 at += len(parts)
                 row += size
+        if cuts:
+            results = iter(refs[n_in : n_in + n_results])
+            for out, (rows, cut) in zip(totals, cuts):
+                whole = jnp.concatenate([out[u * rows : (u + 1) * rows, :] for u in range(out.shape[0] // rows)], 1)
+                for value in finals(whole, cut):
+                    next(results)[...] = value
 
     moved = 256 * (sum(t[2] for t in terms) + sum(sizes))
     in_vmem = pl.BlockSpec(memory_space=pltpu.VMEM)
     return pl.pallas_call(
         kernel,
-        out_shape=[jax.ShapeDtypeStruct((size, 128), kind) for size in sizes]
-        + ([jax.ShapeDtypeStruct(sums[0].shape, F32)] if sums else []),
+        out_shape=shapes + ([jax.ShapeDtypeStruct(sums[0].shape, F32)] if sums else []),
         in_specs=[in_vmem] * n_sums + [ANYWHERE] * (n_in - n_sums),
-        out_specs=[in_vmem] * (n_out + (1 if sums else 0)),
-        scratch_shapes=[pltpu.VMEM((size, 128), BF) for _, _, size in terms] + [pltpu.SemaphoreType.DMA((n_terms,))],
+        out_specs=[in_vmem] * (n_results + (1 if sums else 0)),
+        scratch_shapes=[pltpu.VMEM((size, 128), F32) for size in sizes if cuts]
+        + [pltpu.VMEM((size, 128), BF) for _, _, size in terms]
+        + [pltpu.SemaphoreType.DMA((n_terms,))],
         compiler_params=pltpu.CompilerParams(vmem_limit_bytes=VMEM_BYTES),
         cost_estimate=pl.CostEstimate(flops=int(micros * COST), bytes_accessed=moved if micros else 0, transcendentals=0),
-    )(*sums, *in_hbm(arrays), *in_hbm(tokens))
+    )(*sums, *in_hbm(arrays), *in_hbm(tokens, 0))
 
 
 def pack_attn_kernel(pos, qkv, out, own, direct):
@@ -393,13 +411,14 @@
     d_enc[...] = nn(d_low, w_embed[...])
 
 
-def enc_down_kernel(pos, rows_at, grad, hidden, mine, *theirs):
+def enc_down_kernel(first, pos, rows_at, grad, hidden, *homes):
     width = hidden.shape[1] // SHARDS
     segments = Segments(grad.shape[1], width)
     grad_turned = turned(rows_at[...], grad[...].astype(BF))
-    for shard, (home, at) in ((1, (theirs, 0)), (3, (theirs, 1)), (0, ((mine,), 0)), (2, ((mine,), 1))):
+    for at in range(2):
+        shard = first + 2 * at
         for block, value in enumerate(units(nn(grad_turned, hidden[:, shard * width : (shard + 1) * width]))):
-            segments.put(home, at, block, value)
+            segments.put(homes, at, block, value)
 
 
 def enc_up_kernel(pos, rows_at, grad, middle, gain, slope, *refs):
@@ -520,6 +539,14 @@
     return lax.dynamic_index_in_dim(value, index, axis, keepdims=False)
 
 
+def finals(total, cuts):
+    results = []
+    for first, size, count, is_turned in cuts:
+        parts = [total[:, first + at * size : first + (at + 1) * size] for at in range(count)]
+        results.append(jnp.stack(parts) if count > 1 else parts[0].T if is_turned else parts[0])
+    return results
+
+
 def source_rows(width):
     size = lax.axis_size("dp")
     number = jnp.arange(8, dtype=jnp.int32)
@@ -595,6 +622,7 @@
     (down_y,) = gate([down_y], [hidden])
     down = (down_weight, down_core, down_x, down_y, swap(down_x, "mp", 1), swap(down_y, "mp", 1))
     (enc,) = call(enc_down_forward_kernel, [((length, width), BF)], (pos, middle, hidden) + down, 4)
+    (p_x,) = gate([p_x], [enc])
     p_packs = (p_send, p_core, p_x, swap(p_x, "mp", 1))
     p_seg, d_seg = Segments(channels, 4 * p_cols + 2 * p_hid), Segments(width, hid)
     u_seg, a_seg = Segments(width, hid), Segments(width, 4 * cols + 128)
@@ -611,6 +639,25 @@
          ((3 * channels, length), BF)],
     )
 
+    p_cuts = [(0, p_cols, 3, False), (3 * p_cols, p_cols, 1, True), (4 * p_cols, p_hid, 1, False), (4 * p_cols + p_hid, p_hid, 1, True)]
+    d_cuts, u_cuts = [(0, hid, 1, True)], [(0, hid, 1, False)]
+    a_cuts = [(0, cols, 3, False), (3 * cols, cols, 1, True), (4 * cols, p_cols, 1, False), (4 * cols + p_cols, 128 - p_cols, 1, True)]
+    small = dp_size == 8
+
+    def sums_of(pieces, tokens, micros, sums=()):
+        outs = [segments for segments, _, _ in pieces]
+        if small:
+            cuts = [(seg.eighth, cut) for _, seg, cut in pieces]
+            return combine(outs, tokens, micros, sums, kind=F32, cuts=cuts)
+        totals = combine(outs, tokens, micros, sums, kind=F32)
+        groups = [[high * 8 + low for high in range(dp_size // 8)] for low in range(8)]
+        results = []
+        for total, (_, seg, cut) in zip(totals, pieces):
+            total = total.reshape(seg.left + seg.right, -1, 128)
+            total = lax.psum_scatter(total, "dp", scatter_dimension=1, axis_index_groups=groups, tiled=True)
+            results += finals(jnp.swapaxes(total, 0, 1).reshape(total.shape[1], -1), cut)
+        return results + list(totals[len(pieces) :])
+
     def from_core(theirs):
         return [swap(part, "mp", 1) for part in theirs]
 
@@ -663,7 +710,8 @@
         return send, got, places
 
     p_away = swap(p_theirs, "mp", 1)
-    d_mine, *d_theirs = call(enc_down_kernel, [(d_seg.shape, BF)] + d_seg.parts(), (pos, rows_at, d_enc, hidden), 30)
+    d_theirs = call(partial(enc_down_kernel, 1), d_seg.parts(), (pos, rows_at, d_enc, hidden), 30)
+    (d_mine,) = call(partial(enc_down_kernel, 0), [(d_seg.shape, BF)], (pos, rows_at, d_enc, hidden), 30, tokens=d_theirs[:1])
     p_own, d_own = (p_mine, [p_away]), (d_mine, from_core(d_theirs))
     send, p_arrived, (p_got, d_got, at_predicted) = stage(
         [first(p_own, p_seg), first(d_own, d_seg), ([[(predicted, 0, predicted.shape[0])]], [])], [], 30
@@ -727,8 +775,9 @@
             segments += terms
         return segments
 
-    (*a_send, z_send, stats), _, (a_then,) = stage(
-        [second(a_own, a_seg, a_got)], u_send, 3, (stats, stats_got), [last(p_z, p_one, 1) + last(d_z, d_one, 1)]
+    filler = [[(a_got[0][0], 0, a_seg.b - a_seg.a)]]
+    (*a_send, z_send, stats), _, (a_then, _) = stage(
+        [second(a_own, a_seg, a_got), ([], filler)], u_send, 3, (stats, stats_got), [last(p_z, p_one, 1) + last(d_z, d_one, 1)]
     )
     a_z = (a_own, a_seg, a_got, a_then)
     z_got = swap(z_send, "dp", 4)
@@ -741,62 +790,50 @@
     d_input, stats, p_two_array = gate([d_input, stats, z_got], [z_send])
     p_two, d_two = (p_two_array, 0), (p_two_array, p_rows)
     stats_got, input_x, input_c = swap(stats, "dp", 4), swap(d_input, "mp", 2), swap(d_input, "mp", 1)
-    p_sum, d_sum = combine([last(p_z, p_one, 0, p_two), last(d_z, d_one, 0, d_two)], [z_send], 3, kind=F32)
+    *p_results, r_down = sums_of(
+        [(last(p_z, p_one, 0, p_two), p_seg, p_cuts), (last(d_z, d_one, 0, d_two), d_seg, d_cuts)], [z_send], 3
+    )
     (predictions,) = call(
         in_order_kernel, [((SHARDS, length, channels), BF)], (pos, predicted, predicted_c, predicted_x, predicted_xc), 3,
-        tokens=(p_sum,),
+        tokens=(p_results[1],),
     )
     z_send, stats = combine([last(a_z, a_one, 1)], [predictions], 3, (stats, stats_got))
     a_two = (swap(z_send, "dp", 4), 0)
     (input_x,) = gate([input_x], [z_send])
-    u_sum, stats = combine([last(u_z, u_one, 0, u_two)], [z_send], 3, (stats, swap(stats, "mp", 2)), kind=F32)
+    r_up, stats = sums_of([(last(u_z, u_one, 0, u_two), u_seg, u_cuts)], [z_send], 3, (stats, swap(stats, "mp", 2)))
     stats_got = swap(stats, "dp", 1)
     (patches_grad,) = call(
         in_order_kernel, [((SHARDS, length, width), BF)], (pos, d_input, input_c, input_x, swap(input_x, "mp", 1)), 2,
-        tokens=(u_sum,),
-    )
-    a_sum, stats = combine([last(a_z, a_one, 0, a_two)], [patches_grad], 3, (stats, stats_got), kind=F32)
+        tokens=(r_up,),
+    )
+    *a_results, stats = sums_of([(last(a_z, a_one, 0, a_two), a_seg, a_cuts)], [patches_grad], 3, (stats, stats_got))
     for at in range(3, dp_size.bit_length() - 1):
         stats = stats + swap(stats, "dp", 1 << at)
-
-    def own_rows(total, seg):
-        total = total.reshape(seg.left + seg.right, -1, 128)
-        if dp_size > 8:
-            groups = [[high * 8 + low for high in range(dp_size // 8)] for low in range(8)]
-            total = lax.psum_scatter(total, "dp", scatter_dimension=1, axis_index_groups=groups, tiled=True)
-        return jnp.swapaxes(total, 0, 1).reshape(total.shape[1], -1)
-
-    r_pred, r_down, r_up, r_attn = (
-        own_rows(total, seg) for total, seg in ((p_sum, p_seg), (d_sum, d_seg), (u_sum, u_seg), (a_sum, a_seg))
-    )
 
     count = dp_size * patches.shape[0] * length
     mean, square = stats[0] / count, stats[1] / count
     n_var = channels // SHARDS
     variance = lax.dynamic_slice_in_dim(square - mean * mean, me * n_var, n_var)
-    tail = r_attn[:, 4 * cols + p_cols :]
-
-    def qkv_of(block, n):
-        return jnp.stack([block[:, i * n : (i + 1) * n] for i in range(3)])
+    tail = a_results[3]
 
     return (
         predictions,
         patches_grad,
         variance,
-        tail[:, 0],
-        qkv_of(r_attn, cols),
-        r_attn[:, 3 * cols : 4 * cols].T,
-        tail[:, 1],
+        tail[0],
+        a_results[0],
+        a_results[1],
+        tail[1],
         r_up,
-        r_down.T,
-        r_attn[:, 4 * cols : 4 * cols + p_cols],
-        tail[:n_small, 4],
-        tail[:n_small, 2],
-        qkv_of(r_pred, p_cols),
-        r_pred[:, 3 * p_cols : 4 * p_cols].T,
-        tail[:n_small, 3],
-        r_pred[:, 4 * p_cols : 4 * p_cols + p_hid],
-        r_pred[:, 4 * p_cols + p_hid :].T,
+        r_down,
+        a_results[2],
+        tail[4, :n_small],
+        tail[2, :n_small],
+        p_results[0],
+        p_results[1],
+        tail[3, :n_small],
+        p_results[2],
+        p_results[3],
     )
 
 

time: 268 us -> 261 us (0.974)
  waiting for transfers between devices: 74.4 us -> 68.2 us
    ppermute x54, waiting for transfers between devices: 74.4 us -> 68.2 us  [swap(): return lax.ppermute(value, axis, [(i, i ^ bit) for i in range(size)])]
    unnamed x191 -> x211, local copies, waits for them, and re-layouts: 29.9 us -> 35.6 us
    pallas_call x12 -> x13, Pallas kernels: 82.3 us -> 80.2 us  [call(): pl.pallas_call(lambda *refs: kernel(*refs[:n_args], *refs[n_all:]), out_s...]
  transfers between devices with their start and end apart: 54 -> 54, of which waited for: 18 -> 20; matrix products, arithmetic and copies ran while one was open for 4% -> 3% of each run, Pallas kernels for 31% -> 32%
where the time goes in v3:
time: 261 us; the launch traced here: 257 us
  Pallas kernels  105 us (40%)
  waiting for transfers between devices  68.2 us (26%)
  local copies, waits for them, and re-layouts  41.4 us (16%)
  starting transfers between devices  39.6 us (15%)
    pallas_call x13, Pallas kernels, call(): pl.pallas_call(lambda *refs: kernel(*refs[:n_args], *refs[n_all:]), out_s...  80.2 us
    ppermute x54, waiting for transfers between devices, swap(): return lax.ppermute(value, axis, [(i, i ^ bit) for i in range(size)])  68.2 us
    ppermute x54, starting transfers between devices, swap(): return lax.ppermute(value, axis, [(i, i ^ bit) for i in range(size)])  39.6 us
    unnamed x211, local copies, waits for them, and re-layouts  35.6 us
    pallas_call x11, Pallas kernels, combine(): pl.pallas_call(kernel, out_shape=shapes + ([jax.ShapeDtypeStruct(sums[0]....  25 us
  transfers between devices with their start and end apart: 54, of which 20 were waited for; matrix products, arithmetic and copies ran while one was open for 3% of the time, Pallas kernels for 32%

profile of v3, /device:TPU:0, one launch (start us, length us, event | category | flops | bytes accessed | tf_op | source)
XLA Modules:
  0.0 257.4 jit_solution(10461425427339143596)
XLA Ops:
  4.7 2.9 %collective-permute-start.1 = (bf16[384,768]{1,0:T(8,128)(2,1)S(1)}, bf16[384,768]{1,0:T(8,128)(2,1)S(1)}, u32[]{:S(2)}, u32[]{:S(2)}) collective-permute-start(bf16[384,768]{1,0:T(8,128)(2,1)S(1)} %get-tuple-element.96.refs_8_), channel_id=1, source_target_pairs={{0,2},{1,3},{2,0},{3,1},{4,6},{5,7},{6,4},{7,5},{8,10},{9,11},{10,... | collective-permute-start | bytes 1769480 | tf_op jit(solution)/shard_map/ppermute | solution.py:535
  11.1 9.9 %collective-permute-done.1.refs_0_ = bf16[384,768]{1,0:T(8,128)(2,1)S(1)} collective-permute-done((bf16[384,768]{1,0:T(8,128)(2,1)S(1)}, bf16[384,768]{1,0:T(8,128)(2,1)S(1)}, u32[]{:S(2)}, u32[]{:S(2)}) %collective-permute-start.1) | collective-permute-done | bytes 589856 | tf_op jit(solution)/shard_map/ppermute | solution.py:535
  25.1 11.6 %collective-permute-done.2.refs_8_.refs_9_ = bf16[384,768]{1,0:T(8,128)(2,1)} collective-permute-done((bf16[384,768]{1,0:T(8,128)(2,1)}, bf16[384,768]{1,0:T(8,128)(2,1)}, u32[]{:S(2)}, u32[]{:S(2)}) %collective-permute-start.2) | collective-permute-done | bytes 589856 | tf_op jit(solution)/shard_map/ppermute | solution.py:535
  41.4 9.1 %shard_map.308 = (f32[256,768]{1,0:T(8,128)S(1)}, bf16[2304,256]{1,0:T(8,128)(2,1)S(1)}, bf16[12,256,256]{2,1,0:T(8,128)(2,1)}, bf16[768,256]{1,0:T(8,128)(2,1)S(1)}) custom-call(s32[4]{0:T(128)S(1)} %pad_add_fusion.refs_0_, bf16[256,768]{1,0:T(8,128)(2,1)S(1)} %copy-done.12, s32[1,256]{1,0:T(1,128)S(1)} %constant_dynamic-slice_fusion.3.refs_2_, ...), custom_call_target="tpu_custom_call" | custom-call | flops 10350000128 | bytes 9049104 | tf_op jit(solution)/shard_map/pallas_call | solution.py:131
  52.1 3.7 %collective-permute-done.7.refs_0_ = bf16[768,384]{1,0:T(8,128)(2,1)} collective-permute-done((bf16[768,384]{1,0:T(8,128)(2,1)}, bf16[768,384]{1,0:T(8,128)(2,1)}, u32[]{:S(2)}, u32[]{:S(2)}) %collective-permute-start.7) | collective-permute-done | bytes 589856 | tf_op jit(solution)/shard_map/ppermute | solution.py:535
  60.9 6.1 %shard_map.310 = (bf16[256,3072]{1,0:T(8,128)(2,1)}, bf16[256,3072]{1,0:T(8,128)(2,1)}) custom-call(s32[4]{0:T(128)S(1)} %pad_add_fusion.refs_0_, f32[256,768]{1,0:T(8,128)S(1)} %copy-done.26, f32[1,768]{1,0:T(1,128)S(1)} %reshape.151.refs_2_.refs_4_, bf16[768,768]{1,0:T(8,128)(2,1)S(1)} %copy-done.61, ...), custom_call_target="tpu_custom_call" | custom-call | flops 6899999744 | bytes 8653840 | tf_op jit(solution)/shard_map/pallas_call | solution.py:131
  67.0 6.1 %collective-permute-done.12.refs_0_ = bf16[384,768]{1,0:T(8,128)(2,1)} collective-permute-done((bf16[384,768]{1,0:T(8,128)(2,1)}, bf16[384,768]{1,0:T(8,128)(2,1)}, u32[]{:S(2)}, u32[]{:S(2)}) %collective-permute-start.12) | collective-permute-done | bytes 589856 | tf_op jit(solution)/shard_map/ppermute | solution.py:535
  73.1 2.2 collective-permute-done.14.refs_8_.refs_17_
  76.4 4.1 %shard_map.313.refs_1_.refs_8_ = bf16[256,768]{1,0:T(8,128)(2,1)S(1)} custom-call(s32[4]{0:T(128)S(1)} %pad_add_fusion.refs_0_, f32[256,768]{1,0:T(8,128)S(1)} %copy-done.27, bf16[256,3072]{1,0:T(8,128)(2,1)} %get-tuple-element.102.refs_1_.refs_2_.refs_3_, bf16[768,768]{1,0:T(8,128)(2,1)S(1)} %copy-done.63, ...), custom_call_target="tpu_custom_call" | custom-call | flops 4600000000 | bytes 7471120 | tf_op jit(solution)/shard_map/pallas_call | solution.py:131
  87.6 18.8 %shard_map.316 = (bf16[768,128]{1,0:T(8,128)(2,1)S(1)}, f32[8,384]{1,0:T(8,128)S(1)}, bf16[6912,128]{1,0:T(8,128)(2,1)}, bf16[6912,128]{1,0:T(8,128)(2,1)}, bf16...) custom-call(s32[4]{0:T(128)S(1)} %pad_add_fusion.refs_0_, bf16[256,768]{1,0:T(8,128)(2,1)S(1)} %copy-done.34, ...), custom_call_target="tpu_custom_call" | custom-call | flops 34500001792 | bytes 9470992 | tf_op jit(solution)/shard_map/pallas_call | solution.py:131
  106.7 3.2 %shard_map.317 = (bf16[2304,128]{1,0:T(8,128)(2,1)S(1)}, bf16[2304,128]{1,0:T(8,128)(2,1)S(1)}, bf16[4608,128]{1,0:T(8,128)(2,1)}) custom-call(s32[4]{0:T(128)S(1)} %pad_add_fusion.refs_0_, s32[768,1]{1,0:T(8,128)S(1)} %add.91.refs_1_, f32[256,768]{1,0:T(8,128)S(1)} %get-tuple-element.107.refs_2_, bf16[256,3072]{1,0:T(8,128)(2,1)S(1)} %copy-done.11), custom_call_target="tpu_custom_call" | custom-call | flops 34500001792 | bytes 4721680 | tf_op jit(solution)/shard_map/pallas_call | solution.py:131
  110.7 2.3 shard_map.318.refs_2_.refs_8_.refs_13_
  116.4 2.5 shard_map.319
  121.9 13.3 %shard_map.320 = (f32[256,768]{1,0:T(8,128)}, f32[1,768]{1,0:T(1,128)S(1)}, bf16[9216,128]{1,0:T(8,128)(2,1)}, bf16[2304,128]{1,0:T(8,128)(2,1)S(1)}, bf16[2304,...) custom-call(s32[4]{0:T(128)S(1)} %pad_add_fusion.refs_0_, s32[768,1]{1,0:T(8,128)S(1)} %add.91.refs_1_, ...), custom_call_target="tpu_custom_call" | custom-call | flops 115000000512 | bytes 18097168 | tf_op jit(solution)/shard_map/pallas_call | solution.py:131
  136.9 10.2 %shard_map.321 = (bf16[2304,256]{1,0:T(8,128)(2,1)S(1)}, bf16[1536,128]{1,0:T(8,128)(2,1)S(1)}, f32[1,768]{1,0:T(1,128)S(1)}) custom-call(s32[4]{0:T(128)S(1)} %pad_add_fusion.refs_0_, bf16[256,768]{1,0:T(8,128)(2,1)S(1)} %copy-done.13, f32[1,768]{1,0:T(1,128)S(1)} %reshape.150.refs_4_.refs_2_.refs_3_, f32[256,768]{1,0:T(8,128)S(1)} %copy-done.28, ...), custom_call_target="tpu_custom_call" | custom-call | flops 1150000000 | bytes 10229776 | tf_op jit(solution)/shard_map/pallas_call | solution.py:131
  150.2 3.0 %shard_map.323 = (bf16[4416,128]{1,0:T(8,128)(2,1)S(1)}, bf16[4416,128]{1,0:T(8,128)(2,1)S(1)}) custom-call(bf16[9216,128]{1,0:T(8,128)(2,1)} %get-tuple-element.121.refs_0_.refs_8_.refs_2_, bf16[2304,128]{1,0:T(8,128)(2,1)} %get-tuple-element.122.refs_1_, bf16[9216,128]{1,0:T(8,128)(2,1)} %copy-done.2, ...), custom_call_target="tpu_custom_call" | custom-call | flops 34500001792 | bytes 7766016 | tf_op jit(solution)/shard_map/pallas_call | solution.py:253
  154.7 6.3 %shard_map.325 = (bf16[10752,128]{1,0:T(8,128)(2,1)}, bf16[2304,128]{1,0:T(8,128)(2,1)S(1)}, bf16[3072,128]{1,0:T(8,128)(2,1)S(1)}, bf16[5376,128]{1,0:T(8,128)(2,1)}) custom-call(s32[4]{0:T(128)S(1)} %pad_add_fusion.refs_0_, s32[768,1]{1,0:T(8,128)S(1)} %add.91.refs_1_, bf16[256,768]{1,0:T(8,128)(2,1)S(1)} %copy-done.13, ...), custom_call_target="tpu_custom_call" | custom-call | flops 115000000512 | bytes 8871952 | tf_op jit(solution)/shard_map/pallas_call | solution.py:131
  165.0 2.1 shard_map.326
  169.9 11.1 %collective-permute-done.27.refs_3_.refs_12_.refs_2_.refs_10_.refs_7_.refs_4_ = bf16[4416,128]{1,0:T(8,128)(2,1)S(1)} collective-permute-done((bf16[4416,128]{1,0:T(8,128)(2,1)S(1)}, bf16[4416,128]{1,0:T(8,128)(2,1)S(1)}, u32[]{:S(2)}, u32[]{:S(2)}) %collective-permute-start.27) | collective-permute-done | bytes 1130528 | tf_op jit(solution)/shard_map/ppermute | solution.py:535
  183.0 2.3 shard_map.327
  191.3 2.3 collective-permute-done.36.refs_5_.refs_4_
  193.6 5.1 %collective-permute-done.35.refs_4_.refs_6_.refs_7_.refs_8_ = bf16[3072,128]{1,0:T(8,128)(2,1)} collective-permute-done((bf16[3072,128]{1,0:T(8,128)(2,1)S(1)}, bf16[3072,128]{1,0:T(8,128)(2,1)}, u32[]{:S(2)}, u32[]{:S(2)}) %collective-permute-start.35) | collective-permute-done | bytes 786464 | tf_op jit(solution)/shard_map/ppermute | solution.py:535
  201.3 2.2 shard_map.329
  210.9 2.6 %collective-permute-start.44 = (bf16[1008,128]{1,0:T(8,128)(2,1)}, bf16[1008,128]{1,0:T(8,128)(2,1)S(1)}, u32[]{:S(2)}, u32[]{:S(2)}) collective-permute-start(bf16[1008,128]{1,0:T(8,128)(2,1)} %copy-done.79), channel_id=1, source_target_pairs={{0,16},{4,20},{8,24},{12,28},{16,0},{20,4},{24,8},{28,12},{1,17},{... | collective-permute-start | bytes 774152 | tf_op jit(solution)/shard_map/ppermute | solution.py:535
  213.4 4.9 %collective-permute-done.40.refs_1_ = f32[8,384]{1,0:T(8,128)S(1)} collective-permute-done((f32[8,384]{1,0:T(8,128)S(1)}, f32[8,384]{1,0:T(8,128)S(1)}, u32[]{:S(2)}, u32[]{:S(2)}) %collective-permute-start.40) | collective-permute-done | bytes 12320 | tf_op jit(solution)/shard_map/ppermute | solution.py:535
  218.9 2.6 %shard_map.332 = (bf16[1344,128]{1,0:T(8,128)(2,1)S(1)}, bf16[576,128]{1,0:T(8,128)(2,1)}, f32[8,384]{1,0:T(8,128)S(1)}) custom-call(f32[8,384]{1,0:T(8,128)S(1)} %get-tuple-element.151.refs_0_, f32[8,384]{1,0:T(8,128)S(1)} %collective-permute-done.40.refs_1_, bf16[10752,128]{1,0:T(8,128)(2,1)} %get-tuple-element.136.refs_0_.refs_2_, ...), custom_call_target="tpu_custom_call" | custom-call | flops 3449999872 | bytes 2605056 | tf_op jit(solution)/shard_map/pallas_call | solution.py:253
  226.2 2.7 %shard_map.334 = (f32[3,48,96]{2,1,0:T(8,128)}, f32[96,48]{1,0:T(8,128)S(1)}, f32[48,384]{1,0:T(8,128)}, f32[384,48]{1,0:T(8,128)S(1)}, f32[768,96]{1,0:T(8,128)S(1)}) custom-call(bf16[6912,128]{1,0:T(8,128)(2,1)} %get-tuple-element.105.refs_0_.refs_5_.refs_4_.refs_6_, bf16[6912,128]{1,0:T(8,128)(2,1)} %copy-done.90, ...), custom_call_target="tpu_custom_call" | custom-call | flops 3449999872 | bytes 1806336 | tf_op jit(solution)/shard_map/pallas_call | solution.py:253
  233.2 2.0 shard_map.335.refs_9_
  243.3 2.2 shard_map.338
  246.7 2.5 shard_map.339.refs_10_
  249.4 3.6 %collective-permute-done.53.refs_7_ = bf16[672,128]{1,0:T(8,128)(2,1)S(1)} collective-permute-done((bf16[672,128]{1,0:T(8,128)(2,1)S(1)}, bf16[672,128]{1,0:T(8,128)(2,1)S(1)}, u32[]{:S(2)}, u32[]{:S(2)}) %collective-permute-start.53) | collective-permute-done | bytes 172064 | tf_op jit(solution)/shard_map/ppermute | solution.py:535
  252.9 2.3 shard_map.340
  (348 shorter events, 89.7 us)
Async XLA Ops:
  4.7 16.3 %collective-permute-start.1 = (bf16[384,768]{1,0:T(8,128)(2,1)S(1)}, bf16[384,768]{1,0:T(8,128)(2,1)S(1)}, u32[]{:S(2)}, u32[]{:S(2)}) collective-permute-start(bf16[384,768]{1,0:T(8,128)(2,1)S(1)} %get-tuple-element.96.refs_8_), channel_id=1, source_target_pairs={{0,2},{1,3},{2,0},{3,1},{4,6},{5,7},{6,4},{7,5},{8,10},{9,11},{10,... | collective-permute-start | bytes 1769480 | tf_op jit(solution)/shard_map/ppermute | solution.py:535
  7.7 30.6 %collective-permute-start = (bf16[768,768]{1,0:T(8,128)(2,1)}, bf16[768,768]{1,0:T(8,128)(2,1)}, u32[]{:S(2)}, u32[]{:S(2)}) collective-permute-start(bf16[768,768]{1,0:T(8,128)(2,1)} %get-tuple-element.95.refs_5_.refs_6_), channel_id=1, source_target_pairs={{0,1},{1,0},{2,3},{3,2},{4,5},{5,4},{6,7},{7,6},{8,9},{9,8},{10,11... | collective-permute-start | bytes 3538952 | tf_op jit(solution)/shard_map/ppermute | solution.py:535
  21.8 14.8 %collective-permute-start.2 = (bf16[384,768]{1,0:T(8,128)(2,1)}, bf16[384,768]{1,0:T(8,128)(2,1)}, u32[]{:S(2)}, u32[]{:S(2)}) collective-permute-start(bf16[384,768]{1,0:T(8,128)(2,1)} %get-tuple-element.99.refs_7_.refs_8_), channel_id=1, source_target_pairs={{0,4},{4,0},{8,12},{12,8},{16,20},{20,16},{24,28},{28,24},{1,5},{5... | collective-permute-start | bytes 1769480 | tf_op jit(solution)/shard_map/ppermute | solution.py:535
  23.6 14.6 %collective-permute-start.6 = (bf16[768,384]{1,0:T(8,128)(2,1)}, bf16[768,384]{1,0:T(8,128)(2,1)}, u32[]{:S(2)}, u32[]{:S(2)}) collective-permute-start(bf16[768,384]{1,0:T(8,128)(2,1)} %get-tuple-element.101), channel_id=1, source_target_pairs={{0,2},{1,3},{2,0},{3,1},{4,6},{5,7},{6,4},{7,5},{8,10},{9,11},{10,... | collective-permute-start | bytes 1769480 | tf_op jit(solution)/shard_map/ppermute | solution.py:535
  25.1 14.7 %collective-permute-start.3 = (bf16[384,768]{1,0:T(8,128)(2,1)}, bf16[384,768]{1,0:T(8,128)(2,1)}, u32[]{:S(2)}, u32[]{:S(2)}) collective-permute-start(bf16[384,768]{1,0:T(8,128)(2,1)} %get-tuple-element.99.refs_7_.refs_8_), channel_id=1, source_target_pairs={{0,1},{1,0},{2,3},{3,2},{4,5},{5,4},{6,7},{7,6},{8,9},{9,8},{10,11... | collective-permute-start | bytes 1769480 | tf_op jit(solution)/shard_map/ppermute | solution.py:535
  36.6 20.4 %collective-permute-start.5 = (bf16[768,768]{1,0:T(8,128)(2,1)}, bf16[768,768]{1,0:T(8,128)(2,1)}, u32[]{:S(2)}, u32[]{:S(2)}) collective-permute-start(bf16[768,768]{1,0:T(8,128)(2,1)} %refs_6_.3), channel_id=1, source_target_pairs={{0,1},{1,0},{2,3},{3,2},{4,5},{5,4},{6,7},{7,6},{8,9},{9,8},{10,11... | collective-permute-start | bytes 3538952 | tf_op jit(solution)/shard_map/ppermute | solution.py:535
  38.1 17.7 %collective-permute-start.15 = (bf16[1344,384]{1,0:T(8,128)(2,1)S(1)}, bf16[1344,384]{1,0:T(8,128)(2,1)}, u32[]{:S(2)}, u32[]{:S(2)}) collective-permute-start(bf16[1344,384]{1,0:T(8,128)(2,1)S(1)} %copy-done.4), channel_id=1, source_target_pairs={{0,1},{1,0},{2,3},{3,2},{4,5},{5,4},{6,7},{7,6},{8,9},{9,8},{10,11... | collective-permute-start | bytes 3096584 | tf_op jit(solution)/shard_map/ppermute | solution.py:535
  38.2 18.2 %collective-permute-start.11 = (bf16[384,768]{1,0:T(8,128)(2,1)}, bf16[384,768]{1,0:T(8,128)(2,1)}, u32[]{:S(2)}, u32[]{:S(2)}) collective-permute-start(bf16[384,768]{1,0:T(8,128)(2,1)} %shard_map.311), channel_id=1, source_target_pairs={{0,2},{1,3},{2,0},{3,1},{4,6},{5,7},{6,4},{7,5},{8,10},{9,11},{10,... | collective-permute-start | bytes 1769480 | tf_op jit(solution)/shard_map/ppermute | solution.py:535
  39.7 17.3 %collective-permute-start.8 = (bf16[768,384]{1,0:T(8,128)(2,1)}, bf16[768,384]{1,0:T(8,128)(2,1)}, u32[]{:S(2)}, u32[]{:S(2)}) collective-permute-start(bf16[768,384]{1,0:T(8,128)(2,1)} %collective-permute-done.6.refs_5_.refs_1_.refs_8_), channel_id=1, source_target_pairs={{0,1},{1,0},{2,3},{3,2},{4,5},{5,4},{6,7},{7,6},{8,9},{9,8},{10,11... | collective-permute-start | bytes 1769480 | tf_op jit(solution)/shard_map/ppermute | solution.py:535
  39.9 15.9 %collective-permute-start.7 = (bf16[768,384]{1,0:T(8,128)(2,1)}, bf16[768,384]{1,0:T(8,128)(2,1)}, u32[]{:S(2)}, u32[]{:S(2)}) collective-permute-start(bf16[768,384]{1,0:T(8,128)(2,1)} %collective-permute-done.6.refs_5_.refs_1_.refs_8_), channel_id=1, source_target_pairs={{0,4},{4,0},{8,12},{12,8},{16,20},{20,16},{24,28},{28,24},{1,5},{5... | collective-permute-start | bytes 1769480 | tf_op jit(solution)/shard_map/ppermute | solution.py:535
  55.8 17.3 %collective-permute-start.10 = (bf16[768,768]{1,0:T(8,128)(2,1)}, bf16[768,768]{1,0:T(8,128)(2,1)}, u32[]{:S(2)}, u32[]{:S(2)}) collective-permute-start(bf16[768,768]{1,0:T(8,128)(2,1)} %refs_12_.1), channel_id=1, source_target_pairs={{0,1},{1,0},{2,3},{3,2},{4,5},{5,4},{6,7},{7,6},{8,9},{9,8},{10,11... | collective-permute-start | bytes 3538952 | tf_op jit(solution)/shard_map/ppermute | solution.py:535
  56.4 25.0 %collective-permute-start.16 = (bf16[1344,384]{1,0:T(8,128)(2,1)}, bf16[1344,384]{1,0:T(8,128)(2,1)S(1)}, u32[]{:S(2)}, u32[]{:S(2)}) collective-permute-start(bf16[1344,384]{1,0:T(8,128)(2,1)} %shard_map.314.refs_10_), channel_id=1, source_target_pairs={{0,2},{1,3},{2,0},{3,1},{4,6},{5,7},{6,4},{7,5},{8,10},{9,11},{10,... | collective-permute-start | bytes 3096584 | tf_op jit(solution)/shard_map/ppermute | solution.py:535
  57.0 16.1 %collective-permute-start.13 = (bf16[384,768]{1,0:T(8,128)(2,1)}, bf16[384,768]{1,0:T(8,128)(2,1)}, u32[]{:S(2)}, u32[]{:S(2)}) collective-permute-start(bf16[384,768]{1,0:T(8,128)(2,1)} %collective-permute-done.11.refs_5_.refs_1_.refs_14_), channel_id=1, source_target_pairs={{0,1},{1,0},{2,3},{3,2},{4,5},{5,4},{6,7},{7,6},{8,9},{9,8},{10,11... | collective-permute-start | bytes 1769480 | tf_op jit(solution)/shard_map/ppermute | solution.py:535
  57.0 16.1 %collective-permute-start.12 = (bf16[384,768]{1,0:T(8,128)(2,1)}, bf16[384,768]{1,0:T(8,128)(2,1)}, u32[]{:S(2)}, u32[]{:S(2)}) collective-permute-start(bf16[384,768]{1,0:T(8,128)(2,1)} %collective-permute-done.11.refs_5_.refs_1_.refs_14_), channel_id=1, source_target_pairs={{0,4},{4,0},{8,12},{12,8},{16,20},{20,16},{24,28},{28,24},{1,5},{5... | collective-permute-start | bytes 1769480 | tf_op jit(solution)/shard_map/ppermute | solution.py:535
  114.5 35.7 %collective-permute-start.25 = (bf16[4608,128]{1,0:T(8,128)(2,1)}, bf16[4608,128]{1,0:T(8,128)(2,1)}, u32[]{:S(2)}, u32[]{:S(2)}) collective-permute-start(bf16[4608,128]{1,0:T(8,128)(2,1)} %get-tuple-element.123), channel_id=1, source_target_pairs={{0,1},{1,0},{2,3},{3,2},{4,5},{5,4},{6,7},{7,6},{8,9},{9,8},{10,11... | collective-permute-start | bytes 3538952 | tf_op jit(solution)/shard_map/ppermute | solution.py:535
  119.0 28.9 %collective-permute-start.22 = (bf16[4224,128]{1,0:T(8,128)(2,1)S(1)}, bf16[4224,128]{1,0:T(8,128)(2,1)S(1)}, u32[]{:S(2)}, u32[]{:S(2)}) collective-permute-start(bf16[4224,128]{1,0:T(8,128)(2,1)S(1)} %get-tuple-element.111.refs_19_), channel_id=1, source_target_pairs={{0,4},{4,0},{8,12},{12,8},{16,20},{20,16},{24,28},{28,24},{1,5},{5... | collective-permute-start | bytes 3244040 | tf_op jit(solution)/shard_map/ppermute | solution.py:535
  120.5 27.8 %collective-permute-start.21 = (bf16[4608,128]{1,0:T(8,128)(2,1)S(1)}, bf16[4608,128]{1,0:T(8,128)(2,1)S(1)}, u32[]{:S(2)}, u32[]{:S(2)}) collective-permute-start(bf16[4608,128]{1,0:T(8,128)(2,1)S(1)} %get-tuple-element.110.refs_18_), channel_id=1, source_target_pairs={{0,2},{1,3},{2,0},{3,1},{4,6},{5,7},{6,4},{7,5},{8,10},{9,11},{10,... | collective-permute-start | bytes 3538952 | tf_op jit(solution)/shard_map/ppermute | solution.py:535
  147.7 20.7 %collective-permute-start.26 = (bf16[4608,128]{1,0:T(8,128)(2,1)}, bf16[4608,128]{1,0:T(8,128)(2,1)}, u32[]{:S(2)}, u32[]{:S(2)}) collective-permute-start(bf16[4608,128]{1,0:T(8,128)(2,1)} %get-tuple-element.130), channel_id=1, source_target_pairs={{0,1},{1,0},{2,3},{3,2},{4,5},{5,4},{6,7},{7,6},{8,9},{9,8},{10,11... | collective-permute-start | bytes 3538952 | tf_op jit(solution)/shard_map/ppermute | solution.py:535
  153.2 27.8 %collective-permute-start.27 = (bf16[4416,128]{1,0:T(8,128)(2,1)S(1)}, bf16[4416,128]{1,0:T(8,128)(2,1)S(1)}, u32[]{:S(2)}, u32[]{:S(2)}) collective-permute-start(bf16[4416,128]{1,0:T(8,128)(2,1)S(1)} %get-tuple-element.126.refs_3_.refs_12_), channel_id=1, source_target_pairs={{0,2},{1,3},{2,0},{3,1},{4,6},{5,7},{6,4},{7,5},{8,10},{9,11},{10,... | collective-permute-start | bytes 3391496 | tf_op jit(solution)/shard_map/ppermute | solution.py:535
  154.0 27.8 %collective-permute-start.28 = (bf16[4416,128]{1,0:T(8,128)(2,1)S(1)}, bf16[4416,128]{1,0:T(8,128)(2,1)S(1)}, u32[]{:S(2)}, u32[]{:S(2)}) collective-permute-start(bf16[4416,128]{1,0:T(8,128)(2,1)S(1)} %get-tuple-element.127.refs_4_.refs_13_), channel_id=1, source_target_pairs={{0,4},{4,0},{8,12},{12,8},{16,20},{20,16},{24,28},{28,24},{1,5},{5... | collective-permute-start | bytes 3391496 | tf_op jit(solution)/shard_map/ppermute | solution.py:535
  163.0 27.2 %collective-permute-start.34 = (bf16[5376,128]{1,0:T(8,128)(2,1)}, bf16[5376,128]{1,0:T(8,128)(2,1)}, u32[]{:S(2)}, u32[]{:S(2)}) collective-permute-start(bf16[5376,128]{1,0:T(8,128)(2,1)} %get-tuple-element.144), channel_id=1, source_target_pairs={{0,1},{1,0},{2,3},{3,2},{4,5},{5,4},{6,7},{7,6},{8,9},{9,8},{10,11... | collective-permute-start | bytes 4128776 | tf_op jit(solution)/shard_map/ppermute | solution.py:535
  167.2 26.4 %collective-permute-start.36 = (bf16[2304,128]{1,0:T(8,128)(2,1)S(1)}, bf16[2304,128]{1,0:T(8,128)(2,1)}, u32[]{:S(2)}, u32[]{:S(2)}) collective-permute-start(bf16[2304,128]{1,0:T(8,128)(2,1)S(1)} %get-tuple-element.139.refs_10_), channel_id=1, source_target_pairs={{0,2},{1,3},{2,0},{3,1},{4,6},{5,7},{6,4},{7,5},{8,10},{9,11},{10,... | collective-permute-start | bytes 1769480 | tf_op jit(solution)/shard_map/ppermute | solution.py:535
  168.4 30.2 %collective-permute-start.35 = (bf16[3072,128]{1,0:T(8,128)(2,1)S(1)}, bf16[3072,128]{1,0:T(8,128)(2,1)}, u32[]{:S(2)}, u32[]{:S(2)}) collective-permute-start(bf16[3072,128]{1,0:T(8,128)(2,1)S(1)} %get-tuple-element.140.refs_11_), channel_id=1, source_target_pairs={{0,4},{4,0},{8,12},{12,8},{16,20},{20,16},{24,28},{28,24},{1,5},{5... | collective-permute-start | bytes 2359304 | tf_op jit(solution)/shard_map/ppermute | solution.py:535
  186.8 13.0 %collective-permute-start.37 = (bf16[2016,128]{1,0:T(8,128)(2,1)S(1)}, bf16[2016,128]{1,0:T(8,128)(2,1)S(1)}, u32[]{:S(2)}, u32[]{:S(2)}) collective-permute-start(bf16[2016,128]{1,0:T(8,128)(2,1)S(1)} %get-tuple-element.145), channel_id=1, source_target_pairs={{0,8},{4,12},{8,0},{12,4},{16,24},{20,28},{24,16},{28,20},{1,9},{5... | collective-permute-start | bytes 1548296 | tf_op jit(solution)/shard_map/ppermute | solution.py:535
  189.7 15.7 %collective-permute-start.31 = (bf16[1152,128]{1,0:T(8,128)(2,1)}, bf16[1152,128]{1,0:T(8,128)(2,1)S(1)}, u32[]{:S(2)}, u32[]{:S(2)}) collective-permute-start(bf16[1152,128]{1,0:T(8,128)(2,1)} %copy-done.17), channel_id=1, source_target_pairs={{0,4},{4,0},{8,12},{12,8},{16,20},{20,16},{24,28},{28,24},{1,5},{5... | collective-permute-start | bytes 884744 | tf_op jit(solution)/shard_map/ppermute | solution.py:535
  190.3 15.2 %collective-permute-start.32 = (bf16[1152,128]{1,0:T(8,128)(2,1)}, bf16[1152,128]{1,0:T(8,128)(2,1)S(1)}, u32[]{:S(2)}, u32[]{:S(2)}) collective-permute-start(bf16[1152,128]{1,0:T(8,128)(2,1)} %copy-done.16), channel_id=1, source_target_pairs={{0,2},{1,3},{2,0},{3,1},{4,6},{5,7},{6,4},{7,5},{8,10},{9,11},{10,... | collective-permute-start | bytes 884744 | tf_op jit(solution)/shard_map/ppermute | solution.py:535
  204.2 14.7 %collective-permute-start.42 = (bf16[1536,128]{1,0:T(8,128)(2,1)S(1)}, bf16[1536,128]{1,0:T(8,128)(2,1)S(1)}, u32[]{:S(2)}, u32[]{:S(2)}) collective-permute-start(bf16[1536,128]{1,0:T(8,128)(2,1)S(1)} %get-tuple-element.146.refs_6_), channel_id=1, source_target_pairs={{0,2},{1,3},{2,0},{3,1},{4,6},{5,7},{6,4},{7,5},{8,10},{9,11},{10,... | collective-permute-start | bytes 1179656 | tf_op jit(solution)/shard_map/ppermute | solution.py:535
  204.8 14.0 %collective-permute-start.41 = (bf16[1536,128]{1,0:T(8,128)(2,1)S(1)}, bf16[1536,128]{1,0:T(8,128)(2,1)S(1)}, u32[]{:S(2)}, u32[]{:S(2)}) collective-permute-start(bf16[1536,128]{1,0:T(8,128)(2,1)S(1)} %get-tuple-element.147.refs_7_), channel_id=1, source_target_pairs={{0,4},{4,0},{8,12},{12,8},{16,20},{20,16},{24,28},{28,24},{1,5},{5... | collective-permute-start | bytes 1179656 | tf_op jit(solution)/shard_map/ppermute | solution.py:535
  218.3 13.4 %collective-permute-start.39 = (bf16[768,128]{1,0:T(8,128)(2,1)}, bf16[768,128]{1,0:T(8,128)(2,1)}, u32[]{:S(2)}, u32[]{:S(2)}) collective-permute-start(bf16[768,128]{1,0:T(8,128)(2,1)} %get-tuple-element.149.refs_3_), channel_id=1, source_target_pairs={{0,1},{1,0},{2,3},{3,2},{4,5},{5,4},{6,7},{7,6},{8,9},{9,8},{10,11... | collective-permute-start | bytes 589832 | tf_op jit(solution)/shard_map/ppermute | solution.py:535
  222.1 13.2 %collective-permute-start.48 = (bf16[1344,128]{1,0:T(8,128)(2,1)S(1)}, bf16[1344,128]{1,0:T(8,128)(2,1)S(1)}, u32[]{:S(2)}, u32[]{:S(2)}) collective-permute-start(bf16[1344,128]{1,0:T(8,128)(2,1)S(1)} %get-tuple-element.154.refs_3_.refs_10_), channel_id=1, source_target_pairs={{0,8},{4,12},{8,0},{12,4},{16,24},{20,28},{24,16},{28,20},{1,9},{5... | collective-permute-start | bytes 1032200 | tf_op jit(solution)/shard_map/ppermute | solution.py:535
  223.9 14.2 %collective-permute-start.46 = (bf16[1536,128]{1,0:T(8,128)(2,1)}, bf16[1536,128]{1,0:T(8,128)(2,1)S(1)}, u32[]{:S(2)}, u32[]{:S(2)}) collective-permute-start(bf16[1536,128]{1,0:T(8,128)(2,1)} %get-tuple-element.157.refs_1_), channel_id=1, source_target_pairs={{0,2},{1,3},{2,0},{3,1},{4,6},{5,7},{6,4},{7,5},{8,10},{9,11},{10,... | collective-permute-start | bytes 1179656 | tf_op jit(solution)/shard_map/ppermute | solution.py:535
  225.3 21.4 %collective-permute-start.45 = (bf16[1536,128]{1,0:T(8,128)(2,1)}, bf16[1536,128]{1,0:T(8,128)(2,1)}, u32[]{:S(2)}, u32[]{:S(2)}) collective-permute-start(bf16[1536,128]{1,0:T(8,128)(2,1)} %get-tuple-element.157.refs_1_), channel_id=1, source_target_pairs={{0,1},{1,0},{2,3},{3,2},{4,5},{5,4},{6,7},{7,6},{8,9},{9,8},{10,11... | collective-permute-start | bytes 1179656 | tf_op jit(solution)/shard_map/ppermute | solution.py:535
  (126 other events, 576.4 us)

commit v4 on v3

--- a/solution.py
+++ b/solution.py
@@ -79,7 +79,7 @@
         mixed_ref[at, :] = nn(qkv_ref[u_at, :], probs).astype(BF)
         return carry
 
-    lax.fori_loop(0, SHARDS * per, one_head, 0, unroll=4)
+    lax.fori_loop(0, SHARDS * per, one_head, 0, unroll=6)
 
 
 def attend_back(qkv_ref, probs_ref, d_mixed_ref, d_qkv_ref, per, head_dim):
@@ -99,7 +99,7 @@
         d_qkv_ref[u_at, :] = nt(d_mixed, low).astype(BF)
         return carry
 
-    lax.fori_loop(0, SHARDS * per, one_head, 0, unroll=4)
+    lax.fori_loop(0, SHARDS * per, one_head, 0, unroll=6)
 
 
 ANYWHERE = pl.BlockSpec(memory_space=pl.ANY)
@@ -639,8 +639,8 @@
          ((3 * channels, length), BF)],
     )
 
-    p_cuts = [(0, p_cols, 3, False), (3 * p_cols, p_cols, 1, True), (4 * p_cols, p_hid, 1, False), (4 * p_cols + p_hid, p_hid, 1, True)]
-    d_cuts, u_cuts = [(0, hid, 1, True)], [(0, hid, 1, False)]
+    p_cuts = [(0, p_cols, 3, False), (3 * p_cols, p_cols, 1, False), (4 * p_cols, p_hid, 1, False), (4 * p_cols + p_hid, p_hid, 1, False)]
+    d_cuts, u_cuts = [(0, hid, 1, False)], [(0, hid, 1, False)]
     a_cuts = [(0, cols, 3, False), (3 * cols, cols, 1, True), (4 * cols, p_cols, 1, False), (4 * cols + p_cols, 128 - p_cols, 1, True)]
     small = dp_size == 8
 
@@ -785,26 +785,28 @@
     u_one, stats_got = (swap(z_send, "dp", 2), 0), swap(stats, "dp", 2)
     predicted, predicted_x = gate([predicted, predicted_x], [z_send])
     predicted_c, predicted_xc = swap(predicted, "mp", 1), swap(predicted_x, "mp", 1)
-    z_send, z_send_u, stats = combine([kept(*a_z, 2, 4), last(u_z, u_one, 1)], [z_send], 3, (stats, stats_got))
+    z_send, z_send_u = combine([kept(*a_z, 2, 4), last(u_z, u_one, 1)], [z_send], 3)
     a_one, u_two = (swap(z_send, "dp", 2), 0), (swap(z_send_u, "dp", 4), 0)
-    d_input, stats, p_two_array = gate([d_input, stats, z_got], [z_send])
+    d_input, p_two_array = gate([d_input, z_got], [z_send])
     p_two, d_two = (p_two_array, 0), (p_two_array, p_rows)
-    stats_got, input_x, input_c = swap(stats, "dp", 4), swap(d_input, "mp", 2), swap(d_input, "mp", 1)
-    *p_results, r_down = sums_of(
-        [(last(p_z, p_one, 0, p_two), p_seg, p_cuts), (last(d_z, d_one, 0, d_two), d_seg, d_cuts)], [z_send], 3
-    )
-    (predictions,) = call(
-        in_order_kernel, [((SHARDS, length, channels), BF)], (pos, predicted, predicted_c, predicted_x, predicted_xc), 3,
-        tokens=(p_results[1],),
-    )
-    z_send, stats = combine([last(a_z, a_one, 1)], [predictions], 3, (stats, stats_got))
+    input_x, input_c = swap(d_input, "mp", 2), swap(d_input, "mp", 1)
+    *p_results, r_down, stats = sums_of(
+        [(last(p_z, p_one, 0, p_two), p_seg, p_cuts), (last(d_z, d_one, 0, d_two), d_seg, d_cuts)], [z_send], 3,
+        (stats, stats_got),
+    )
+    stats_got = swap(stats, "dp", 4)
+    z_send, stats = combine([last(a_z, a_one, 1)], [p_results[1]], 3, (stats, stats_got))
     a_two = (swap(z_send, "dp", 4), 0)
     (input_x,) = gate([input_x], [z_send])
     r_up, stats = sums_of([(last(u_z, u_one, 0, u_two), u_seg, u_cuts)], [z_send], 3, (stats, swap(stats, "mp", 2)))
     stats_got = swap(stats, "dp", 1)
+    (predictions,) = call(
+        in_order_kernel, [((SHARDS, length, channels), BF)], (pos, predicted, predicted_c, predicted_x, predicted_xc), 3,
+        tokens=(r_up,),
+    )
     (patches_grad,) = call(
         in_order_kernel, [((SHARDS, length, width), BF)], (pos, d_input, input_c, input_x, swap(input_x, "mp", 1)), 2,
-        tokens=(r_up,),
+        tokens=(predictions,),
     )
     *a_results, stats = sums_of([(last(a_z, a_one, 0, a_two), a_seg, a_cuts)], [patches_grad], 3, (stats, stats_got))
     for at in range(3, dp_size.bit_length() - 1):
@@ -825,15 +827,15 @@
         a_results[1],
         tail[1],
         r_up,
-        r_down,
+        r_down.T,
         a_results[2],
         tail[4, :n_small],
         tail[2, :n_small],
         p_results[0],
-        p_results[1],
+        p_results[1].T,
         tail[3, :n_small],
         p_results[2],
-        p_results[3],
+        p_results[3].T,
     )
 
 

time: 261 us -> 256 us (0.981)
  local copies, waits for them, and re-layouts: 41.4 us -> 34.4 us
  waiting for transfers between devices: 68.2 us -> 72.1 us
    unnamed x211 -> x172, local copies, waits for them, and re-layouts: 35.6 us -> 28.5 us
    ppermute x54, waiting for transfers between devices: 68.2 us -> 72.1 us  [swap(): return lax.ppermute(value, axis, [(i, i ^ bit) for i in range(size)])]
  transfers between devices with their start and end apart: 54 -> 54, of which waited for: 20 -> 20; matrix products, arithmetic and copies ran while one was open for 3% -> 2% of each run, Pallas kernels for 32% -> 33%
where the time goes in v4:
time: 256 us; the launch traced here: 253 us
  Pallas kernels  105 us (41%)
  waiting for transfers between devices  72.1 us (28%)
  starting transfers between devices  38.7 us (15%)
  local copies, waits for them, and re-layouts  34.4 us (13%)
    pallas_call x13, Pallas kernels, call(): pl.pallas_call(lambda *refs: kernel(*refs[:n_args], *refs[n_all:]), out_s...  79.5 us
    ppermute x54, waiting for transfers between devices, swap(): return lax.ppermute(value, axis, [(i, i ^ bit) for i in range(size)])  72.1 us
    ppermute x54, starting transfers between devices, swap(): return lax.ppermute(value, axis, [(i, i ^ bit) for i in range(size)])  38.7 us
    unnamed x172, local copies, waits for them, and re-layouts  28.5 us
    pallas_call x11, Pallas kernels, combine(): pl.pallas_call(kernel, out_shape=shapes + ([jax.ShapeDtypeStruct(sums[0]....  25.4 us
  transfers between devices with their start and end apart: 54, of which 20 were waited for; matrix products, arithmetic and copies ran while one was open for 2% of the time, Pallas kernels for 33%

profile of v4, /device:TPU:0, one launch (start us, length us, event | category | flops | bytes accessed | tf_op | source)
XLA Modules:
  0.0 252.6 jit_solution(16465732323803180234)
XLA Ops:
  4.7 2.9 %collective-permute-start.1 = (bf16[384,768]{1,0:T(8,128)(2,1)S(1)}, bf16[384,768]{1,0:T(8,128)(2,1)S(1)}, u32[]{:S(2)}, u32[]{:S(2)}) collective-permute-start(bf16[384,768]{1,0:T(8,128)(2,1)S(1)} %get-tuple-element.95.refs_8_), channel_id=1, source_target_pairs={{0,2},{1,3},{2,0},{3,1},{4,6},{5,7},{6,4},{7,5},{8,10},{9,11},{10,... | collective-permute-start | bytes 1769480 | tf_op jit(solution)/shard_map/ppermute | solution.py:535
  11.1 9.9 %collective-permute-done.1.refs_0_ = bf16[384,768]{1,0:T(8,128)(2,1)S(1)} collective-permute-done((bf16[384,768]{1,0:T(8,128)(2,1)S(1)}, bf16[384,768]{1,0:T(8,128)(2,1)S(1)}, u32[]{:S(2)}, u32[]{:S(2)}) %collective-permute-start.1) | collective-permute-done | bytes 589856 | tf_op jit(solution)/shard_map/ppermute | solution.py:535
  25.0 11.6 %collective-permute-done.2.refs_8_.refs_9_ = bf16[384,768]{1,0:T(8,128)(2,1)} collective-permute-done((bf16[384,768]{1,0:T(8,128)(2,1)}, bf16[384,768]{1,0:T(8,128)(2,1)}, u32[]{:S(2)}, u32[]{:S(2)}) %collective-permute-start.2) | collective-permute-done | bytes 589856 | tf_op jit(solution)/shard_map/ppermute | solution.py:535
  41.4 8.9 %shard_map.308 = (f32[256,768]{1,0:T(8,128)S(1)}, bf16[2304,256]{1,0:T(8,128)(2,1)S(1)}, bf16[12,256,256]{2,1,0:T(8,128)(2,1)}, bf16[768,256]{1,0:T(8,128)(2,1)S(1)}) custom-call(s32[4]{0:T(128)S(1)} %pad_add_fusion.refs_0_, bf16[256,768]{1,0:T(8,128)(2,1)S(1)} %copy-done.12, s32[1,256]{1,0:T(1,128)S(1)} %constant_dynamic-slice_fusion.3.refs_2_, ...), custom_call_target="tpu_custom_call" | custom-call | flops 10350000128 | bytes 9049104 | tf_op jit(solution)/shard_map/pallas_call | solution.py:131
  51.9 3.8 %collective-permute-done.7.refs_0_ = bf16[768,384]{1,0:T(8,128)(2,1)} collective-permute-done((bf16[768,384]{1,0:T(8,128)(2,1)}, bf16[768,384]{1,0:T(8,128)(2,1)}, u32[]{:S(2)}, u32[]{:S(2)}) %collective-permute-start.7) | collective-permute-done | bytes 589856 | tf_op jit(solution)/shard_map/ppermute | solution.py:535
  60.9 6.1 %shard_map.310 = (bf16[256,3072]{1,0:T(8,128)(2,1)}, bf16[256,3072]{1,0:T(8,128)(2,1)}) custom-call(s32[4]{0:T(128)S(1)} %pad_add_fusion.refs_0_, f32[256,768]{1,0:T(8,128)S(1)} %copy-done.26, f32[1,768]{1,0:T(1,128)S(1)} %reshape.151.refs_2_.refs_4_, bf16[768,768]{1,0:T(8,128)(2,1)S(1)} %copy-done.47, ...), custom_call_target="tpu_custom_call" | custom-call | flops 6899999744 | bytes 8653840 | tf_op jit(solution)/shard_map/pallas_call | solution.py:131
  66.9 6.1 %collective-permute-done.12.refs_0_ = bf16[384,768]{1,0:T(8,128)(2,1)} collective-permute-done((bf16[384,768]{1,0:T(8,128)(2,1)}, bf16[384,768]{1,0:T(8,128)(2,1)}, u32[]{:S(2)}, u32[]{:S(2)}) %collective-permute-start.12) | collective-permute-done | bytes 589856 | tf_op jit(solution)/shard_map/ppermute | solution.py:535
  73.0 2.2 collective-permute-done.14.refs_8_.refs_17_
  76.4 4.1 %shard_map.313.refs_1_.refs_8_ = bf16[256,768]{1,0:T(8,128)(2,1)S(1)} custom-call(s32[4]{0:T(128)S(1)} %pad_add_fusion.refs_0_, f32[256,768]{1,0:T(8,128)S(1)} %copy-done.27, bf16[256,3072]{1,0:T(8,128)(2,1)} %get-tuple-element.101.refs_1_.refs_2_.refs_3_, bf16[768,768]{1,0:T(8,128)(2,1)S(1)} %copy-done.49, ...), custom_call_target="tpu_custom_call" | custom-call | flops 4600000000 | bytes 7471120 | tf_op jit(solution)/shard_map/pallas_call | solution.py:131
  87.6 18.6 %shard_map.316 = (bf16[768,128]{1,0:T(8,128)(2,1)S(1)}, f32[8,384]{1,0:T(8,128)S(1)}, bf16[6912,128]{1,0:T(8,128)(2,1)}, bf16[6912,128]{1,0:T(8,128)(2,1)}, bf16...) custom-call(s32[4]{0:T(128)S(1)} %pad_add_fusion.refs_0_, bf16[256,768]{1,0:T(8,128)(2,1)S(1)} %copy-done.34, ...), custom_call_target="tpu_custom_call" | custom-call | flops 34500001792 | bytes 9470992 | tf_op jit(solution)/shard_map/pallas_call | solution.py:131
  106.5 3.2 %shard_map.317 = (bf16[2304,128]{1,0:T(8,128)(2,1)S(1)}, bf16[2304,128]{1,0:T(8,128)(2,1)S(1)}, bf16[4608,128]{1,0:T(8,128)(2,1)}) custom-call(s32[4]{0:T(128)S(1)} %pad_add_fusion.refs_0_, s32[768,1]{1,0:T(8,128)S(1)} %add.91.refs_1_, f32[256,768]{1,0:T(8,128)S(1)} %get-tuple-element.106.refs_2_, bf16[256,3072]{1,0:T(8,128)(2,1)S(1)} %copy-done.11), custom_call_target="tpu_custom_call" | custom-call | flops 34500001792 | bytes 4721680 | tf_op jit(solution)/shard_map/pallas_call | solution.py:131
  110.6 2.3 shard_map.318.refs_2_.refs_8_.refs_13_.refs_10_
  116.3 2.5 shard_map.319
  121.9 13.6 %shard_map.320 = (f32[256,768]{1,0:T(8,128)}, f32[1,768]{1,0:T(1,128)S(1)}, bf16[9216,128]{1,0:T(8,128)(2,1)}, bf16[2304,128]{1,0:T(8,128)(2,1)S(1)}, bf16[2304,...) custom-call(s32[4]{0:T(128)S(1)} %pad_add_fusion.refs_0_, s32[768,1]{1,0:T(8,128)S(1)} %add.91.refs_1_, ...), custom_call_target="tpu_custom_call" | custom-call | flops 115000000512 | bytes 18097168 | tf_op jit(solution)/shard_map/pallas_call | solution.py:131
  137.1 9.6 %shard_map.321 = (bf16[2304,256]{1,0:T(8,128)(2,1)S(1)}, bf16[1536,128]{1,0:T(8,128)(2,1)S(1)}, f32[1,768]{1,0:T(1,128)S(1)}) custom-call(s32[4]{0:T(128)S(1)} %pad_add_fusion.refs_0_, bf16[256,768]{1,0:T(8,128)(2,1)S(1)} %copy-done.13, f32[1,768]{1,0:T(1,128)S(1)} %reshape.150.refs_4_.refs_2_.refs_3_, f32[256,768]{1,0:T(8,128)S(1)} %copy-done.28, ...), custom_call_target="tpu_custom_call" | custom-call | flops 1150000000 | bytes 10229776 | tf_op jit(solution)/shard_map/pallas_call | solution.py:131
  149.9 3.0 %shard_map.323 = (bf16[4416,128]{1,0:T(8,128)(2,1)S(1)}, bf16[4416,128]{1,0:T(8,128)(2,1)S(1)}) custom-call(bf16[9216,128]{1,0:T(8,128)(2,1)} %get-tuple-element.120.refs_0_.refs_6_.refs_2_, bf16[2304,128]{1,0:T(8,128)(2,1)} %get-tuple-element.121.refs_1_, bf16[9216,128]{1,0:T(8,128)(2,1)} %copy-done.2, ...), custom_call_target="tpu_custom_call" | custom-call | flops 34500001792 | bytes 7766016 | tf_op jit(solution)/shard_map/pallas_call | solution.py:253
  154.3 6.4 %shard_map.325 = (bf16[10752,128]{1,0:T(8,128)(2,1)}, bf16[2304,128]{1,0:T(8,128)(2,1)S(1)}, bf16[3072,128]{1,0:T(8,128)(2,1)S(1)}, bf16[5376,128]{1,0:T(8,128)(2,1)}) custom-call(s32[4]{0:T(128)S(1)} %pad_add_fusion.refs_0_, s32[768,1]{1,0:T(8,128)S(1)} %add.91.refs_1_, bf16[256,768]{1,0:T(8,128)(2,1)S(1)} %copy-done.13, ...), custom_call_target="tpu_custom_call" | custom-call | flops 115000000512 | bytes 8871952 | tf_op jit(solution)/shard_map/pallas_call | solution.py:131
  164.8 2.1 shard_map.326
  169.7 11.0 %collective-permute-done.27.refs_3_.refs_12_.refs_2_.refs_8_.refs_9_.refs_4_ = bf16[4416,128]{1,0:T(8,128)(2,1)S(1)} collective-permute-done((bf16[4416,128]{1,0:T(8,128)(2,1)S(1)}, bf16[4416,128]{1,0:T(8,128)(2,1)S(1)}, u32[]{:S(2)}, u32[]{:S(2)}) %collective-permute-start.27) | collective-permute-done | bytes 1130528 | tf_op jit(solution)/shard_map/ppermute | solution.py:535
  182.9 2.3 shard_map.327
  191.1 1.9 collective-permute-done.36.refs_5_.refs_2_.refs_4_
  193.0 5.4 %collective-permute-done.35.refs_4_.refs_7_.refs_8_ = bf16[3072,128]{1,0:T(8,128)(2,1)} collective-permute-done((bf16[3072,128]{1,0:T(8,128)(2,1)S(1)}, bf16[3072,128]{1,0:T(8,128)(2,1)}, u32[]{:S(2)}, u32[]{:S(2)}) %collective-permute-start.35) | collective-permute-done | bytes 786464 | tf_op jit(solution)/shard_map/ppermute | solution.py:535
  200.3 2.9 %shard_map.329 = (bf16[1536,128]{1,0:T(8,128)(2,1)S(1)}, bf16[1536,128]{1,0:T(8,128)(2,1)S(1)}, bf16[1008,128]{1,0:T(8,128)(2,1)}, f32[8,384]{1,0:T(8,128)S(1)}) custom-call(f32[8,384]{1,0:T(8,128)S(1)} %copy-done.43, f32[8,384]{1,0:T(8,128)S(1)} %collective-permute-done.33.refs_1_, bf16[10752,128]{1,0:T(8,128)(2,1)} %get-tuple-element.135.refs_0_.refs_2_, ...), custom_call_target="tpu_custom_call" | custom-call | flops 3449999872 | bytes 4497408 | tf_op jit(solution)/shard_map/pallas_call | solution.py:253
  208.1 2.6 %collective-permute-start.41 = (bf16[1008,128]{1,0:T(8,128)(2,1)}, bf16[1008,128]{1,0:T(8,128)(2,1)S(1)}, u32[]{:S(2)}, u32[]{:S(2)}) collective-permute-start(bf16[1008,128]{1,0:T(8,128)(2,1)} %get-tuple-element.151), channel_id=1, source_target_pairs={{0,16},{4,20},{8,24},{12,28},{16,0},{20,4},{24,8},{28,12},{1,17},{... | collective-permute-start | bytes 774152 | tf_op jit(solution)/shard_map/ppermute | solution.py:535
  210.7 8.3 %collective-permute-done.44.refs_10_.refs_6_ = bf16[1152,128]{1,0:T(8,128)(2,1)S(1)} collective-permute-done((bf16[1152,128]{1,0:T(8,128)(2,1)S(1)}, bf16[1152,128]{1,0:T(8,128)(2,1)S(1)}, u32[]{:S(2)}, u32[]{:S(2)}) %collective-permute-start.44) | collective-permute-done | bytes 294944 | tf_op jit(solution)/shard_map/ppermute | solution.py:535
  219.1 2.6 %shard_map.332 = (bf16[1344,128]{1,0:T(8,128)(2,1)S(1)}, bf16[576,128]{1,0:T(8,128)(2,1)}) custom-call(bf16[10752,128]{1,0:T(8,128)(2,1)} %get-tuple-element.135.refs_0_.refs_2_, bf16[5376,128]{1,0:T(8,128)(2,1)} %collective-permute-done.34.refs_3_.refs_1_, bf16[2304,128]{1,0:T(8,128)(2,1)} %collective-permute-done.36.refs_5_.refs_2_.refs_4_, ...), custom_call_target="tpu_custom_call" | custom-call | flops 3449999872 | bytes 2605056 | tf_op jit(solution)/shard_map/pallas_call | solution.py:253
  226.7 2.5 shard_map.334
  229.2 2.5 collective-permute-start.45
  239.6 2.2 shard_map.336
  242.8 2.0 shard_map.337.refs_5_
  244.8 2.4 shard_map.339.refs_10_
  248.4 2.4 shard_map.340
  (309 shorter events, 83.1 us)
Async XLA Ops:
  4.7 16.3 %collective-permute-start.1 = (bf16[384,768]{1,0:T(8,128)(2,1)S(1)}, bf16[384,768]{1,0:T(8,128)(2,1)S(1)}, u32[]{:S(2)}, u32[]{:S(2)}) collective-permute-start(bf16[384,768]{1,0:T(8,128)(2,1)S(1)} %get-tuple-element.95.refs_8_), channel_id=1, source_target_pairs={{0,2},{1,3},{2,0},{3,1},{4,6},{5,7},{6,4},{7,5},{8,10},{9,11},{10,... | collective-permute-start | bytes 1769480 | tf_op jit(solution)/shard_map/ppermute | solution.py:535
  7.6 30.6 %collective-permute-start = (bf16[768,768]{1,0:T(8,128)(2,1)}, bf16[768,768]{1,0:T(8,128)(2,1)}, u32[]{:S(2)}, u32[]{:S(2)}) collective-permute-start(bf16[768,768]{1,0:T(8,128)(2,1)} %get-tuple-element.94.refs_5_.refs_6_), channel_id=1, source_target_pairs={{0,1},{1,0},{2,3},{3,2},{4,5},{5,4},{6,7},{7,6},{8,9},{9,8},{10,11... | collective-permute-start | bytes 3538952 | tf_op jit(solution)/shard_map/ppermute | solution.py:535
  21.8 14.8 %collective-permute-start.2 = (bf16[384,768]{1,0:T(8,128)(2,1)}, bf16[384,768]{1,0:T(8,128)(2,1)}, u32[]{:S(2)}, u32[]{:S(2)}) collective-permute-start(bf16[384,768]{1,0:T(8,128)(2,1)} %get-tuple-element.98.refs_7_.refs_8_), channel_id=1, source_target_pairs={{0,4},{4,0},{8,12},{12,8},{16,20},{20,16},{24,28},{28,24},{1,5},{5... | collective-permute-start | bytes 1769480 | tf_op jit(solution)/shard_map/ppermute | solution.py:535
  23.5 14.6 %collective-permute-start.6 = (bf16[768,384]{1,0:T(8,128)(2,1)}, bf16[768,384]{1,0:T(8,128)(2,1)}, u32[]{:S(2)}, u32[]{:S(2)}) collective-permute-start(bf16[768,384]{1,0:T(8,128)(2,1)} %get-tuple-element.100), channel_id=1, source_target_pairs={{0,2},{1,3},{2,0},{3,1},{4,6},{5,7},{6,4},{7,5},{8,10},{9,11},{10,... | collective-permute-start | bytes 1769480 | tf_op jit(solution)/shard_map/ppermute | solution.py:535
  25.0 14.7 %collective-permute-start.3 = (bf16[384,768]{1,0:T(8,128)(2,1)}, bf16[384,768]{1,0:T(8,128)(2,1)}, u32[]{:S(2)}, u32[]{:S(2)}) collective-permute-start(bf16[384,768]{1,0:T(8,128)(2,1)} %get-tuple-element.98.refs_7_.refs_8_), channel_id=1, source_target_pairs={{0,1},{1,0},{2,3},{3,2},{4,5},{5,4},{6,7},{7,6},{8,9},{9,8},{10,11... | collective-permute-start | bytes 1769480 | tf_op jit(solution)/shard_map/ppermute | solution.py:535
  36.6 20.4 %collective-permute-start.5 = (bf16[768,768]{1,0:T(8,128)(2,1)}, bf16[768,768]{1,0:T(8,128)(2,1)}, u32[]{:S(2)}, u32[]{:S(2)}) collective-permute-start(bf16[768,768]{1,0:T(8,128)(2,1)} %refs_6_.3), channel_id=1, source_target_pairs={{0,1},{1,0},{2,3},{3,2},{4,5},{5,4},{6,7},{7,6},{8,9},{9,8},{10,11... | collective-permute-start | bytes 3538952 | tf_op jit(solution)/shard_map/ppermute | solution.py:535
  38.1 17.7 %collective-permute-start.15 = (bf16[1344,384]{1,0:T(8,128)(2,1)S(1)}, bf16[1344,384]{1,0:T(8,128)(2,1)}, u32[]{:S(2)}, u32[]{:S(2)}) collective-permute-start(bf16[1344,384]{1,0:T(8,128)(2,1)S(1)} %copy-done.4), channel_id=1, source_target_pairs={{0,1},{1,0},{2,3},{3,2},{4,5},{5,4},{6,7},{7,6},{8,9},{9,8},{10,11... | collective-permute-start | bytes 3096584 | tf_op jit(solution)/shard_map/ppermute | solution.py:535
  38.2 18.2 %collective-permute-start.11 = (bf16[384,768]{1,0:T(8,128)(2,1)}, bf16[384,768]{1,0:T(8,128)(2,1)}, u32[]{:S(2)}, u32[]{:S(2)}) collective-permute-start(bf16[384,768]{1,0:T(8,128)(2,1)} %shard_map.311), channel_id=1, source_target_pairs={{0,2},{1,3},{2,0},{3,1},{4,6},{5,7},{6,4},{7,5},{8,10},{9,11},{10,... | collective-permute-start | bytes 1769480 | tf_op jit(solution)/shard_map/ppermute | solution.py:535
  39.7 17.3 %collective-permute-start.8 = (bf16[768,384]{1,0:T(8,128)(2,1)}, bf16[768,384]{1,0:T(8,128)(2,1)}, u32[]{:S(2)}, u32[]{:S(2)}) collective-permute-start(bf16[768,384]{1,0:T(8,128)(2,1)} %collective-permute-done.6.refs_5_.refs_1_.refs_8_), channel_id=1, source_target_pairs={{0,1},{1,0},{2,3},{3,2},{4,5},{5,4},{6,7},{7,6},{8,9},{9,8},{10,11... | collective-permute-start | bytes 1769480 | tf_op jit(solution)/shard_map/ppermute | solution.py:535
  39.8 15.9 %collective-permute-start.7 = (bf16[768,384]{1,0:T(8,128)(2,1)}, bf16[768,384]{1,0:T(8,128)(2,1)}, u32[]{:S(2)}, u32[]{:S(2)}) collective-permute-start(bf16[768,384]{1,0:T(8,128)(2,1)} %collective-permute-done.6.refs_5_.refs_1_.refs_8_), channel_id=1, source_target_pairs={{0,4},{4,0},{8,12},{12,8},{16,20},{20,16},{24,28},{28,24},{1,5},{5... | collective-permute-start | bytes 1769480 | tf_op jit(solution)/shard_map/ppermute | solution.py:535
  55.8 17.3 %collective-permute-start.10 = (bf16[768,768]{1,0:T(8,128)(2,1)}, bf16[768,768]{1,0:T(8,128)(2,1)}, u32[]{:S(2)}, u32[]{:S(2)}) collective-permute-start(bf16[768,768]{1,0:T(8,128)(2,1)} %refs_12_.1), channel_id=1, source_target_pairs={{0,1},{1,0},{2,3},{3,2},{4,5},{5,4},{6,7},{7,6},{8,9},{9,8},{10,11... | collective-permute-start | bytes 3538952 | tf_op jit(solution)/shard_map/ppermute | solution.py:535
  56.4 25.0 %collective-permute-start.16 = (bf16[1344,384]{1,0:T(8,128)(2,1)}, bf16[1344,384]{1,0:T(8,128)(2,1)S(1)}, u32[]{:S(2)}, u32[]{:S(2)}) collective-permute-start(bf16[1344,384]{1,0:T(8,128)(2,1)} %shard_map.314.refs_10_), channel_id=1, source_target_pairs={{0,2},{1,3},{2,0},{3,1},{4,6},{5,7},{6,4},{7,5},{8,10},{9,11},{10,... | collective-permute-start | bytes 3096584 | tf_op jit(solution)/shard_map/ppermute | solution.py:535
  57.0 16.1 %collective-permute-start.13 = (bf16[384,768]{1,0:T(8,128)(2,1)}, bf16[384,768]{1,0:T(8,128)(2,1)}, u32[]{:S(2)}, u32[]{:S(2)}) collective-permute-start(bf16[384,768]{1,0:T(8,128)(2,1)} %collective-permute-done.11.refs_5_.refs_1_.refs_14_), channel_id=1, source_target_pairs={{0,1},{1,0},{2,3},{3,2},{4,5},{5,4},{6,7},{7,6},{8,9},{9,8},{10,11... | collective-permute-start | bytes 1769480 | tf_op jit(solution)/shard_map/ppermute | solution.py:535
  57.0 16.1 %collective-permute-start.12 = (bf16[384,768]{1,0:T(8,128)(2,1)}, bf16[384,768]{1,0:T(8,128)(2,1)}, u32[]{:S(2)}, u32[]{:S(2)}) collective-permute-start(bf16[384,768]{1,0:T(8,128)(2,1)} %collective-permute-done.11.refs_5_.refs_1_.refs_14_), channel_id=1, source_target_pairs={{0,4},{4,0},{8,12},{12,8},{16,20},{20,16},{24,28},{28,24},{1,5},{5... | collective-permute-start | bytes 1769480 | tf_op jit(solution)/shard_map/ppermute | solution.py:535
  114.4 35.5 %collective-permute-start.25 = (bf16[4608,128]{1,0:T(8,128)(2,1)}, bf16[4608,128]{1,0:T(8,128)(2,1)}, u32[]{:S(2)}, u32[]{:S(2)}) collective-permute-start(bf16[4608,128]{1,0:T(8,128)(2,1)} %get-tuple-element.122), channel_id=1, source_target_pairs={{0,1},{1,0},{2,3},{3,2},{4,5},{5,4},{6,7},{7,6},{8,9},{9,8},{10,11... | collective-permute-start | bytes 3538952 | tf_op jit(solution)/shard_map/ppermute | solution.py:535
  118.9 28.6 %collective-permute-start.22 = (bf16[4224,128]{1,0:T(8,128)(2,1)S(1)}, bf16[4224,128]{1,0:T(8,128)(2,1)S(1)}, u32[]{:S(2)}, u32[]{:S(2)}) collective-permute-start(bf16[4224,128]{1,0:T(8,128)(2,1)S(1)} %get-tuple-element.110.refs_19_), channel_id=1, source_target_pairs={{0,4},{4,0},{8,12},{12,8},{16,20},{20,16},{24,28},{28,24},{1,5},{5... | collective-permute-start | bytes 3244040 | tf_op jit(solution)/shard_map/ppermute | solution.py:535
  120.4 27.8 %collective-permute-start.21 = (bf16[4608,128]{1,0:T(8,128)(2,1)S(1)}, bf16[4608,128]{1,0:T(8,128)(2,1)S(1)}, u32[]{:S(2)}, u32[]{:S(2)}) collective-permute-start(bf16[4608,128]{1,0:T(8,128)(2,1)S(1)} %get-tuple-element.109.refs_18_), channel_id=1, source_target_pairs={{0,2},{1,3},{2,0},{3,1},{4,6},{5,7},{6,4},{7,5},{8,10},{9,11},{10,... | collective-permute-start | bytes 3538952 | tf_op jit(solution)/shard_map/ppermute | solution.py:535
  147.3 20.9 %collective-permute-start.26 = (bf16[4608,128]{1,0:T(8,128)(2,1)}, bf16[4608,128]{1,0:T(8,128)(2,1)}, u32[]{:S(2)}, u32[]{:S(2)}) collective-permute-start(bf16[4608,128]{1,0:T(8,128)(2,1)} %get-tuple-element.129), channel_id=1, source_target_pairs={{0,1},{1,0},{2,3},{3,2},{4,5},{5,4},{6,7},{7,6},{8,9},{9,8},{10,11... | collective-permute-start | bytes 3538952 | tf_op jit(solution)/shard_map/ppermute | solution.py:535
  152.9 27.8 %collective-permute-start.27 = (bf16[4416,128]{1,0:T(8,128)(2,1)S(1)}, bf16[4416,128]{1,0:T(8,128)(2,1)S(1)}, u32[]{:S(2)}, u32[]{:S(2)}) collective-permute-start(bf16[4416,128]{1,0:T(8,128)(2,1)S(1)} %get-tuple-element.125.refs_3_.refs_12_), channel_id=1, source_target_pairs={{0,2},{1,3},{2,0},{3,1},{4,6},{5,7},{6,4},{7,5},{8,10},{9,11},{10,... | collective-permute-start | bytes 3391496 | tf_op jit(solution)/shard_map/ppermute | solution.py:535
  153.7 27.8 %collective-permute-start.28 = (bf16[4416,128]{1,0:T(8,128)(2,1)S(1)}, bf16[4416,128]{1,0:T(8,128)(2,1)S(1)}, u32[]{:S(2)}, u32[]{:S(2)}) collective-permute-start(bf16[4416,128]{1,0:T(8,128)(2,1)S(1)} %get-tuple-element.126.refs_4_.refs_13_), channel_id=1, source_target_pairs={{0,4},{4,0},{8,12},{12,8},{16,20},{20,16},{24,28},{28,24},{1,5},{5... | collective-permute-start | bytes 3391496 | tf_op jit(solution)/shard_map/ppermute | solution.py:535
  162.8 27.3 %collective-permute-start.34 = (bf16[5376,128]{1,0:T(8,128)(2,1)}, bf16[5376,128]{1,0:T(8,128)(2,1)}, u32[]{:S(2)}, u32[]{:S(2)}) collective-permute-start(bf16[5376,128]{1,0:T(8,128)(2,1)} %get-tuple-element.143), channel_id=1, source_target_pairs={{0,1},{1,0},{2,3},{3,2},{4,5},{5,4},{6,7},{7,6},{8,9},{9,8},{10,11... | collective-permute-start | bytes 4128776 | tf_op jit(solution)/shard_map/ppermute | solution.py:535
  166.9 26.1 %collective-permute-start.36 = (bf16[2304,128]{1,0:T(8,128)(2,1)S(1)}, bf16[2304,128]{1,0:T(8,128)(2,1)}, u32[]{:S(2)}, u32[]{:S(2)}) collective-permute-start(bf16[2304,128]{1,0:T(8,128)(2,1)S(1)} %get-tuple-element.138.refs_10_), channel_id=1, source_target_pairs={{0,2},{1,3},{2,0},{3,1},{4,6},{5,7},{6,4},{7,5},{8,10},{9,11},{10,... | collective-permute-start | bytes 1769480 | tf_op jit(solution)/shard_map/ppermute | solution.py:535
  168.2 30.3 %collective-permute-start.35 = (bf16[3072,128]{1,0:T(8,128)(2,1)S(1)}, bf16[3072,128]{1,0:T(8,128)(2,1)}, u32[]{:S(2)}, u32[]{:S(2)}) collective-permute-start(bf16[3072,128]{1,0:T(8,128)(2,1)S(1)} %get-tuple-element.139.refs_11_), channel_id=1, source_target_pairs={{0,4},{4,0},{8,12},{12,8},{16,20},{20,16},{24,28},{28,24},{1,5},{5... | collective-permute-start | bytes 2359304 | tf_op jit(solution)/shard_map/ppermute | solution.py:535
  186.6 12.9 %collective-permute-start.37 = (bf16[2016,128]{1,0:T(8,128)(2,1)S(1)}, bf16[2016,128]{1,0:T(8,128)(2,1)}, u32[]{:S(2)}, u32[]{:S(2)}) collective-permute-start(bf16[2016,128]{1,0:T(8,128)(2,1)S(1)} %get-tuple-element.144), channel_id=1, source_target_pairs={{0,8},{4,12},{8,0},{12,4},{16,24},{20,28},{24,16},{28,20},{1,9},{5... | collective-permute-start | bytes 1548296 | tf_op jit(solution)/shard_map/ppermute | solution.py:535
  189.6 15.0 %collective-permute-start.31 = (bf16[1152,128]{1,0:T(8,128)(2,1)}, bf16[1152,128]{1,0:T(8,128)(2,1)S(1)}, u32[]{:S(2)}, u32[]{:S(2)}) collective-permute-start(bf16[1152,128]{1,0:T(8,128)(2,1)} %copy-done.17), channel_id=1, source_target_pairs={{0,4},{4,0},{8,12},{12,8},{16,20},{20,16},{24,28},{28,24},{1,5},{5... | collective-permute-start | bytes 884744 | tf_op jit(solution)/shard_map/ppermute | solution.py:535
  190.1 14.5 %collective-permute-start.32 = (bf16[1152,128]{1,0:T(8,128)(2,1)}, bf16[1152,128]{1,0:T(8,128)(2,1)S(1)}, u32[]{:S(2)}, u32[]{:S(2)}) collective-permute-start(bf16[1152,128]{1,0:T(8,128)(2,1)} %copy-done.16), channel_id=1, source_target_pairs={{0,2},{1,3},{2,0},{3,1},{4,6},{5,7},{6,4},{7,5},{8,10},{9,11},{10,... | collective-permute-start | bytes 884744 | tf_op jit(solution)/shard_map/ppermute | solution.py:535
  203.2 15.9 %collective-permute-start.43 = (bf16[1536,128]{1,0:T(8,128)(2,1)S(1)}, bf16[1536,128]{1,0:T(8,128)(2,1)S(1)}, u32[]{:S(2)}, u32[]{:S(2)}) collective-permute-start(bf16[1536,128]{1,0:T(8,128)(2,1)S(1)} %get-tuple-element.145.refs_6_), channel_id=1, source_target_pairs={{0,2},{1,3},{2,0},{3,1},{4,6},{5,7},{6,4},{7,5},{8,10},{9,11},{10,... | collective-permute-start | bytes 1179656 | tf_op jit(solution)/shard_map/ppermute | solution.py:535
  203.7 15.4 %collective-permute-start.42 = (bf16[1536,128]{1,0:T(8,128)(2,1)S(1)}, bf16[1536,128]{1,0:T(8,128)(2,1)S(1)}, u32[]{:S(2)}, u32[]{:S(2)}) collective-permute-start(bf16[1536,128]{1,0:T(8,128)(2,1)S(1)} %get-tuple-element.146.refs_7_), channel_id=1, source_target_pairs={{0,4},{4,0},{8,12},{12,8},{16,20},{20,16},{24,28},{28,24},{1,5},{5... | collective-permute-start | bytes 1179656 | tf_op jit(solution)/shard_map/ppermute | solution.py:535
  206.1 13.0 %collective-permute-start.44 = (bf16[1152,128]{1,0:T(8,128)(2,1)S(1)}, bf16[1152,128]{1,0:T(8,128)(2,1)S(1)}, u32[]{:S(2)}, u32[]{:S(2)}) collective-permute-start(bf16[1152,128]{1,0:T(8,128)(2,1)S(1)} %shard_map.330.refs_2_.refs_13_), channel_id=1, source_target_pairs={{0,8},{4,12},{8,0},{12,4},{16,24},{20,28},{24,16},{28,20},{1,9},{5... | collective-permute-start | bytes 884744 | tf_op jit(solution)/shard_map/ppermute | solution.py:535
  207.7 18.0 %collective-permute-start.40 = (f32[8,384]{1,0:T(8,128)S(1)}, f32[8,384]{1,0:T(8,128)S(1)}, u32[]{:S(2)}, u32[]{:S(2)}) collective-permute-start(f32[8,384]{1,0:T(8,128)S(1)} %get-tuple-element.149.refs_0_), channel_id=1, source_target_pairs={{0,8},{4,12},{8,0},{12,4},{16,24},{20,28},{24,16},{28,20},{1,9},{5... | collective-permute-start | bytes 36872 | tf_op jit(solution)/shard_map/ppermute | solution.py:535
  208.1 15.3 %collective-permute-start.41 = (bf16[1008,128]{1,0:T(8,128)(2,1)}, bf16[1008,128]{1,0:T(8,128)(2,1)S(1)}, u32[]{:S(2)}, u32[]{:S(2)}) collective-permute-start(bf16[1008,128]{1,0:T(8,128)(2,1)} %get-tuple-element.151), channel_id=1, source_target_pairs={{0,16},{4,20},{8,24},{12,28},{16,0},{20,4},{24,8},{28,12},{1,17},{... | collective-permute-start | bytes 774152 | tf_op jit(solution)/shard_map/ppermute | solution.py:535
  221.7 12.3 %collective-permute-start.46 = (bf16[1344,128]{1,0:T(8,128)(2,1)S(1)}, bf16[1344,128]{1,0:T(8,128)(2,1)}, u32[]{:S(2)}, u32[]{:S(2)}) collective-permute-start(bf16[1344,128]{1,0:T(8,128)(2,1)S(1)} %get-tuple-element.152.refs_2_.refs_12_), channel_id=1, source_target_pairs={{0,8},{4,12},{8,0},{12,4},{16,24},{20,28},{24,16},{28,20},{1,9},{5... | collective-permute-start | bytes 1032200 | tf_op jit(solution)/shard_map/ppermute | solution.py:535
  (108 other events, 492.0 us)

commit v5 on v4

--- a/solution.py
+++ b/solution.py
@@ -746,7 +746,7 @@
     p_z = (p_own, p_seg, p_got, p_then)
     d_z = (d_own, d_seg, d_got, d_then)
     (*u_send, z_send), _, (u_then,) = stage(
-        [second(u_own, u_seg, u_got)], a_send, 3, (), [kept(*p_z, 2, 4) + kept(*d_z, 2, 4)]
+        [second(u_own, u_seg, u_got)], a_send, 12, (), [kept(*p_z, 2, 4) + kept(*d_z, 2, 4)]
     )
     (stats,) = gate([stats], u_send)
     u_z = (u_own, u_seg, u_got, u_then)
@@ -777,7 +777,7 @@
 
     filler = [[(a_got[0][0], 0, a_seg.b - a_seg.a)]]
     (*a_send, z_send, stats), _, (a_then, _) = stage(
-        [second(a_own, a_seg, a_got), ([], filler)], u_send, 3, (stats, stats_got), [last(p_z, p_one, 1) + last(d_z, d_one, 1)]
+        [second(a_own, a_seg, a_got), ([], filler)], u_send, 12, (stats, stats_got), [last(p_z, p_one, 1) + last(d_z, d_one, 1)]
     )
     a_z = (a_own, a_seg, a_got, a_then)
     z_got = swap(z_send, "dp", 4)
@@ -785,7 +785,8 @@
     u_one, stats_got = (swap(z_send, "dp", 2), 0), swap(stats, "dp", 2)
     predicted, predicted_x = gate([predicted, predicted_x], [z_send])
     predicted_c, predicted_xc = swap(predicted, "mp", 1), swap(predicted_x, "mp", 1)
-    z_send, z_send_u = combine([kept(*a_z, 2, 4), last(u_z, u_one, 1)], [z_send], 3)
+    (z_send,) = combine([kept(*a_z, 2, 4)], [z_send], 3)
+    (z_send_u,) = combine([last(u_z, u_one, 1)], [z_send], 3)
     a_one, u_two = (swap(z_send, "dp", 2), 0), (swap(z_send_u, "dp", 4), 0)
     d_input, p_two_array = gate([d_input, z_got], [z_send])
     p_two, d_two = (p_two_array, 0), (p_two_array, p_rows)

time: 256 us -> 256 us (level)
  waiting for transfers between devices: 72.1 us -> 68.9 us
    ppermute x54, waiting for transfers between devices: 72.1 us -> 68.9 us  [swap(): return lax.ppermute(value, axis, [(i, i ^ bit) for i in range(size)])]
    unnamed x172 -> x182, local copies, waits for them, and re-layouts: 28.5 us -> 29.9 us
    pallas_call x11 -> x12, Pallas kernels: 25.4 us -> 25.1 us  [combine(): pl.pallas_call(kernel, out_shape=shapes + ([jax.ShapeDtypeStruct(sums[0]....]
  transfers between devices with their start and end apart: 54 -> 54, of which waited for: 20 -> 21; matrix products, arithmetic and copies ran while one was open for 2% -> 2% of each run, Pallas kernels for 33% -> 32%
where the time goes in v5:
time: 256 us; the launch traced here: 252 us
  Pallas kernels  104 us (41%)
  waiting for transfers between devices  68.9 us (27%)
  starting transfers between devices  40.9 us (16%)
  local copies, waits for them, and re-layouts  35.6 us (14%)
    pallas_call x13, Pallas kernels, call(): pl.pallas_call(lambda *refs: kernel(*refs[:n_args], *refs[n_all:]), out_s...  79.3 us
    ppermute x54, waiting for transfers between devices, swap(): return lax.ppermute(value, axis, [(i, i ^ bit) for i in range(size)])  68.9 us
    ppermute x54, starting transfers between devices, swap(): return lax.ppermute(value, axis, [(i, i ^ bit) for i in range(size)])  40.9 us
    unnamed x182, local copies, waits for them, and re-layouts  29.9 us
    pallas_call x12, Pallas kernels, combine(): pl.pallas_call(kernel, out_shape=shapes + ([jax.ShapeDtypeStruct(sums[0]....  25.1 us
  transfers between devices with their start and end apart: 54, of which 21 were waited for; matrix products, arithmetic and copies ran while one was open for 2% of the time, Pallas kernels for 32%

profile of v5, /device:TPU:0, one launch (start us, length us, event | category | flops | bytes accessed | tf_op | source)
XLA Modules:
  0.0 252.3 jit_solution(8181811010584253416)
XLA Ops:
  4.7 2.9 %collective-permute-start.1 = (bf16[384,768]{1,0:T(8,128)(2,1)S(1)}, bf16[384,768]{1,0:T(8,128)(2,1)S(1)}, u32[]{:S(2)}, u32[]{:S(2)}) collective-permute-start(bf16[384,768]{1,0:T(8,128)(2,1)S(1)} %get-tuple-element.93.refs_8_), channel_id=1, source_target_pairs={{0,2},{1,3},{2,0},{3,1},{4,6},{5,7},{6,4},{7,5},{8,10},{9,11},{10,... | collective-permute-start | bytes 1769480 | tf_op jit(solution)/shard_map/ppermute | solution.py:535
  11.1 9.9 %collective-permute-done.1.refs_0_ = bf16[384,768]{1,0:T(8,128)(2,1)S(1)} collective-permute-done((bf16[384,768]{1,0:T(8,128)(2,1)S(1)}, bf16[384,768]{1,0:T(8,128)(2,1)S(1)}, u32[]{:S(2)}, u32[]{:S(2)}) %collective-permute-start.1) | collective-permute-done | bytes 589856 | tf_op jit(solution)/shard_map/ppermute | solution.py:535
  25.1 11.6 %collective-permute-done.2.refs_8_.refs_9_ = bf16[384,768]{1,0:T(8,128)(2,1)} collective-permute-done((bf16[384,768]{1,0:T(8,128)(2,1)}, bf16[384,768]{1,0:T(8,128)(2,1)}, u32[]{:S(2)}, u32[]{:S(2)}) %collective-permute-start.2) | collective-permute-done | bytes 589856 | tf_op jit(solution)/shard_map/ppermute | solution.py:535
  41.4 8.9 %shard_map.308 = (f32[256,768]{1,0:T(8,128)S(1)}, bf16[2304,256]{1,0:T(8,128)(2,1)S(1)}, bf16[12,256,256]{2,1,0:T(8,128)(2,1)}, bf16[768,256]{1,0:T(8,128)(2,1)S(1)}) custom-call(s32[4]{0:T(128)S(1)} %pad_add_fusion.refs_0_, bf16[256,768]{1,0:T(8,128)(2,1)S(1)} %copy-done.11, s32[1,256]{1,0:T(1,128)S(1)} %constant_dynamic-slice_fusion.3.refs_2_, ...), custom_call_target="tpu_custom_call" | custom-call | flops 10350000128 | bytes 9049104 | tf_op jit(solution)/shard_map/pallas_call | solution.py:131
  52.0 3.8 %collective-permute-done.7.refs_0_ = bf16[768,384]{1,0:T(8,128)(2,1)} collective-permute-done((bf16[768,384]{1,0:T(8,128)(2,1)}, bf16[768,384]{1,0:T(8,128)(2,1)}, u32[]{:S(2)}, u32[]{:S(2)}) %collective-permute-start.7) | collective-permute-done | bytes 589856 | tf_op jit(solution)/shard_map/ppermute | solution.py:535
  60.9 6.1 %shard_map.310 = (bf16[256,3072]{1,0:T(8,128)(2,1)}, bf16[256,3072]{1,0:T(8,128)(2,1)}) custom-call(s32[4]{0:T(128)S(1)} %pad_add_fusion.refs_0_, f32[256,768]{1,0:T(8,128)S(1)} %copy-done.21, f32[1,768]{1,0:T(1,128)S(1)} %reshape.151.refs_2_.refs_4_, bf16[768,768]{1,0:T(8,128)(2,1)S(1)} %copy-done.45, ...), custom_call_target="tpu_custom_call" | custom-call | flops 6899999744 | bytes 8653840 | tf_op jit(solution)/shard_map/pallas_call | solution.py:131
  67.0 6.0 %collective-permute-done.12.refs_0_ = bf16[384,768]{1,0:T(8,128)(2,1)} collective-permute-done((bf16[384,768]{1,0:T(8,128)(2,1)}, bf16[384,768]{1,0:T(8,128)(2,1)}, u32[]{:S(2)}, u32[]{:S(2)}) %collective-permute-start.12) | collective-permute-done | bytes 589856 | tf_op jit(solution)/shard_map/ppermute | solution.py:535
  73.1 2.2 collective-permute-done.14.refs_8_.refs_17_
  76.4 4.1 %shard_map.313.refs_1_.refs_8_ = bf16[256,768]{1,0:T(8,128)(2,1)S(1)} custom-call(s32[4]{0:T(128)S(1)} %pad_add_fusion.refs_0_, f32[256,768]{1,0:T(8,128)S(1)} %copy-done.22, bf16[256,3072]{1,0:T(8,128)(2,1)} %get-tuple-element.99.refs_1_.refs_2_.refs_3_, bf16[768,768]{1,0:T(8,128)(2,1)S(1)} %copy-done.47, ...), custom_call_target="tpu_custom_call" | custom-call | flops 4600000000 | bytes 7471120 | tf_op jit(solution)/shard_map/pallas_call | solution.py:131
  87.6 18.7 %shard_map.316 = (bf16[768,128]{1,0:T(8,128)(2,1)S(1)}, f32[8,384]{1,0:T(8,128)S(1)}, bf16[6912,128]{1,0:T(8,128)(2,1)}, bf16[6912,128]{1,0:T(8,128)(2,1)}, bf16...) custom-call(s32[4]{0:T(128)S(1)} %pad_add_fusion.refs_0_, bf16[256,768]{1,0:T(8,128)(2,1)S(1)} %copy-done.28, ...), custom_call_target="tpu_custom_call" | custom-call | flops 34500001792 | bytes 9470992 | tf_op jit(solution)/shard_map/pallas_call | solution.py:131
  106.6 3.2 %shard_map.317 = (bf16[2304,128]{1,0:T(8,128)(2,1)S(1)}, bf16[2304,128]{1,0:T(8,128)(2,1)S(1)}, bf16[4608,128]{1,0:T(8,128)(2,1)}) custom-call(s32[4]{0:T(128)S(1)} %pad_add_fusion.refs_0_, s32[768,1]{1,0:T(8,128)S(1)} %add.91.refs_1_, f32[256,768]{1,0:T(8,128)S(1)} %get-tuple-element.104.refs_2_, bf16[256,3072]{1,0:T(8,128)(2,1)S(1)} %copy-done.10), custom_call_target="tpu_custom_call" | custom-call | flops 34500001792 | bytes 4721680 | tf_op jit(solution)/shard_map/pallas_call | solution.py:131
  110.7 2.3 shard_map.318.refs_2_.refs_8_.refs_13_.refs_10_
  116.3 2.5 shard_map.319
  121.8 13.4 %shard_map.320 = (f32[256,768]{1,0:T(8,128)}, f32[1,768]{1,0:T(1,128)S(1)}, bf16[9216,128]{1,0:T(8,128)(2,1)}, bf16[2304,128]{1,0:T(8,128)(2,1)S(1)}, bf16[2304,...) custom-call(s32[4]{0:T(128)S(1)} %pad_add_fusion.refs_0_, s32[768,1]{1,0:T(8,128)S(1)} %add.91.refs_1_, ...), custom_call_target="tpu_custom_call" | custom-call | flops 115000000512 | bytes 18097168 | tf_op jit(solution)/shard_map/pallas_call | solution.py:131
  136.9 9.8 %shard_map.321 = (bf16[2304,256]{1,0:T(8,128)(2,1)S(1)}, bf16[1536,128]{1,0:T(8,128)(2,1)S(1)}, f32[1,768]{1,0:T(1,128)S(1)}) custom-call(s32[4]{0:T(128)S(1)} %pad_add_fusion.refs_0_, bf16[256,768]{1,0:T(8,128)(2,1)S(1)} %copy-done.12, f32[1,768]{1,0:T(1,128)S(1)} %reshape.150.refs_4_.refs_2_.refs_3_, f32[256,768]{1,0:T(8,128)S(1)} %copy-done.23, ...), custom_call_target="tpu_custom_call" | custom-call | flops 1150000000 | bytes 10229776 | tf_op jit(solution)/shard_map/pallas_call | solution.py:131
  150.0 3.0 %shard_map.323 = (bf16[4416,128]{1,0:T(8,128)(2,1)S(1)}, bf16[4416,128]{1,0:T(8,128)(2,1)S(1)}) custom-call(bf16[9216,128]{1,0:T(8,128)(2,1)} %get-tuple-element.118.refs_0_.refs_2_, bf16[2304,128]{1,0:T(8,128)(2,1)} %get-tuple-element.119.refs_1_, bf16[9216,128]{1,0:T(8,128)(2,1)} %copy-done.69, ...), custom_call_target="tpu_custom_call" | custom-call | flops 34500001792 | bytes 7766016 | tf_op jit(solution)/shard_map/pallas_call | solution.py:253
  154.4 6.3 %shard_map.325 = (bf16[10752,128]{1,0:T(8,128)(2,1)}, bf16[2304,128]{1,0:T(8,128)(2,1)S(1)}, bf16[3072,128]{1,0:T(8,128)(2,1)S(1)}, bf16[5376,128]{1,0:T(8,128)(2,1)}) custom-call(s32[4]{0:T(128)S(1)} %pad_add_fusion.refs_0_, s32[768,1]{1,0:T(8,128)S(1)} %add.91.refs_1_, bf16[256,768]{1,0:T(8,128)(2,1)S(1)} %copy-done.12, ...), custom_call_target="tpu_custom_call" | custom-call | flops 115000000512 | bytes 8871952 | tf_op jit(solution)/shard_map/pallas_call | solution.py:131
  161.2 2.6 %collective-permute-done.29.refs_1_ = bf16[2304,128]{1,0:T(8,128)(2,1)S(1)} collective-permute-done((bf16[2304,128]{1,0:T(8,128)(2,1)S(1)}, bf16[2304,128]{1,0:T(8,128)(2,1)S(1)}, u32[]{:S(2)}, u32[]{:S(2)}) %collective-permute-start.29) | collective-permute-done | bytes 589856 | tf_op jit(solution)/shard_map/ppermute | solution.py:535
  165.1 2.1 shard_map.326
  169.9 10.9 %collective-permute-done.27.refs_3_.refs_12_.refs_2_.refs_9_.refs_4_ = bf16[4416,128]{1,0:T(8,128)(2,1)S(1)} collective-permute-done((bf16[4416,128]{1,0:T(8,128)(2,1)S(1)}, bf16[4416,128]{1,0:T(8,128)(2,1)S(1)}, u32[]{:S(2)}, u32[]{:S(2)}) %collective-permute-start.27) | collective-permute-done | bytes 1130528 | tf_op jit(solution)/shard_map/ppermute | solution.py:535
  182.8 2.3 shard_map.327
  191.1 2.0 collective-permute-done.36.refs_5_.refs_2_.refs_4_
  193.1 5.3 %collective-permute-done.35.refs_4_.refs_7_.refs_8_ = bf16[3072,128]{1,0:T(8,128)(2,1)} collective-permute-done((bf16[3072,128]{1,0:T(8,128)(2,1)S(1)}, bf16[3072,128]{1,0:T(8,128)(2,1)}, u32[]{:S(2)}, u32[]{:S(2)}) %collective-permute-start.35) | collective-permute-done | bytes 786464 | tf_op jit(solution)/shard_map/ppermute | solution.py:535
  200.7 2.2 shard_map.329
  207.5 2.6 %collective-permute-start.41 = (bf16[1008,128]{1,0:T(8,128)(2,1)S(1)}, bf16[1008,128]{1,0:T(8,128)(2,1)S(1)}, u32[]{:S(2)}, u32[]{:S(2)}) collective-permute-start(bf16[1008,128]{1,0:T(8,128)(2,1)S(1)} %get-tuple-element.149), channel_id=1, source_target_pairs={{0,16},{4,20},{8,24},{12,28},{16,0},{20,4},{24,8},{28,12},{1,17},{... | collective-permute-start | bytes 774152 | tf_op jit(solution)/shard_map/ppermute | solution.py:535
  216.0 3.4 %collective-permute-done.41.refs_1_ = bf16[1008,128]{1,0:T(8,128)(2,1)S(1)} collective-permute-done((bf16[1008,128]{1,0:T(8,128)(2,1)S(1)}, bf16[1008,128]{1,0:T(8,128)(2,1)S(1)}, u32[]{:S(2)}, u32[]{:S(2)}) %collective-permute-start.41) | collective-permute-done | bytes 258080 | tf_op jit(solution)/shard_map/ppermute | solution.py:535
  221.1 2.5 %shard_map.334 = (f32[3,48,96]{2,1,0:T(8,128)}, f32[48,96]{1,0:T(8,128)}, f32[48,384]{1,0:T(8,128)}, f32[48,384]{1,0:T(8,128)}, f32[96,768]{1,0:T(8,128)}, /*index=5*/f32[8,384]{1,0:T(8,128)S(1)}) custom-call(f32[8,384]{1,0:T(8,128)S(1)} %get-tuple-element.147.refs_0_, f32[8,384]{1,0:T(8,128)S(1)} %collective-permute-done.40.refs_1_, ...), custom_call_target="tpu_custom_call" | custom-call | flops 3449999872 | bytes 1806336 | tf_op jit(solution)/shard_map/pallas_call | solution.py:253
  227.0 2.3 collective-permute-start.48
  229.3 4.4 %collective-permute-done.45.refs_6_ = bf16[1344,128]{1,0:T(8,128)(2,1)} collective-permute-done((bf16[1344,128]{1,0:T(8,128)(2,1)S(1)}, bf16[1344,128]{1,0:T(8,128)(2,1)}, u32[]{:S(2)}, u32[]{:S(2)}) %collective-permute-start.45) | collective-permute-done | bytes 344096 | tf_op jit(solution)/shard_map/ppermute | solution.py:535
  239.5 2.1 shard_map.337
  244.8 2.5 shard_map.340.refs_10_
  248.1 2.4 shard_map.341
  (320 shorter events, 86.3 us)
Async XLA Ops:
  4.7 16.3 %collective-permute-start.1 = (bf16[384,768]{1,0:T(8,128)(2,1)S(1)}, bf16[384,768]{1,0:T(8,128)(2,1)S(1)}, u32[]{:S(2)}, u32[]{:S(2)}) collective-permute-start(bf16[384,768]{1,0:T(8,128)(2,1)S(1)} %get-tuple-element.93.refs_8_), channel_id=1, source_target_pairs={{0,2},{1,3},{2,0},{3,1},{4,6},{5,7},{6,4},{7,5},{8,10},{9,11},{10,... | collective-permute-start | bytes 1769480 | tf_op jit(solution)/shard_map/ppermute | solution.py:535
  7.7 30.6 %collective-permute-start = (bf16[768,768]{1,0:T(8,128)(2,1)}, bf16[768,768]{1,0:T(8,128)(2,1)}, u32[]{:S(2)}, u32[]{:S(2)}) collective-permute-start(bf16[768,768]{1,0:T(8,128)(2,1)} %get-tuple-element.92.refs_5_.refs_6_), channel_id=1, source_target_pairs={{0,1},{1,0},{2,3},{3,2},{4,5},{5,4},{6,7},{7,6},{8,9},{9,8},{10,11... | collective-permute-start | bytes 3538952 | tf_op jit(solution)/shard_map/ppermute | solution.py:535
  21.8 14.8 %collective-permute-start.2 = (bf16[384,768]{1,0:T(8,128)(2,1)}, bf16[384,768]{1,0:T(8,128)(2,1)}, u32[]{:S(2)}, u32[]{:S(2)}) collective-permute-start(bf16[384,768]{1,0:T(8,128)(2,1)} %get-tuple-element.96.refs_7_.refs_8_), channel_id=1, source_target_pairs={{0,4},{4,0},{8,12},{12,8},{16,20},{20,16},{24,28},{28,24},{1,5},{5... | collective-permute-start | bytes 1769480 | tf_op jit(solution)/shard_map/ppermute | solution.py:535
  23.6 14.6 %collective-permute-start.6 = (bf16[768,384]{1,0:T(8,128)(2,1)}, bf16[768,384]{1,0:T(8,128)(2,1)}, u32[]{:S(2)}, u32[]{:S(2)}) collective-permute-start(bf16[768,384]{1,0:T(8,128)(2,1)} %get-tuple-element.98), channel_id=1, source_target_pairs={{0,2},{1,3},{2,0},{3,1},{4,6},{5,7},{6,4},{7,5},{8,10},{9,11},{10,... | collective-permute-start | bytes 1769480 | tf_op jit(solution)/shard_map/ppermute | solution.py:535
  25.1 14.7 %collective-permute-start.3 = (bf16[384,768]{1,0:T(8,128)(2,1)}, bf16[384,768]{1,0:T(8,128)(2,1)}, u32[]{:S(2)}, u32[]{:S(2)}) collective-permute-start(bf16[384,768]{1,0:T(8,128)(2,1)} %get-tuple-element.96.refs_7_.refs_8_), channel_id=1, source_target_pairs={{0,1},{1,0},{2,3},{3,2},{4,5},{5,4},{6,7},{7,6},{8,9},{9,8},{10,11... | collective-permute-start | bytes 1769480 | tf_op jit(solution)/shard_map/ppermute | solution.py:535
  36.7 20.4 %collective-permute-start.5 = (bf16[768,768]{1,0:T(8,128)(2,1)}, bf16[768,768]{1,0:T(8,128)(2,1)}, u32[]{:S(2)}, u32[]{:S(2)}) collective-permute-start(bf16[768,768]{1,0:T(8,128)(2,1)} %refs_6_.3), channel_id=1, source_target_pairs={{0,1},{1,0},{2,3},{3,2},{4,5},{5,4},{6,7},{7,6},{8,9},{9,8},{10,11... | collective-permute-start | bytes 3538952 | tf_op jit(solution)/shard_map/ppermute | solution.py:535
  38.1 17.7 %collective-permute-start.15 = (bf16[1344,384]{1,0:T(8,128)(2,1)S(1)}, bf16[1344,384]{1,0:T(8,128)(2,1)}, u32[]{:S(2)}, u32[]{:S(2)}) collective-permute-start(bf16[1344,384]{1,0:T(8,128)(2,1)S(1)} %copy-done.3), channel_id=1, source_target_pairs={{0,1},{1,0},{2,3},{3,2},{4,5},{5,4},{6,7},{7,6},{8,9},{9,8},{10,11... | collective-permute-start | bytes 3096584 | tf_op jit(solution)/shard_map/ppermute | solution.py:535
  38.2 18.2 %collective-permute-start.11 = (bf16[384,768]{1,0:T(8,128)(2,1)}, bf16[384,768]{1,0:T(8,128)(2,1)}, u32[]{:S(2)}, u32[]{:S(2)}) collective-permute-start(bf16[384,768]{1,0:T(8,128)(2,1)} %shard_map.311), channel_id=1, source_target_pairs={{0,2},{1,3},{2,0},{3,1},{4,6},{5,7},{6,4},{7,5},{8,10},{9,11},{10,... | collective-permute-start | bytes 1769480 | tf_op jit(solution)/shard_map/ppermute | solution.py:535
  39.7 17.3 %collective-permute-start.8 = (bf16[768,384]{1,0:T(8,128)(2,1)}, bf16[768,384]{1,0:T(8,128)(2,1)}, u32[]{:S(2)}, u32[]{:S(2)}) collective-permute-start(bf16[768,384]{1,0:T(8,128)(2,1)} %collective-permute-done.6.refs_5_.refs_1_.refs_8_), channel_id=1, source_target_pairs={{0,1},{1,0},{2,3},{3,2},{4,5},{5,4},{6,7},{7,6},{8,9},{9,8},{10,11... | collective-permute-start | bytes 1769480 | tf_op jit(solution)/shard_map/ppermute | solution.py:535
  39.9 15.9 %collective-permute-start.7 = (bf16[768,384]{1,0:T(8,128)(2,1)}, bf16[768,384]{1,0:T(8,128)(2,1)}, u32[]{:S(2)}, u32[]{:S(2)}) collective-permute-start(bf16[768,384]{1,0:T(8,128)(2,1)} %collective-permute-done.6.refs_5_.refs_1_.refs_8_), channel_id=1, source_target_pairs={{0,4},{4,0},{8,12},{12,8},{16,20},{20,16},{24,28},{28,24},{1,5},{5... | collective-permute-start | bytes 1769480 | tf_op jit(solution)/shard_map/ppermute | solution.py:535
  55.8 17.3 %collective-permute-start.10 = (bf16[768,768]{1,0:T(8,128)(2,1)}, bf16[768,768]{1,0:T(8,128)(2,1)}, u32[]{:S(2)}, u32[]{:S(2)}) collective-permute-start(bf16[768,768]{1,0:T(8,128)(2,1)} %refs_12_.1), channel_id=1, source_target_pairs={{0,1},{1,0},{2,3},{3,2},{4,5},{5,4},{6,7},{7,6},{8,9},{9,8},{10,11... | collective-permute-start | bytes 3538952 | tf_op jit(solution)/shard_map/ppermute | solution.py:535
  56.4 25.0 %collective-permute-start.16 = (bf16[1344,384]{1,0:T(8,128)(2,1)}, bf16[1344,384]{1,0:T(8,128)(2,1)S(1)}, u32[]{:S(2)}, u32[]{:S(2)}) collective-permute-start(bf16[1344,384]{1,0:T(8,128)(2,1)} %shard_map.314.refs_10_), channel_id=1, source_target_pairs={{0,2},{1,3},{2,0},{3,1},{4,6},{5,7},{6,4},{7,5},{8,10},{9,11},{10,... | collective-permute-start | bytes 3096584 | tf_op jit(solution)/shard_map/ppermute | solution.py:535
  57.0 16.1 %collective-permute-start.13 = (bf16[384,768]{1,0:T(8,128)(2,1)}, bf16[384,768]{1,0:T(8,128)(2,1)}, u32[]{:S(2)}, u32[]{:S(2)}) collective-permute-start(bf16[384,768]{1,0:T(8,128)(2,1)} %collective-permute-done.11.refs_5_.refs_1_.refs_14_), channel_id=1, source_target_pairs={{0,1},{1,0},{2,3},{3,2},{4,5},{5,4},{6,7},{7,6},{8,9},{9,8},{10,11... | collective-permute-start | bytes 1769480 | tf_op jit(solution)/shard_map/ppermute | solution.py:535
  57.0 16.1 %collective-permute-start.12 = (bf16[384,768]{1,0:T(8,128)(2,1)}, bf16[384,768]{1,0:T(8,128)(2,1)}, u32[]{:S(2)}, u32[]{:S(2)}) collective-permute-start(bf16[384,768]{1,0:T(8,128)(2,1)} %collective-permute-done.11.refs_5_.refs_1_.refs_14_), channel_id=1, source_target_pairs={{0,4},{4,0},{8,12},{12,8},{16,20},{20,16},{24,28},{28,24},{1,5},{5... | collective-permute-start | bytes 1769480 | tf_op jit(solution)/shard_map/ppermute | solution.py:535
  114.4 35.5 %collective-permute-start.25 = (bf16[4608,128]{1,0:T(8,128)(2,1)}, bf16[4608,128]{1,0:T(8,128)(2,1)}, u32[]{:S(2)}, u32[]{:S(2)}) collective-permute-start(bf16[4608,128]{1,0:T(8,128)(2,1)} %get-tuple-element.120), channel_id=1, source_target_pairs={{0,1},{1,0},{2,3},{3,2},{4,5},{5,4},{6,7},{7,6},{8,9},{9,8},{10,11... | collective-permute-start | bytes 3538952 | tf_op jit(solution)/shard_map/ppermute | solution.py:535
  118.8 28.7 %collective-permute-start.22 = (bf16[4224,128]{1,0:T(8,128)(2,1)S(1)}, bf16[4224,128]{1,0:T(8,128)(2,1)S(1)}, u32[]{:S(2)}, u32[]{:S(2)}) collective-permute-start(bf16[4224,128]{1,0:T(8,128)(2,1)S(1)} %get-tuple-element.108.refs_19_), channel_id=1, source_target_pairs={{0,4},{4,0},{8,12},{12,8},{16,20},{20,16},{24,28},{28,24},{1,5},{5... | collective-permute-start | bytes 3244040 | tf_op jit(solution)/shard_map/ppermute | solution.py:535
  120.4 27.8 %collective-permute-start.21 = (bf16[4608,128]{1,0:T(8,128)(2,1)S(1)}, bf16[4608,128]{1,0:T(8,128)(2,1)S(1)}, u32[]{:S(2)}, u32[]{:S(2)}) collective-permute-start(bf16[4608,128]{1,0:T(8,128)(2,1)S(1)} %get-tuple-element.107.refs_18_), channel_id=1, source_target_pairs={{0,2},{1,3},{2,0},{3,1},{4,6},{5,7},{6,4},{7,5},{8,10},{9,11},{10,... | collective-permute-start | bytes 3538952 | tf_op jit(solution)/shard_map/ppermute | solution.py:535
  135.3 12.1 %collective-permute-start.23 = (bf16[2304,128]{1,0:T(8,128)(2,1)S(1)}, bf16[2304,128]{1,0:T(8,128)(2,1)S(1)}, u32[]{:S(2)}, u32[]{:S(2)}) collective-permute-start(bf16[2304,128]{1,0:T(8,128)(2,1)S(1)} %get-tuple-element.110), channel_id=1, source_target_pairs={{0,1},{1,0},{2,3},{3,2},{4,5},{5,4},{6,7},{7,6},{8,9},{9,8},{10,11... | collective-permute-start | bytes 1769480 | tf_op jit(solution)/shard_map/ppermute | solution.py:535
  135.3 12.2 %collective-permute-start.24 = (bf16[2304,128]{1,0:T(8,128)(2,1)S(1)}, bf16[2304,128]{1,0:T(8,128)(2,1)S(1)}, u32[]{:S(2)}, u32[]{:S(2)}) collective-permute-start(bf16[2304,128]{1,0:T(8,128)(2,1)S(1)} %get-tuple-element.111), channel_id=1, source_target_pairs={{0,1},{1,0},{2,3},{3,2},{4,5},{5,4},{6,7},{7,6},{8,9},{9,8},{10,11... | collective-permute-start | bytes 1769480 | tf_op jit(solution)/shard_map/ppermute | solution.py:535
  147.3 21.1 %collective-permute-start.26 = (bf16[4608,128]{1,0:T(8,128)(2,1)}, bf16[4608,128]{1,0:T(8,128)(2,1)}, u32[]{:S(2)}, u32[]{:S(2)}) collective-permute-start(bf16[4608,128]{1,0:T(8,128)(2,1)} %get-tuple-element.127), channel_id=1, source_target_pairs={{0,1},{1,0},{2,3},{3,2},{4,5},{5,4},{6,7},{7,6},{8,9},{9,8},{10,11... | collective-permute-start | bytes 3538952 | tf_op jit(solution)/shard_map/ppermute | solution.py:535
  153.0 27.8 %collective-permute-start.27 = (bf16[4416,128]{1,0:T(8,128)(2,1)S(1)}, bf16[4416,128]{1,0:T(8,128)(2,1)S(1)}, u32[]{:S(2)}, u32[]{:S(2)}) collective-permute-start(bf16[4416,128]{1,0:T(8,128)(2,1)S(1)} %get-tuple-element.123.refs_3_.refs_12_), channel_id=1, source_target_pairs={{0,2},{1,3},{2,0},{3,1},{4,6},{5,7},{6,4},{7,5},{8,10},{9,11},{10,... | collective-permute-start | bytes 3391496 | tf_op jit(solution)/shard_map/ppermute | solution.py:535
  153.7 27.8 %collective-permute-start.28 = (bf16[4416,128]{1,0:T(8,128)(2,1)S(1)}, bf16[4416,128]{1,0:T(8,128)(2,1)S(1)}, u32[]{:S(2)}, u32[]{:S(2)}) collective-permute-start(bf16[4416,128]{1,0:T(8,128)(2,1)S(1)} %get-tuple-element.124.refs_4_.refs_13_), channel_id=1, source_target_pairs={{0,4},{4,0},{8,12},{12,8},{16,20},{20,16},{24,28},{28,24},{1,5},{5... | collective-permute-start | bytes 3391496 | tf_op jit(solution)/shard_map/ppermute | solution.py:535
  163.9 26.2 %collective-permute-start.34 = (bf16[5376,128]{1,0:T(8,128)(2,1)}, bf16[5376,128]{1,0:T(8,128)(2,1)}, u32[]{:S(2)}, u32[]{:S(2)}) collective-permute-start(bf16[5376,128]{1,0:T(8,128)(2,1)} %get-tuple-element.141), channel_id=1, source_target_pairs={{0,1},{1,0},{2,3},{3,2},{4,5},{5,4},{6,7},{7,6},{8,9},{9,8},{10,11... | collective-permute-start | bytes 4128776 | tf_op jit(solution)/shard_map/ppermute | solution.py:535
  167.2 25.8 %collective-permute-start.36 = (bf16[2304,128]{1,0:T(8,128)(2,1)S(1)}, bf16[2304,128]{1,0:T(8,128)(2,1)}, u32[]{:S(2)}, u32[]{:S(2)}) collective-permute-start(bf16[2304,128]{1,0:T(8,128)(2,1)S(1)} %get-tuple-element.136.refs_10_), channel_id=1, source_target_pairs={{0,2},{1,3},{2,0},{3,1},{4,6},{5,7},{6,4},{7,5},{8,10},{9,11},{10,... | collective-permute-start | bytes 1769480 | tf_op jit(solution)/shard_map/ppermute | solution.py:535
  168.4 30.0 %collective-permute-start.35 = (bf16[3072,128]{1,0:T(8,128)(2,1)S(1)}, bf16[3072,128]{1,0:T(8,128)(2,1)}, u32[]{:S(2)}, u32[]{:S(2)}) collective-permute-start(bf16[3072,128]{1,0:T(8,128)(2,1)S(1)} %get-tuple-element.137.refs_11_), channel_id=1, source_target_pairs={{0,4},{4,0},{8,12},{12,8},{16,20},{20,16},{24,28},{28,24},{1,5},{5... | collective-permute-start | bytes 2359304 | tf_op jit(solution)/shard_map/ppermute | solution.py:535
  186.6 12.7 %collective-permute-start.37 = (bf16[2016,128]{1,0:T(8,128)(2,1)S(1)}, bf16[2016,128]{1,0:T(8,128)(2,1)S(1)}, u32[]{:S(2)}, u32[]{:S(2)}) collective-permute-start(bf16[2016,128]{1,0:T(8,128)(2,1)S(1)} %get-tuple-element.142), channel_id=1, source_target_pairs={{0,8},{4,12},{8,0},{12,4},{16,24},{20,28},{24,16},{28,20},{1,9},{5... | collective-permute-start | bytes 1548296 | tf_op jit(solution)/shard_map/ppermute | solution.py:535
  189.5 18.0 %collective-permute-start.31 = (bf16[1152,128]{1,0:T(8,128)(2,1)}, bf16[1152,128]{1,0:T(8,128)(2,1)S(1)}, u32[]{:S(2)}, u32[]{:S(2)}) collective-permute-start(bf16[1152,128]{1,0:T(8,128)(2,1)} %copy-done.34), channel_id=1, source_target_pairs={{0,4},{4,0},{8,12},{12,8},{16,20},{20,16},{24,28},{28,24},{1,5},{5... | collective-permute-start | bytes 884744 | tf_op jit(solution)/shard_map/ppermute | solution.py:535
  190.0 20.1 %collective-permute-start.32 = (bf16[1152,128]{1,0:T(8,128)(2,1)}, bf16[1152,128]{1,0:T(8,128)(2,1)}, u32[]{:S(2)}, u32[]{:S(2)}) collective-permute-start(bf16[1152,128]{1,0:T(8,128)(2,1)} %copy-done.33), channel_id=1, source_target_pairs={{0,2},{1,3},{2,0},{3,1},{4,6},{5,7},{6,4},{7,5},{8,10},{9,11},{10,... | collective-permute-start | bytes 884744 | tf_op jit(solution)/shard_map/ppermute | solution.py:535
  205.9 14.2 %collective-permute-start.40 = (f32[8,384]{1,0:T(8,128)S(1)}, f32[8,384]{1,0:T(8,128)S(1)}, u32[]{:S(2)}, u32[]{:S(2)}) collective-permute-start(f32[8,384]{1,0:T(8,128)S(1)} %get-tuple-element.147.refs_0_), channel_id=1, source_target_pairs={{0,8},{4,12},{8,0},{12,4},{16,24},{20,28},{24,16},{28,20},{1,9},{5... | collective-permute-start | bytes 36872 | tf_op jit(solution)/shard_map/ppermute | solution.py:535
  211.6 14.0 %collective-permute-start.47 = (bf16[1152,128]{1,0:T(8,128)(2,1)S(1)}, bf16[1152,128]{1,0:T(8,128)(2,1)}, u32[]{:S(2)}, u32[]{:S(2)}) collective-permute-start(bf16[1152,128]{1,0:T(8,128)(2,1)S(1)} %shard_map.330.refs_2_.refs_6_), channel_id=1, source_target_pairs={{0,8},{4,12},{8,0},{12,4},{16,24},{20,28},{24,16},{28,20},{1,9},{5... | collective-permute-start | bytes 884744 | tf_op jit(solution)/shard_map/ppermute | solution.py:535
  214.4 19.3 %collective-permute-start.45 = (bf16[1344,128]{1,0:T(8,128)(2,1)S(1)}, bf16[1344,128]{1,0:T(8,128)(2,1)}, u32[]{:S(2)}, u32[]{:S(2)}) collective-permute-start(bf16[1344,128]{1,0:T(8,128)(2,1)S(1)} %shard_map.332.refs_2_.refs_12_.refs_7_), channel_id=1, source_target_pairs={{0,8},{4,12},{8,0},{12,4},{16,24},{20,28},{24,16},{28,20},{1,9},{5... | collective-permute-start | bytes 1032200 | tf_op jit(solution)/shard_map/ppermute | solution.py:535
  224.4 13.1 %collective-permute-start.50 = (bf16[1536,128]{1,0:T(8,128)(2,1)S(1)}, bf16[1536,128]{1,0:T(8,128)(2,1)S(1)}, u32[]{:S(2)}, u32[]{:S(2)}) collective-permute-start(bf16[1536,128]{1,0:T(8,128)(2,1)S(1)} %copy-done.9), channel_id=1, source_target_pairs={{0,2},{1,3},{2,0},{3,1},{4,6},{5,7},{6,4},{7,5},{8,10},{9,11},{10,... | collective-permute-start | bytes 1179656 | tf_op jit(solution)/shard_map/ppermute | solution.py:535
  (113 other events, 499.7 us)
